TPU v7x, 512 devices: a whole 4x8x8 slice. The times are simulated.
512 devices in a mesh: dp: 512 (over x, z, y, core).
Axes of the slice: x: 4, y: 8, z: 8, core: 2. Of those that a mesh axis runs over, the one named last changes fastest.
Arguments:
- student_image_vectors: bfloat16 [196608, 768], P('dp'), may hold values from -6 to 6
- teacher_emb: bfloat16 [196608, 768], P('dp'), may hold values from -6 to 6
- text_emb: bfloat16 [196608, 768], P('dp'), may hold values from -6 to 6
- species: int32 [196608], P('dp'), may hold values from 0 to 999
Outputs:
- grad_student: float32 [196608, 768], P('dp')
- grad_text: float32 [196608, 768], P('dp')
- loss_rows: float32 [196608], P('dp')
Inputs may be any that keep to these rules, and one draw needn't show every extreme that they name: species ids; pairs with equal ids count as positives.
All inputs are finite; a program needn't handle non-finite values.
Results may differ from a plain program's by a relative error of at most 0.0015.
Values may be sent and summed in bfloat16 or wider, within the bound.
No kernel may reach another device: no remote copies, remote signals or barrier semaphores. Data moves between devices by JAX's collectives and lax.ppermute only.
A program may use at most 64 MiB of HBM per device.

v0:
```python
import math

import jax
import jax.numpy as jnp
from jax import lax
from jax.sharding import PartitionSpec as P

HOPS = 3


SOFTMAX_TEMP_VALUE = 4.0
LOGIT_BIAS = -3.0


def shifted(value, axis, by):
    length = lax.axis_size(axis)
    return lax.ppermute(value, axis, [(i, (i + by) % length) for i in range(length)])


def block_terms(
    student_image_vectors, teacher_emb, own_species, caption_block, caption_species_labels
):
    logit_scale_multiplier = SOFTMAX_TEMP_VALUE / math.sqrt(student_image_vectors.shape[1])
    contract = (((1,), (1,)), ((), ()))
    student_pair_logit = (
        lax.dot_general(
            student_image_vectors, caption_block, contract, preferred_element_type=jnp.float32
        )
        * logit_scale_multiplier
        + LOGIT_BIAS
    )
    teacher_logit = (
        lax.dot_general(teacher_emb, caption_block, contract, preferred_element_type=jnp.float32)
        * logit_scale_multiplier
        + LOGIT_BIAS
    )
    positive = (own_species[:, None] == caption_species_labels[None, :]).astype(jnp.float32)
    target = 0.5 * positive + 0.5 * jax.nn.sigmoid(teacher_logit)
    per_row_loss = jnp.sum(
        jax.nn.softplus(student_pair_logit) - target * student_pair_logit, axis=1
    )
    slope = (jax.nn.sigmoid(student_pair_logit) - target).astype(jnp.bfloat16)
    grad_rows = (
        jnp.dot(slope, caption_block, preferred_element_type=jnp.float32) * logit_scale_multiplier
    )
    grad_cols = (
        lax.dot_general(
            slope,
            student_image_vectors,
            (((0,), (0,)), ((), ())),
            preferred_element_type=jnp.float32,
        )
        * logit_scale_multiplier
    )
    return (per_row_loss, grad_rows, grad_cols)


def shards(student_image_vectors, teacher_emb, text_emb, species):
    row_count = student_image_vectors.shape[0]
    loss_sum, grad_student, grad_text = block_terms(
        student_image_vectors, teacher_emb, species, text_emb, species
    )
    offsets = list(range(1, HOPS + 1)) + list(range(-HOPS, 0))
    for offset in offsets:
        caption_block, caption_species_labels = shifted((text_emb, species), "dp", -offset)
        per_row_loss, grad_rows, grad_cols = block_terms(
            student_image_vectors, teacher_emb, species, caption_block, caption_species_labels
        )
        loss_sum = loss_sum + per_row_loss
        grad_student = grad_student + grad_rows
        grad_text = grad_text + shifted(grad_cols, "dp", offset)
    loss_rows = loss_sum / float((2 * HOPS + 1) * row_count)
    return (grad_student, grad_text, loss_rows)


def solution(mesh):
    return jax.shard_map(
        shards,
        mesh=mesh,
        in_specs=(P("dp", None), P("dp", None), P("dp", None), P("dp")),
        out_specs=(P("dp", None), P("dp", None), P("dp")),
        check_vma=False,
    )
```

profile of v0, /device:TPU:6, one launch (start us, length us, event | category | flops | bytes accessed | tf_op | source)
XLA Modules:
  0.0 201.8 jit_solution(17445013638786904519)
XLA Ops:
  0.7 13.7 %collective-permute-start = (bf16[384,768]{1,0:T(8,128)(2,1)}, bf16[384,768]{1,0:T(8,128)(2,1)S(1)}, u32[]{:S(2)}, u32[]{:S(2)}) collective-permute-start(bf16[384,768]{1,0:T(8,128)(2,1)} %param.6), channel_id=1, source_target_pairs={{0,511},{1,0},{2,1},{3,2},{4,3},{5,4},{6,5},{7,6},{8,7},{9,8},{10,... | collective-permute-start | bytes 1769480 | tf_op jit(solution)/shard_map/ppermute | solution.py:17
  14.4 3.3 %collective-permute-start.2 = (bf16[384,768]{1,0:T(8,128)(2,1)}, bf16[384,768]{1,0:T(8,128)(2,1)S(1)}, u32[]{:S(2)}, u32[]{:S(2)}) collective-permute-start(bf16[384,768]{1,0:T(8,128)(2,1)} %param.6), channel_id=1, source_target_pairs={{0,510},{1,511},{2,0},{3,1},{4,2},{5,3},{6,4},{7,5},{8,6},{9,7},{1... | collective-permute-start | bytes 1769480 | tf_op jit(solution)/shard_map/ppermute | solution.py:17
  17.6 2.3 %collective-permute-start.1 = (s32[384]{0:T(512)}, s32[384]{0:T(512)S(1)}, u32[]{:S(2)}, u32[]{:S(2)}) collective-permute-start(s32[384]{0:T(512)} %param.7), channel_id=1, source_target_pairs={{0,511},{1,0},{2,1},{3,2},{4,3},{5,4},{6,5},{7,6},{8,7},{9,8},{10,... | collective-permute-start | bytes 4616 | tf_op jit(solution)/shard_map/ppermute | solution.py:17
  19.9 3.3 %collective-permute-start.3 = (s32[384]{0:T(512)}, s32[384]{0:T(512)S(1)}, u32[]{:S(2)}, u32[]{:S(2)}) collective-permute-start(s32[384]{0:T(512)} %param.7), channel_id=1, source_target_pairs={{0,510},{1,511},{2,0},{3,1},{4,2},{5,3},{6,4},{7,5},{8,6},{9,7},{1... | collective-permute-start | bytes 4616 | tf_op jit(solution)/shard_map/ppermute | solution.py:17
  23.2 2.7 %collective-permute-start.4 = (bf16[384,768]{1,0:T(8,128)(2,1)}, bf16[384,768]{1,0:T(8,128)(2,1)S(1)}, u32[]{:S(2)}, u32[]{:S(2)}) collective-permute-start(bf16[384,768]{1,0:T(8,128)(2,1)} %param.6), channel_id=1, source_target_pairs={{0,509},{1,510},{2,511},{3,0},{4,1},{5,2},{6,3},{7,4},{8,5},{9,6},... | collective-permute-start | bytes 1769480 | tf_op jit(solution)/shard_map/ppermute | solution.py:17
  29.1 15.4 %collective-permute-done.2 = bf16[384,768]{1,0:T(8,128)(2,1)S(1)} collective-permute-done((bf16[384,768]{1,0:T(8,128)(2,1)}, bf16[384,768]{1,0:T(8,128)(2,1)S(1)}, u32[]{:S(2)}, u32[]{:S(2)}) %collective-permute-start.2) | collective-permute-done | bytes 589856 | tf_op jit(solution)/shard_map/ppermute | solution.py:17
  47.5 6.2 %collective-permute-done.4 = bf16[384,768]{1,0:T(8,128)(2,1)S(1)} collective-permute-done((bf16[384,768]{1,0:T(8,128)(2,1)}, bf16[384,768]{1,0:T(8,128)(2,1)S(1)}, u32[]{:S(2)}, u32[]{:S(2)}) %collective-permute-start.4) | collective-permute-done | bytes 589856 | tf_op jit(solution)/shard_map/ppermute | solution.py:17
  56.7 13.0 %collective-permute-done.6 = bf16[384,768]{1,0:T(8,128)(2,1)S(1)} collective-permute-done((bf16[384,768]{1,0:T(8,128)(2,1)S(1)}, bf16[384,768]{1,0:T(8,128)(2,1)S(1)}, u32[]{:S(2)}, u32[]{:S(2)}) %collective-permute-start.6) | collective-permute-done | bytes 589856 | tf_op jit(solution)/shard_map/ppermute | solution.py:17
  69.7 4.5 %collective-permute-start.10 = (bf16[384,768]{1,0:T(8,128)(2,1)S(1)}, bf16[384,768]{1,0:T(8,128)(2,1)S(1)}, u32[]{:S(2)}, u32[]{:S(2)}) collective-permute-start(bf16[384,768]{1,0:T(8,128)(2,1)S(1)} %copy-done.1), channel_id=1, source_target_pairs={{0,1},{1,2},{2,3},{3,4},{4,5},{5,6},{6,7},{7,8},{8,9},{9,10},{10,1... | collective-permute-start | bytes 1769480 | tf_op jit(solution)/shard_map/ppermute | solution.py:17
  75.2 5.5 %collective-permute-done.8 = bf16[384,768]{1,0:T(8,128)(2,1)S(1)} collective-permute-done((bf16[384,768]{1,0:T(8,128)(2,1)S(1)}, bf16[384,768]{1,0:T(8,128)(2,1)S(1)}, u32[]{:S(2)}, u32[]{:S(2)}) %collective-permute-start.8) | collective-permute-done | bytes 589856 | tf_op jit(solution)/shard_map/ppermute | solution.py:17
  83.7 2.4 %collective-permute-done.10 = bf16[384,768]{1,0:T(8,128)(2,1)S(1)} collective-permute-done((bf16[384,768]{1,0:T(8,128)(2,1)S(1)}, bf16[384,768]{1,0:T(8,128)(2,1)S(1)}, u32[]{:S(2)}, u32[]{:S(2)}) %collective-permute-start.10) | collective-permute-done | bytes 589856 | tf_op jit(solution)/shard_map/ppermute | solution.py:17
  91.0 1.9 collective-permute-start.11
  93.5 2.6 %collective-permute-done.7 = s32[384]{0:T(512)S(1)} collective-permute-done((s32[384]{0:T(512)S(1)}, s32[384]{0:T(512)S(1)}, u32[]{:S(2)}, u32[]{:S(2)}) %collective-permute-start.7) | collective-permute-done | bytes 1568 | tf_op jit(solution)/shard_map/ppermute | solution.py:17
  96.1 2.7 %collective-permute-done.9 = s32[384]{0:T(512)S(1)} collective-permute-done((s32[384]{0:T(512)S(1)}, s32[384]{0:T(512)S(1)}, u32[]{:S(2)}, u32[]{:S(2)}) %collective-permute-start.9) | collective-permute-done | bytes 1568 | tf_op jit(solution)/shard_map/ppermute | solution.py:17
  100.2 4.0 %fusion.64 = (f32[384]{0:T(512)S(1)}, f32[384]{0:T(512)S(1)}, f32[384]{0:T(512)S(1)}, f32[384]{0:T(512)S(1)}, f32[384]{0:T(512)S(1)}, /*index=5*/f32[384]{0:T(51...) fusion(f32[384,384]{0,1:T(8,128)S(1)} %fusion.25, ...), kind=kOutput, calls=%fused_computation.94 | convolution fusion | flops 241825536 | bytes 9457152 | tf_op jit(solution)/shard_map/dot_general | solution.py:26
  107.0 3.9 %collective-permute-start.16 = (f32[384,768]{1,0:T(8,128)S(1)}, f32[384,768]{1,0:T(8,128)S(1)}, u32[]{:S(2)}, u32[]{:S(2)}) collective-permute-start(f32[384,768]{1,0:T(8,128)S(1)} %convolution_multiply_fusion.1), channel_id=1, source_target_pairs={{0,510},{1,511},{2,0},{3,1},{4,2},{5,3},{6,4},{7,5},{8,6},{9,7},{1... | collective-permute-start | bytes 3538952 | tf_op jit(solution)/shard_map/ppermute | solution.py:17
  111.4 2.6 %collective-permute-start.15 = (f32[384,768]{1,0:T(8,128)S(1)}, f32[384,768]{1,0:T(8,128)S(1)}, u32[]{:S(2)}, u32[]{:S(2)}) collective-permute-start(f32[384,768]{1,0:T(8,128)S(1)} %convolution_multiply_fusion.2), channel_id=1, source_target_pairs={{0,509},{1,510},{2,511},{3,0},{4,1},{5,2},{6,3},{7,4},{8,5},{9,6},... | collective-permute-start | bytes 3538952 | tf_op jit(solution)/shard_map/ppermute | solution.py:17
  114.5 2.9 %collective-permute-start.14 = (f32[384,768]{1,0:T(8,128)S(1)}, f32[384,768]{1,0:T(8,128)S(1)}, u32[]{:S(2)}, u32[]{:S(2)}) collective-permute-start(f32[384,768]{1,0:T(8,128)S(1)} %convolution_multiply_fusion.3), channel_id=1, source_target_pairs={{0,3},{1,4},{2,5},{3,6},{4,7},{5,8},{6,9},{7,10},{8,11},{9,12},{10... | collective-permute-start | bytes 3538952 | tf_op jit(solution)/shard_map/ppermute | solution.py:17
  117.9 2.7 %collective-permute-start.13 = (f32[384,768]{1,0:T(8,128)S(1)}, f32[384,768]{1,0:T(8,128)S(1)}, u32[]{:S(2)}, u32[]{:S(2)}) collective-permute-start(f32[384,768]{1,0:T(8,128)S(1)} %convolution_multiply_fusion.4), channel_id=1, source_target_pairs={{0,2},{1,3},{2,4},{3,5},{4,6},{5,7},{6,8},{7,9},{8,10},{9,11},{10,... | collective-permute-start | bytes 3538952 | tf_op jit(solution)/shard_map/ppermute | solution.py:17
  122.6 6.3 %collective-permute-done.17 = f32[384,768]{1,0:T(8,128)S(1)} collective-permute-done((f32[384,768]{1,0:T(8,128)S(1)}, f32[384,768]{1,0:T(8,128)S(1)}, u32[]{:S(2)}, u32[]{:S(2)}) %collective-permute-start.17) | collective-permute-done | bytes 1179680 | tf_op jit(solution)/shard_map/ppermute | solution.py:17
  134.1 22.7 %collective-permute-done.16 = f32[384,768]{1,0:T(8,128)S(1)} collective-permute-done((f32[384,768]{1,0:T(8,128)S(1)}, f32[384,768]{1,0:T(8,128)S(1)}, u32[]{:S(2)}, u32[]{:S(2)}) %collective-permute-start.16) | collective-permute-done | bytes 1179680 | tf_op jit(solution)/shard_map/ppermute | solution.py:17
  156.8 26.6 %collective-permute-done.15 = f32[384,768]{1,0:T(8,128)S(1)} collective-permute-done((f32[384,768]{1,0:T(8,128)S(1)}, f32[384,768]{1,0:T(8,128)S(1)}, u32[]{:S(2)}, u32[]{:S(2)}) %collective-permute-start.15) | collective-permute-done | bytes 1179680 | tf_op jit(solution)/shard_map/ppermute | solution.py:17
  183.4 3.9 %collective-permute-done.13 = f32[384,768]{1,0:T(8,128)S(1)} collective-permute-done((f32[384,768]{1,0:T(8,128)S(1)}, f32[384,768]{1,0:T(8,128)S(1)}, u32[]{:S(2)}, u32[]{:S(2)}) %collective-permute-start.13) | collective-permute-done | bytes 1179680 | tf_op jit(solution)/shard_map/ppermute | solution.py:17
  187.3 12.9 %collective-permute-done.12 = f32[384,768]{1,0:T(8,128)S(1)} collective-permute-done((f32[384,768]{1,0:T(8,128)S(1)}, f32[384,768]{1,0:T(8,128)S(1)}, u32[]{:S(2)}, u32[]{:S(2)}) %collective-permute-start.12) | collective-permute-done | bytes 1179680 | tf_op jit(solution)/shard_map/ppermute | solution.py:17
  (49 shorter events, 32.9 us)
Async XLA Ops:
  0.6 27.1 %copy-start = (bf16[384,768]{1,0:T(8,128)(2,1)S(1)}, bf16[384,768]{1,0:T(8,128)(2,1)}, u32[]{:S(2)}) copy-start(bf16[384,768]{1,0:T(8,128)(2,1)} %param.4) | copy-start | bytes 1769476
  0.6 27.1 %copy-start.1 = (bf16[384,768]{1,0:T(8,128)(2,1)S(1)}, bf16[384,768]{1,0:T(8,128)(2,1)}, u32[]{:S(2)}) copy-start(bf16[384,768]{1,0:T(8,128)(2,1)} %param.6) | copy-start | bytes 1769476
  0.7 90.4 %collective-permute-start = (bf16[384,768]{1,0:T(8,128)(2,1)}, bf16[384,768]{1,0:T(8,128)(2,1)S(1)}, u32[]{:S(2)}, u32[]{:S(2)}) collective-permute-start(bf16[384,768]{1,0:T(8,128)(2,1)} %param.6), channel_id=1, source_target_pairs={{0,511},{1,0},{2,1},{3,2},{4,3},{5,4},{6,5},{7,6},{8,7},{9,8},{10,... | collective-permute-start | bytes 1769480 | tf_op jit(solution)/shard_map/ppermute | solution.py:17
  14.4 30.2 %collective-permute-start.2 = (bf16[384,768]{1,0:T(8,128)(2,1)}, bf16[384,768]{1,0:T(8,128)(2,1)S(1)}, u32[]{:S(2)}, u32[]{:S(2)}) collective-permute-start(bf16[384,768]{1,0:T(8,128)(2,1)} %param.6), channel_id=1, source_target_pairs={{0,510},{1,511},{2,0},{3,1},{4,2},{5,3},{6,4},{7,5},{8,6},{9,7},{1... | collective-permute-start | bytes 1769480 | tf_op jit(solution)/shard_map/ppermute | solution.py:17
  17.6 71.5 %collective-permute-start.1 = (s32[384]{0:T(512)}, s32[384]{0:T(512)S(1)}, u32[]{:S(2)}, u32[]{:S(2)}) collective-permute-start(s32[384]{0:T(512)} %param.7), channel_id=1, source_target_pairs={{0,511},{1,0},{2,1},{3,2},{4,3},{5,4},{6,5},{7,6},{8,7},{9,8},{10,... | collective-permute-start | bytes 4616 | tf_op jit(solution)/shard_map/ppermute | solution.py:17
  19.9 73.6 %collective-permute-start.3 = (s32[384]{0:T(512)}, s32[384]{0:T(512)S(1)}, u32[]{:S(2)}, u32[]{:S(2)}) collective-permute-start(s32[384]{0:T(512)} %param.7), channel_id=1, source_target_pairs={{0,510},{1,511},{2,0},{3,1},{4,2},{5,3},{6,4},{7,5},{8,6},{9,7},{1... | collective-permute-start | bytes 4616 | tf_op jit(solution)/shard_map/ppermute | solution.py:17
  23.2 30.5 %collective-permute-start.4 = (bf16[384,768]{1,0:T(8,128)(2,1)}, bf16[384,768]{1,0:T(8,128)(2,1)S(1)}, u32[]{:S(2)}, u32[]{:S(2)}) collective-permute-start(bf16[384,768]{1,0:T(8,128)(2,1)} %param.6), channel_id=1, source_target_pairs={{0,509},{1,510},{2,511},{3,0},{4,1},{5,2},{6,3},{7,4},{8,5},{9,6},... | collective-permute-start | bytes 1769480 | tf_op jit(solution)/shard_map/ppermute | solution.py:17
  29.1 17.8 %copy-start.2 = (bf16[384,768]{1,0:T(8,128)(2,1)S(1)}, bf16[384,768]{1,0:T(8,128)(2,1)}, u32[]{:S(2)}) copy-start(bf16[384,768]{1,0:T(8,128)(2,1)} %param.5) | copy-start | bytes 1769476
  44.5 25.1 %collective-permute-start.6 = (bf16[384,768]{1,0:T(8,128)(2,1)S(1)}, bf16[384,768]{1,0:T(8,128)(2,1)S(1)}, u32[]{:S(2)}, u32[]{:S(2)}) collective-permute-start(bf16[384,768]{1,0:T(8,128)(2,1)S(1)} %copy-done.1), channel_id=1, source_target_pairs={{0,3},{1,4},{2,5},{3,6},{4,7},{5,8},{6,9},{7,10},{8,11},{9,12},{10... | collective-permute-start | bytes 1769480 | tf_op jit(solution)/shard_map/ppermute | solution.py:17
  53.7 27.1 %collective-permute-start.8 = (bf16[384,768]{1,0:T(8,128)(2,1)S(1)}, bf16[384,768]{1,0:T(8,128)(2,1)S(1)}, u32[]{:S(2)}, u32[]{:S(2)}) collective-permute-start(bf16[384,768]{1,0:T(8,128)(2,1)S(1)} %copy-done.1), channel_id=1, source_target_pairs={{0,2},{1,3},{2,4},{3,5},{4,6},{5,7},{6,8},{7,9},{8,10},{9,11},{10,... | collective-permute-start | bytes 1769480 | tf_op jit(solution)/shard_map/ppermute | solution.py:17
  69.7 16.5 %collective-permute-start.10 = (bf16[384,768]{1,0:T(8,128)(2,1)S(1)}, bf16[384,768]{1,0:T(8,128)(2,1)S(1)}, u32[]{:S(2)}, u32[]{:S(2)}) collective-permute-start(bf16[384,768]{1,0:T(8,128)(2,1)S(1)} %copy-done.1), channel_id=1, source_target_pairs={{0,1},{1,2},{2,3},{3,4},{4,5},{5,6},{6,7},{7,8},{8,9},{9,10},{10,1... | collective-permute-start | bytes 1769480 | tf_op jit(solution)/shard_map/ppermute | solution.py:17
  74.7 6.1 %copy-start.3 = (s32[384]{0:T(512)S(1)}, s32[384]{0:T(512)}, u32[]{:S(2)}) copy-start(s32[384]{0:T(512)} %param.7) | copy-start | bytes 4612
  80.8 12.7 %collective-permute-start.5 = (s32[384]{0:T(512)S(1)}, s32[384]{0:T(512)S(1)}, u32[]{:S(2)}, u32[]{:S(2)}) collective-permute-start(s32[384]{0:T(512)S(1)} %copy-done.3), channel_id=1, source_target_pairs={{0,509},{1,510},{2,511},{3,0},{4,1},{5,2},{6,3},{7,4},{8,5},{9,6},... | collective-permute-start | bytes 4616 | tf_op jit(solution)/shard_map/ppermute | solution.py:17
  86.1 10.0 %collective-permute-start.7 = (s32[384]{0:T(512)S(1)}, s32[384]{0:T(512)S(1)}, u32[]{:S(2)}, u32[]{:S(2)}) collective-permute-start(s32[384]{0:T(512)S(1)} %copy-done.3), channel_id=1, source_target_pairs={{0,3},{1,4},{2,5},{3,6},{4,7},{5,8},{6,9},{7,10},{8,11},{9,12},{10... | collective-permute-start | bytes 4616 | tf_op jit(solution)/shard_map/ppermute | solution.py:17
  89.1 9.7 %collective-permute-start.9 = (s32[384]{0:T(512)S(1)}, s32[384]{0:T(512)S(1)}, u32[]{:S(2)}, u32[]{:S(2)}) collective-permute-start(s32[384]{0:T(512)S(1)} %copy-done.3), channel_id=1, source_target_pairs={{0,2},{1,3},{2,4},{3,5},{4,6},{5,7},{6,8},{7,9},{8,10},{9,11},{10,... | collective-permute-start | bytes 4616 | tf_op jit(solution)/shard_map/ppermute | solution.py:17
  91.0 9.1 %collective-permute-start.11 = (s32[384]{0:T(512)S(1)}, s32[384]{0:T(512)S(1)}, u32[]{:S(2)}, u32[]{:S(2)}) collective-permute-start(s32[384]{0:T(512)S(1)} %copy-done.3), channel_id=1, source_target_pairs={{0,1},{1,2},{2,3},{3,4},{4,5},{5,6},{6,7},{7,8},{8,9},{9,10},{10,1... | collective-permute-start | bytes 4616 | tf_op jit(solution)/shard_map/ppermute | solution.py:17
  104.6 24.3 %collective-permute-start.17 = (f32[384,768]{1,0:T(8,128)S(1)}, f32[384,768]{1,0:T(8,128)S(1)}, u32[]{:S(2)}, u32[]{:S(2)}) collective-permute-start(f32[384,768]{1,0:T(8,128)S(1)} %convolution_multiply_fusion), channel_id=1, source_target_pairs={{0,511},{1,0},{2,1},{3,2},{4,3},{5,4},{6,5},{7,6},{8,7},{9,8},{10,... | collective-permute-start | bytes 3538952 | tf_op jit(solution)/shard_map/ppermute | solution.py:17
  107.0 49.8 %collective-permute-start.16 = (f32[384,768]{1,0:T(8,128)S(1)}, f32[384,768]{1,0:T(8,128)S(1)}, u32[]{:S(2)}, u32[]{:S(2)}) collective-permute-start(f32[384,768]{1,0:T(8,128)S(1)} %convolution_multiply_fusion.1), channel_id=1, source_target_pairs={{0,510},{1,511},{2,0},{3,1},{4,2},{5,3},{6,4},{7,5},{8,6},{9,7},{1... | collective-permute-start | bytes 3538952 | tf_op jit(solution)/shard_map/ppermute | solution.py:17
  111.4 72.0 %collective-permute-start.15 = (f32[384,768]{1,0:T(8,128)S(1)}, f32[384,768]{1,0:T(8,128)S(1)}, u32[]{:S(2)}, u32[]{:S(2)}) collective-permute-start(f32[384,768]{1,0:T(8,128)S(1)} %convolution_multiply_fusion.2), channel_id=1, source_target_pairs={{0,509},{1,510},{2,511},{3,0},{4,1},{5,2},{6,3},{7,4},{8,5},{9,6},... | collective-permute-start | bytes 3538952 | tf_op jit(solution)/shard_map/ppermute | solution.py:17
  114.5 68.9 %collective-permute-start.14 = (f32[384,768]{1,0:T(8,128)S(1)}, f32[384,768]{1,0:T(8,128)S(1)}, u32[]{:S(2)}, u32[]{:S(2)}) collective-permute-start(f32[384,768]{1,0:T(8,128)S(1)} %convolution_multiply_fusion.3), channel_id=1, source_target_pairs={{0,3},{1,4},{2,5},{3,6},{4,7},{5,8},{6,9},{7,10},{8,11},{9,12},{10... | collective-permute-start | bytes 3538952 | tf_op jit(solution)/shard_map/ppermute | solution.py:17
  117.9 69.3 %collective-permute-start.13 = (f32[384,768]{1,0:T(8,128)S(1)}, f32[384,768]{1,0:T(8,128)S(1)}, u32[]{:S(2)}, u32[]{:S(2)}) collective-permute-start(f32[384,768]{1,0:T(8,128)S(1)} %convolution_multiply_fusion.4), channel_id=1, source_target_pairs={{0,2},{1,3},{2,4},{3,5},{4,6},{5,7},{6,8},{7,9},{8,10},{9,11},{10,... | collective-permute-start | bytes 3538952 | tf_op jit(solution)/shard_map/ppermute | solution.py:17
  128.9 71.3 %collective-permute-start.12 = (f32[384,768]{1,0:T(8,128)S(1)}, f32[384,768]{1,0:T(8,128)S(1)}, u32[]{:S(2)}, u32[]{:S(2)}) collective-permute-start(f32[384,768]{1,0:T(8,128)S(1)} %convolution_multiply_fusion.5), channel_id=1, source_target_pairs={{0,1},{1,2},{2,3},{3,4},{4,5},{5,6},{6,7},{7,8},{8,9},{9,10},{10,1... | collective-permute-start | bytes 3538952 | tf_op jit(solution)/shard_map/ppermute | solution.py:17
where the time goes:
time: 202 us
  waiting for transfers between devices  122 us (60%)
  starting transfers between devices  57.2 us (28%)
  matrix products  21.5 us (11%)
    ppermute x18, waiting for transfers between devices, shifted(): lax.ppermute(value, axis, [(i, (i + by) % length) for i in range(length)])  122 us
    ppermute x18, starting transfers between devices, shifted(): lax.ppermute(value, axis, [(i, (i + by) % length) for i in range(length)])  57.2 us
    dot_general x7, matrix products, block_terms(): lax.dot_general(student_image_vectors, caption_block, contract, preferred...  7.33 us
    dot_general x7, matrix products, block_terms(): lax.dot_general(teacher_emb, caption_block, contract, preferred_element_t...  5.03 us
    dot_general x7, matrix products, block_terms(): jnp.dot(slope, caption_block, preferred_element_type=jnp.float32)  4.65 us
    dot_general x7, matrix products, block_terms(): lax.dot_general(slope, student_image_vectors, (((0,), (0,)), ((), ())), p...  4.44 us
  transfers between devices with their start and end apart: 18, of which 13 were waited for; matrix products, arithmetic and copies ran while one was open for 8% of the time, Pallas kernels for 0%

commit v1 on v0

v1 whole, which is shorter than its diff:
```python
import jax
import jax.numpy as jnp
from jax import lax
from jax.experimental import pallas as pl
from jax.experimental.pallas import tpu as pltpu
from jax.sharding import PartitionSpec as P

SOFTMAX_TEMP_VALUE = 4.0
LOGIT_BIAS = -3.0
WINDOW = 7
DIGIT = 32.0
LANES = 128
EXTRA = 16

BF16 = jnp.bfloat16
F32 = jnp.float32


def moved(value, even, odd):
    length = lax.axis_size("dp")
    return lax.ppermute(
        value, "dp", [(i, (i + (odd if i % 2 else even)) % length) for i in range(length)]
    )


def within(value):
    return moved(value, 1, -1)


def across(value):
    return moved(value, -1, 1)


def onward(value):
    return moved(value, 2, -2)


def back(value):
    return moved(value, -2, 2)


def call(body, out_shape, flops, *args):
    in_bytes = sum(a.size * a.dtype.itemsize for a in args)
    out_bytes = sum(o.size * o.dtype.itemsize for o in out_shape)
    return pl.pallas_call(
        body,
        out_shape=out_shape,
        in_specs=[pl.BlockSpec(memory_space=pltpu.VMEM)] * len(args),
        out_specs=[pl.BlockSpec(memory_space=pltpu.VMEM)] * len(out_shape),
        compiler_params=pltpu.CompilerParams(vmem_limit_bytes=40 * 1024 * 1024),
        cost_estimate=pl.CostEstimate(
            flops=flops, bytes_accessed=in_bytes + out_bytes, transcendentals=0
        ),
    )(*args)


def digits(species_ref):
    ids = species_ref[...].astype(F32)
    high = jnp.floor(ids / DIGIT)
    low = ids - high * DIGIT
    rows = species_ref.shape[1]
    place = lax.broadcasted_iota(jnp.int32, (EXTRA, rows), 0)
    return jnp.where(place == 0, high, jnp.where(place == 1, low, 0.0)).astype(BF16)


def pack_text(text_ref, species_ref, out_ref):
    rows, width = text_ref.shape
    out_ref[:rows, :] = text_ref[...]
    out_ref[rows:, :rows] = digits(species_ref)
    out_ref[rows:, rows:] = jnp.zeros((EXTRA, width - rows), BF16)


def pack_images(student_ref, teacher_ref, species_ref, out_ref):
    rows, width = student_ref.shape
    out_ref[:rows, :] = student_ref[...]
    out_ref[rows : 2 * rows, :] = teacher_ref[...]
    out_ref[2 * rows :, :rows] = digits(species_ref)
    out_ref[2 * rows :, rows:] = jnp.zeros((EXTRA, width - rows), BF16)


def ids_of(ref, rows, start):
    digit = ref[start : start + EXTRA, :rows].astype(F32)
    return digit[0:1, :] * DIGIT + digit[1:2, :]


def pair(student, teacher, ids, text, text_ids):
    rows, width = student.shape
    half_scale = 0.5 * SOFTMAX_TEMP_VALUE / float(width) ** 0.5
    contract = (((1,), (1,)), ((), ()))
    half_z = (
        lax.dot_general(student, text, contract, preferred_element_type=F32) * half_scale
        + 0.5 * LOGIT_BIAS
    )
    half_w = (
        lax.dot_general(teacher, text, contract, preferred_element_type=F32) * half_scale
        + 0.5 * LOGIT_BIAS
    )
    column = jnp.transpose(jnp.broadcast_to(ids, (LANES, rows)))
    column = jnp.concatenate([column] * (rows // LANES), axis=1)
    shift = jnp.where(column == text_ids, 0.75, 0.25)
    target = 0.25 * jnp.tanh(half_w) + shift
    tanh_z = jnp.tanh(half_z)
    slope = (0.5 * tanh_z + 0.5) - target
    z = half_z + half_z
    loss = (jnp.maximum(z, 0.0) - target * z) - jnp.log(0.5 * jnp.abs(tanh_z) + 0.5)
    folded = sum(loss[:, k : k + LANES] for k in range(0, rows, LANES))
    return slope.astype(BF16), folded


def text_term(slope, student):
    return lax.dot_general(slope, student, (((0,), (0,)), ((), ())), preferred_element_type=F32)


def two_blocks(first, images_ref, other_ref, text_ref, *refs):
    if first:
        own_out, other_out, term_ref = refs
    else:
        own_in, other_in, own_out, other_out, term_ref = refs
    rows, width = term_ref.shape
    text = text_ref[:rows, :]
    text_ids = ids_of(text_ref, rows, rows)
    term = None
    for block, (ref, out) in enumerate(((images_ref, own_out), (other_ref, other_out))):
        student = ref[:rows, :]
        slope, folded = pair(
            student, ref[rows : 2 * rows, :], ids_of(ref, rows, 2 * rows), text, text_ids
        )
        grad = jnp.dot(slope, text, preferred_element_type=F32)
        if not first:
            was = (own_in, other_in)[block]
            grad = grad + was[:, :width]
            folded = folded + was[:, width:]
        out[:, :width] = grad
        out[:, width:] = folded
        part = text_term(slope, student)
        term = part if term is None else term + part
    term_ref[...] = term.astype(term_ref.dtype)


def one_block(images_ref, text_ref, own_in, own_out, term_ref):
    rows, width = term_ref.shape
    text = text_ref[:rows, :]
    student = images_ref[:rows, :]
    slope, folded = pair(
        student,
        images_ref[rows : 2 * rows, :],
        ids_of(images_ref, rows, 2 * rows),
        text,
        ids_of(text_ref, rows, rows),
    )
    own_out[:, :width] = own_in[:, :width] + jnp.dot(slope, text, preferred_element_type=F32)
    own_out[:, width:] = own_in[:, width:] + folded
    term_ref[...] = text_term(slope, student).astype(term_ref.dtype)


def add_far(near_ref, far_ref, out_ref):
    out_ref[...] = (near_ref[...] + far_ref[...].astype(F32)).astype(out_ref.dtype)


def finish_images(own_ref, other_ref, grad_ref, loss_ref):
    rows, width = grad_ref.shape
    scale = SOFTMAX_TEMP_VALUE / float(width) ** 0.5
    grad_ref[...] = (own_ref[:, :width] + other_ref[:, :width]) * scale
    folded = jnp.transpose(own_ref[:, width:] + other_ref[:, width:])
    loss_ref[...] = jnp.sum(folded, axis=0, keepdims=True) / float(WINDOW * rows)


def finish_text(own_ref, after_ref, before_ref, out_ref):
    scale = SOFTMAX_TEMP_VALUE / float(out_ref.shape[1]) ** 0.5
    total = own_ref[...] + after_ref[...].astype(F32) + before_ref[...].astype(F32)
    out_ref[...] = total * scale


def shards(student_image_vectors, teacher_emb, text_emb, species):
    rows, width = text_emb.shape
    dot = 2 * rows * rows * width
    ids = species.reshape(1, rows)

    def spec(n, m, dtype):
        return jax.ShapeDtypeStruct((n, m), dtype)

    sums = spec(rows, width + LANES, F32)
    (text,) = call(pack_text, [spec(rows + EXTRA, width, BF16)], 0, text_emb, ids)
    near = across(text)
    (images,) = call(
        pack_images,
        [spec(2 * rows + EXTRA, width, BF16)],
        0,
        student_image_vectors,
        teacher_emb,
        ids,
    )
    other = within(images)
    second = onward(text)
    far = onward(near)

    own_sum, other_sum, own_term = call(
        lambda *refs: two_blocks(True, *refs),
        [sums, sums, spec(rows, width, F32)],
        8 * dot,
        images,
        other,
        text,
    )
    own_sum, other_sum, near_term = call(
        lambda *refs: two_blocks(False, *refs),
        [sums, sums, spec(rows, width, F32)],
        8 * dot,
        images,
        other,
        near,
        own_sum,
        other_sum,
    )
    own_sum, other_sum, second_term = call(
        lambda *refs: two_blocks(False, *refs),
        [sums, sums, spec(rows, width, BF16)],
        8 * dot,
        images,
        other,
        second,
        own_sum,
        other_sum,
    )
    second_back = back(second_term)
    other_back = within(other_sum)
    own_sum, far_term = call(
        one_block, [sums, spec(rows, width, BF16)], 4 * dot, images, far, own_sum
    )
    far_back = back(far_term)
    (near_total,) = call(add_far, [spec(rows, width, BF16)], 0, near_term, far_back)
    near_back = across(near_total)
    grad_student, loss = call(
        finish_images, [spec(rows, width, F32), spec(1, rows, F32)], 0, own_sum, other_back
    )
    (grad_text,) = call(
        finish_text, [spec(rows, width, F32)], 0, own_term, second_back, near_back
    )
    return grad_student, grad_text, loss.reshape(rows)


def solution(mesh):
    return jax.shard_map(
        shards,
        mesh=mesh,
        in_specs=(P("dp", None), P("dp", None), P("dp", None), P("dp")),
        out_specs=(P("dp", None), P("dp", None), P("dp")),
        check_vma=False,
    )
```

time: 202 us -> 89.1 us (0.44)
  the two profiles are of different devices: /device:TPU:6 before, /device:TPU:1 now
where the time goes in v1:
time: 89.1 us; the launch traced here: 88.7 us
  starting transfers between devices  44.3 us (50%)
  waiting for transfers between devices  26.4 us (30%)
  Pallas kernels  13.8 us (15%)
  local copies, waits for them, and re-layouts  2.88 us (3%)
    ppermute x8, starting transfers between devices, moved(): lax.ppermute(value, 'dp', [(i, (i + (odd if i % 2 else even)) % length) f...  44.3 us
    ppermute x8, waiting for transfers between devices, moved(): lax.ppermute(value, 'dp', [(i, (i + (odd if i % 2 else even)) % length) f...  26.4 us
    pallas_call x9, Pallas kernels, call(): pl.pallas_call(body, out_shape=out_shape, in_specs=[pl.BlockSpec(memory_s...  13.8 us
    unnamed x6, local copies, waits for them, and re-layouts  2.13 us
  transfers between devices with their start and end apart: 8, of which 4 were waited for; matrix products, arithmetic and copies ran while one was open for 0% of the time, Pallas kernels for 14%

profile of v1, /device:TPU:1, one launch (start us, length us, event | category | flops | bytes accessed | tf_op | source)
XLA Modules:
  0.0 88.7 jit_solution(3579809055892960499)
XLA Ops:
  0.6 0.7 reshape.12.species_ref
  1.4 1.1 %copy-done.1 = bf16[384,768]{1,0:T(8,128)(2,1)S(1)} copy-done((bf16[384,768]{1,0:T(8,128)(2,1)S(1)}, bf16[384,768]{1,0:T(8,128)(2,1)}, u32[]{:S(2)}) %copy-start.1) | copy-done | bytes 589848
  2.5 1.1 %copy-done.2 = bf16[384,768]{1,0:T(8,128)(2,1)S(1)} copy-done((bf16[384,768]{1,0:T(8,128)(2,1)S(1)}, bf16[384,768]{1,0:T(8,128)(2,1)}, u32[]{:S(2)}) %copy-start.2) | copy-done | bytes 589848
  3.5 0.1 shard_map.67.refs_0_.images_ref
  3.6 8.8 %collective-permute-start.2 = (bf16[784,768]{1,0:T(8,128)(2,1)S(1)}, bf16[784,768]{1,0:T(8,128)(2,1)S(1)}, u32[]{:S(2)}, u32[]{:S(2)}) collective-permute-start(bf16[784,768]{1,0:T(8,128)(2,1)S(1)} %shard_map.67.refs_0_.images_ref), channel_id=1, source_target_pairs={{0,1},{1,0},{2,3},{3,2},{4,5},{5,4},{6,7},{7,6},{8,9},{9,8},{10,11... | collective-permute-start | bytes 3612680 | tf_op jit(solution)/shard_map/ppermute | solution.py:21
  12.5 1.9 %collective-permute-start = (bf16[400,768]{1,0:T(8,128)(2,1)S(1)}, bf16[400,768]{1,0:T(8,128)(2,1)S(1)}, u32[]{:S(2)}, u32[]{:S(2)}) collective-permute-start(bf16[400,768]{1,0:T(8,128)(2,1)S(1)} %shard_map.68.refs_2_), channel_id=1, source_target_pairs={{0,511},{1,2},{2,1},{3,4},{4,3},{5,6},{6,5},{7,8},{8,7},{9,10},{10... | collective-permute-start | bytes 1843208 | tf_op jit(solution)/shard_map/ppermute | solution.py:21
  14.4 10.4 %collective-permute-start.3 = (bf16[400,768]{1,0:T(8,128)(2,1)S(1)}, bf16[400,768]{1,0:T(8,128)(2,1)S(1)}, u32[]{:S(2)}, u32[]{:S(2)}) collective-permute-start(bf16[400,768]{1,0:T(8,128)(2,1)S(1)} %shard_map.68.refs_2_), channel_id=1, source_target_pairs={{0,2},{1,511},{2,4},{3,1},{4,6},{5,3},{6,8},{7,5},{8,10},{9,7},{10... | collective-permute-start | bytes 1843208 | tf_op jit(solution)/shard_map/ppermute | solution.py:21
  24.8 4.6 %collective-permute-done.refs_2_ = bf16[400,768]{1,0:T(8,128)(2,1)S(1)} collective-permute-done((bf16[400,768]{1,0:T(8,128)(2,1)S(1)}, bf16[400,768]{1,0:T(8,128)(2,1)S(1)}, u32[]{:S(2)}, u32[]{:S(2)}) %collective-permute-start) | collective-permute-done | bytes 614432 | tf_op jit(solution)/shard_map/ppermute | solution.py:21
  29.4 15.5 %collective-permute-start.1 = (bf16[400,768]{1,0:T(8,128)(2,1)S(1)}, bf16[400,768]{1,0:T(8,128)(2,1)S(1)}, u32[]{:S(2)}, u32[]{:S(2)}) collective-permute-start(bf16[400,768]{1,0:T(8,128)(2,1)S(1)} %collective-permute-done.refs_2_), channel_id=1, source_target_pairs={{0,2},{1,511},{2,4},{3,1},{4,6},{5,3},{6,8},{7,5},{8,10},{9,7},{10... | collective-permute-start | bytes 1843208 | tf_op jit(solution)/shard_map/ppermute | solution.py:21
  44.9 3.1 %shard_map.69 = (f32[384,896]{1,0:T(8,128)S(1)}, f32[384,896]{1,0:T(8,128)S(1)}, f32[384,768]{1,0:T(8,128)S(1)}) custom-call(bf16[784,768]{1,0:T(8,128)(2,1)S(1)} %shard_map.67.refs_0_.images_ref, bf16[784,768]{1,0:T(8,128)(2,1)S(1)} %collective-permute-done.2.refs_1_, bf16[400,768]{1,0:T(8,128)(2,1)S(1)} %shard_map.68.refs_2_), custom_call_target="tpu_custom_call" | custom-call | flops 1811939328 | bytes 6955008 | tf_op jit(solution)/shard_map/pallas_call | solution.py:45
  48.1 3.1 %shard_map.70 = (f32[384,896]{1,0:T(8,128)S(1)}, f32[384,896]{1,0:T(8,128)S(1)}, f32[384,768]{1,0:T(8,128)S(1)}) custom-call(bf16[784,768]{1,0:T(8,128)(2,1)S(1)} %shard_map.67.refs_0_.images_ref, bf16[784,768]{1,0:T(8,128)(2,1)S(1)} %collective-permute-done.2.refs_1_, bf16[400,768]{1,0:T(8,128)(2,1)S(1)} %collective-permute-done.refs_2_, ...), custom_call_target="tpu_custom_call" | custom-call | flops 1811939328 | bytes 9707520 | tf_op jit(solution)/shard_map/pallas_call | solution.py:45
  51.2 3.2 %shard_map.71 = (f32[384,896]{1,0:T(8,128)S(1)}, f32[384,896]{1,0:T(8,128)S(1)}, bf16[384,768]{1,0:T(8,128)(2,1)S(1)}) custom-call(bf16[784,768]{1,0:T(8,128)(2,1)S(1)} %shard_map.67.refs_0_.images_ref, bf16[784,768]{1,0:T(8,128)(2,1)S(1)} %collective-permute-done.2.refs_1_, bf16[400,768]{1,0:T(8,128)(2,1)S(1)} %collective-permute-done.3.refs_2_, ...), custom_call_target="tpu_custom_call" | custom-call | flops 1811939328 | bytes 9117696 | tf_op jit(solution)/shard_map/pallas_call | solution.py:45
  54.4 1.9 %collective-permute-start.4 = (f32[384,896]{1,0:T(8,128)S(1)}, f32[384,896]{1,0:T(8,128)S(1)}, u32[]{:S(2)}, u32[]{:S(2)}) collective-permute-start(f32[384,896]{1,0:T(8,128)S(1)} %get-tuple-element.22), channel_id=1, source_target_pairs={{0,1},{1,0},{2,3},{3,2},{4,5},{5,4},{6,7},{7,6},{8,9},{9,8},{10,11... | collective-permute-start | bytes 4128776 | tf_op jit(solution)/shard_map/ppermute | solution.py:21
  56.3 1.6 %shard_map.72 = (f32[384,896]{1,0:T(8,128)S(1)}, bf16[384,768]{1,0:T(8,128)(2,1)S(1)}) custom-call(bf16[784,768]{1,0:T(8,128)(2,1)S(1)} %shard_map.67.refs_0_.images_ref, bf16[400,768]{1,0:T(8,128)(2,1)S(1)} %collective-permute-done.1.text_ref, f32[384,896]{1,0:T(8,128)S(1)} %get-tuple-element.20.own_in), custom_call_target="tpu_custom_call" | custom-call | flops 905969664 | bytes 5160960 | tf_op jit(solution)/shard_map/pallas_call | solution.py:45
  58.0 1.9 %collective-permute-start.6 = (bf16[384,768]{1,0:T(8,128)(2,1)S(1)}, bf16[384,768]{1,0:T(8,128)(2,1)S(1)}, u32[]{:S(2)}, u32[]{:S(2)}) collective-permute-start(bf16[384,768]{1,0:T(8,128)(2,1)S(1)} %get-tuple-element.27), channel_id=1, source_target_pairs={{0,510},{1,3},{2,0},{3,5},{4,2},{5,7},{6,4},{7,9},{8,6},{9,11},{10... | collective-permute-start | bytes 1769480 | tf_op jit(solution)/shard_map/ppermute | solution.py:21
  59.9 1.9 %collective-permute-start.5 = (bf16[384,768]{1,0:T(8,128)(2,1)S(1)}, bf16[384,768]{1,0:T(8,128)(2,1)S(1)}, u32[]{:S(2)}, u32[]{:S(2)}) collective-permute-start(bf16[384,768]{1,0:T(8,128)(2,1)S(1)} %get-tuple-element.25), channel_id=1, source_target_pairs={{0,510},{1,3},{2,0},{3,5},{4,2},{5,7},{6,4},{7,9},{8,6},{9,11},{10... | collective-permute-start | bytes 1769480 | tf_op jit(solution)/shard_map/ppermute | solution.py:21
  61.8 12.2 %collective-permute-done.6.far_ref = bf16[384,768]{1,0:T(8,128)(2,1)S(1)} collective-permute-done((bf16[384,768]{1,0:T(8,128)(2,1)S(1)}, bf16[384,768]{1,0:T(8,128)(2,1)S(1)}, u32[]{:S(2)}, u32[]{:S(2)}) %collective-permute-start.6) | collective-permute-done | bytes 589856 | tf_op jit(solution)/shard_map/ppermute | solution.py:21
  74.0 0.1 shard_map.74
  74.1 1.9 %collective-permute-start.7 = (bf16[384,768]{1,0:T(8,128)(2,1)S(1)}, bf16[384,768]{1,0:T(8,128)(2,1)S(1)}, u32[]{:S(2)}, u32[]{:S(2)}) collective-permute-start(bf16[384,768]{1,0:T(8,128)(2,1)S(1)} %shard_map.74), channel_id=1, source_target_pairs={{0,511},{1,2},{2,1},{3,4},{4,3},{5,6},{6,5},{7,8},{8,7},{9,10},{10... | collective-permute-start | bytes 1769480 | tf_op jit(solution)/shard_map/ppermute | solution.py:21
  76.0 4.3 %collective-permute-done.5.after_ref = bf16[384,768]{1,0:T(8,128)(2,1)S(1)} collective-permute-done((bf16[384,768]{1,0:T(8,128)(2,1)S(1)}, bf16[384,768]{1,0:T(8,128)(2,1)S(1)}, u32[]{:S(2)}, u32[]{:S(2)}) %collective-permute-start.5) | collective-permute-done | bytes 589856 | tf_op jit(solution)/shard_map/ppermute | solution.py:21
  80.3 5.3 %collective-permute-done.7.before_ref = bf16[384,768]{1,0:T(8,128)(2,1)S(1)} collective-permute-done((bf16[384,768]{1,0:T(8,128)(2,1)S(1)}, bf16[384,768]{1,0:T(8,128)(2,1)S(1)}, u32[]{:S(2)}, u32[]{:S(2)}) %collective-permute-start.7) | collective-permute-done | bytes 589856 | tf_op jit(solution)/shard_map/ppermute | solution.py:21
  85.6 1.2 %shard_map.75 = f32[384,768]{1,0:T(8,128)} custom-call(f32[384,768]{1,0:T(8,128)S(1)} %get-tuple-element.24.own_ref, bf16[384,768]{1,0:T(8,128)(2,1)S(1)} %collective-permute-done.5.after_ref, bf16[384,768]{1,0:T(8,128)(2,1)S(1)} %collective-permute-done.7.before_ref), custom_call_target="tpu_custom_call" | custom-call | bytes 3538944 | tf_op jit(solution)/shard_map/pallas_call | solution.py:45
  86.8 1.3 %shard_map.73 = (f32[384,768]{1,0:T(8,128)}, f32[1,384]{1,0:T(1,128)S(1)}) custom-call(f32[384,896]{1,0:T(8,128)S(1)} %get-tuple-element.21.own_ref, f32[384,896]{1,0:T(8,128)S(1)} %collective-permute-done.4.other_ref), custom_call_target="tpu_custom_call" | custom-call | bytes 3933696 | tf_op jit(solution)/shard_map/pallas_call | solution.py:45
  88.1 0.6 reduce
  (9 shorter events, 0.1 us)
Async XLA Ops:
  0.6 11.8 %copy-start = (bf16[384,768]{1,0:T(8,128)(2,1)S(1)}, bf16[384,768]{1,0:T(8,128)(2,1)}, u32[]{:S(2)}) copy-start(bf16[384,768]{1,0:T(8,128)(2,1)} %text_ref.1) | copy-start | bytes 1769476
  1.4 1.1 %copy-start.1 = (bf16[384,768]{1,0:T(8,128)(2,1)S(1)}, bf16[384,768]{1,0:T(8,128)(2,1)}, u32[]{:S(2)}) copy-start(bf16[384,768]{1,0:T(8,128)(2,1)} %student_ref.1) | copy-start | bytes 1769476
  2.5 1.1 %copy-start.2 = (bf16[384,768]{1,0:T(8,128)(2,1)S(1)}, bf16[384,768]{1,0:T(8,128)(2,1)}, u32[]{:S(2)}) copy-start(bf16[384,768]{1,0:T(8,128)(2,1)} %teacher_ref.1) | copy-start | bytes 1769476
  3.6 41.3 %collective-permute-start.2 = (bf16[784,768]{1,0:T(8,128)(2,1)S(1)}, bf16[784,768]{1,0:T(8,128)(2,1)S(1)}, u32[]{:S(2)}, u32[]{:S(2)}) collective-permute-start(bf16[784,768]{1,0:T(8,128)(2,1)S(1)} %shard_map.67.refs_0_.images_ref), channel_id=1, source_target_pairs={{0,1},{1,0},{2,3},{3,2},{4,5},{5,4},{6,7},{7,6},{8,9},{9,8},{10,11... | collective-permute-start | bytes 3612680 | tf_op jit(solution)/shard_map/ppermute | solution.py:21
  12.5 16.9 %collective-permute-start = (bf16[400,768]{1,0:T(8,128)(2,1)S(1)}, bf16[400,768]{1,0:T(8,128)(2,1)S(1)}, u32[]{:S(2)}, u32[]{:S(2)}) collective-permute-start(bf16[400,768]{1,0:T(8,128)(2,1)S(1)} %shard_map.68.refs_2_), channel_id=1, source_target_pairs={{0,511},{1,2},{2,1},{3,4},{4,3},{5,6},{6,5},{7,8},{8,7},{9,10},{10... | collective-permute-start | bytes 1843208 | tf_op jit(solution)/shard_map/ppermute | solution.py:21
  14.4 36.8 %collective-permute-start.3 = (bf16[400,768]{1,0:T(8,128)(2,1)S(1)}, bf16[400,768]{1,0:T(8,128)(2,1)S(1)}, u32[]{:S(2)}, u32[]{:S(2)}) collective-permute-start(bf16[400,768]{1,0:T(8,128)(2,1)S(1)} %shard_map.68.refs_2_), channel_id=1, source_target_pairs={{0,2},{1,511},{2,4},{3,1},{4,6},{5,3},{6,8},{7,5},{8,10},{9,7},{10... | collective-permute-start | bytes 1843208 | tf_op jit(solution)/shard_map/ppermute | solution.py:21
  29.4 26.9 %collective-permute-start.1 = (bf16[400,768]{1,0:T(8,128)(2,1)S(1)}, bf16[400,768]{1,0:T(8,128)(2,1)S(1)}, u32[]{:S(2)}, u32[]{:S(2)}) collective-permute-start(bf16[400,768]{1,0:T(8,128)(2,1)S(1)} %collective-permute-done.refs_2_), channel_id=1, source_target_pairs={{0,2},{1,511},{2,4},{3,1},{4,6},{5,3},{6,8},{7,5},{8,10},{9,7},{10... | collective-permute-start | bytes 1843208 | tf_op jit(solution)/shard_map/ppermute | solution.py:21
  54.4 32.4 %collective-permute-start.4 = (f32[384,896]{1,0:T(8,128)S(1)}, f32[384,896]{1,0:T(8,128)S(1)}, u32[]{:S(2)}, u32[]{:S(2)}) collective-permute-start(f32[384,896]{1,0:T(8,128)S(1)} %get-tuple-element.22), channel_id=1, source_target_pairs={{0,1},{1,0},{2,3},{3,2},{4,5},{5,4},{6,7},{7,6},{8,9},{9,8},{10,11... | collective-permute-start | bytes 4128776 | tf_op jit(solution)/shard_map/ppermute | solution.py:21
  58.0 16.1 %collective-permute-start.6 = (bf16[384,768]{1,0:T(8,128)(2,1)S(1)}, bf16[384,768]{1,0:T(8,128)(2,1)S(1)}, u32[]{:S(2)}, u32[]{:S(2)}) collective-permute-start(bf16[384,768]{1,0:T(8,128)(2,1)S(1)} %get-tuple-element.27), channel_id=1, source_target_pairs={{0,510},{1,3},{2,0},{3,5},{4,2},{5,7},{6,4},{7,9},{8,6},{9,11},{10... | collective-permute-start | bytes 1769480 | tf_op jit(solution)/shard_map/ppermute | solution.py:21
  59.9 20.4 %collective-permute-start.5 = (bf16[384,768]{1,0:T(8,128)(2,1)S(1)}, bf16[384,768]{1,0:T(8,128)(2,1)S(1)}, u32[]{:S(2)}, u32[]{:S(2)}) collective-permute-start(bf16[384,768]{1,0:T(8,128)(2,1)S(1)} %get-tuple-element.25), channel_id=1, source_target_pairs={{0,510},{1,3},{2,0},{3,5},{4,2},{5,7},{6,4},{7,9},{8,6},{9,11},{10... | collective-permute-start | bytes 1769480 | tf_op jit(solution)/shard_map/ppermute | solution.py:21
  74.1 11.5 %collective-permute-start.7 = (bf16[384,768]{1,0:T(8,128)(2,1)S(1)}, bf16[384,768]{1,0:T(8,128)(2,1)S(1)}, u32[]{:S(2)}, u32[]{:S(2)}) collective-permute-start(bf16[384,768]{1,0:T(8,128)(2,1)S(1)} %shard_map.74), channel_id=1, source_target_pairs={{0,511},{1,2},{2,1},{3,4},{4,3},{5,6},{6,5},{7,8},{8,7},{9,10},{10... | collective-permute-start | bytes 1769480 | tf_op jit(solution)/shard_map/ppermute | solution.py:21

commit v2 on v1

v2 whole, which is shorter than its diff:
```python
import jax
import jax.numpy as jnp
from jax import lax
from jax.experimental import pallas as pl
from jax.experimental.pallas import tpu as pltpu
from jax.sharding import PartitionSpec as P

SOFTMAX_TEMP_VALUE = 4.0
LOGIT_BIAS = -3.0
WINDOW = 7
DIGIT = 32.0
LANES = 128
EXTRA = 16

BF16 = jnp.bfloat16
F32 = jnp.float32


def moved(value, even, odd):
    length = lax.axis_size("dp")
    return lax.ppermute(
        value, "dp", [(i, (i + (odd if i % 2 else even)) % length) for i in range(length)]
    )


def within(value):
    return moved(value, 1, -1)


def across(value):
    return moved(value, -1, 1)


def onward(value):
    return moved(value, 2, -2)


def back(value):
    return moved(value, -2, 2)


def call(body, out_shape, flops, *args, after=()):
    count = len(args)

    def ordered(*refs):
        body(*refs[:count], *refs[count + len(after) :])

    in_bytes = sum(a.size * a.dtype.itemsize for a in args)
    out_bytes = sum(o.size * o.dtype.itemsize for o in out_shape)
    return pl.pallas_call(
        ordered,
        out_shape=out_shape,
        in_specs=[pl.BlockSpec(memory_space=pltpu.VMEM)] * count
        + [pl.BlockSpec(memory_space=pl.ANY)] * len(after),
        out_specs=[pl.BlockSpec(memory_space=pltpu.VMEM)] * len(out_shape),
        compiler_params=pltpu.CompilerParams(vmem_limit_bytes=40 * 1024 * 1024),
        cost_estimate=pl.CostEstimate(
            flops=flops, bytes_accessed=in_bytes + out_bytes, transcendentals=0
        ),
    )(*args, *after)


def digits(species_ref):
    rows = species_ref.shape[0]
    ids = species_ref[...].reshape(1, rows).astype(F32)
    high = jnp.floor(ids / DIGIT)
    low = ids - high * DIGIT
    place = lax.broadcasted_iota(jnp.int32, (EXTRA, rows), 0)
    return jnp.where(place == 0, high, jnp.where(place == 1, low, 0.0)).astype(BF16)


def put_digits(species_ref, out_ref, start):
    rows, width = species_ref.shape[0], out_ref.shape[1]
    out_ref[start:, :rows] = digits(species_ref)
    out_ref[start:, rows:] = jnp.zeros((EXTRA, width - rows), BF16)


def pack_text(text_ref, species_ref, out_ref):
    rows = text_ref.shape[0]
    out_ref[:rows, :] = text_ref[...]
    put_digits(species_ref, out_ref, rows)


def pack_images(student_ref, teacher_ref, species_ref, out_ref):
    rows = student_ref.shape[0]
    out_ref[:rows, :] = student_ref[...]
    out_ref[rows : 2 * rows, :] = teacher_ref[...]
    put_digits(species_ref, out_ref, 2 * rows)


def ids_of(ref, rows, start):
    digit = ref[start : start + EXTRA, :rows].astype(F32)
    return digit[0:1, :] * DIGIT + digit[1:2, :]


def pair(student, teacher, ids, text, text_ids):
    rows, width = student.shape
    half_scale = 0.5 * SOFTMAX_TEMP_VALUE / float(width) ** 0.5
    contract = (((1,), (1,)), ((), ()))
    half_z = (
        lax.dot_general(student, text, contract, preferred_element_type=F32) * half_scale
        + 0.5 * LOGIT_BIAS
    )
    half_w = (
        lax.dot_general(teacher, text, contract, preferred_element_type=F32) * half_scale
        + 0.5 * LOGIT_BIAS
    )
    column = jnp.transpose(jnp.broadcast_to(ids, (LANES, rows)))
    column = jnp.concatenate([column] * (rows // LANES), axis=1)
    shift = jnp.where(column == text_ids, 0.75, 0.25)
    target = 0.25 * jnp.tanh(half_w) + shift
    tanh_z = jnp.tanh(half_z)
    slope = (0.5 * tanh_z + 0.5) - target
    z = half_z + half_z
    loss = (jnp.maximum(z, 0.0) - target * z) - jnp.log(0.5 * jnp.abs(tanh_z) + 0.5)
    folded = sum(loss[:, k : k + LANES] for k in range(0, rows, LANES))
    return slope.astype(BF16), folded


def text_term(slope, student):
    return lax.dot_general(slope, student, (((0,), (0,)), ((), ())), preferred_element_type=F32)


def packed_images(ref, rows):
    return ref.at[:rows, :], ref.at[rows : 2 * rows, :], ids_of(ref, rows, 2 * rows)


def add_block(images_ref, text_ref, was_ref, sums_ref):
    rows = sums_ref.shape[0]
    width = text_ref.shape[1]
    student_ref, teacher_ref, ids = packed_images(images_ref, rows)
    text = text_ref[:rows, :]
    student = student_ref[...]
    slope, folded = pair(student, teacher_ref[...], ids, text, ids_of(text_ref, rows, rows))
    grad = jnp.dot(slope, text, preferred_element_type=F32)
    if was_ref is not None:
        grad = grad + was_ref[:, :width]
        folded = folded + was_ref[:, width:]
    sums_ref[:, :width] = grad.astype(sums_ref.dtype)
    sums_ref[:, width:] = folded.astype(sums_ref.dtype)
    return text_term(slope, student)


def own_first(own_ref, text_ref, own_out, term_ref):
    term_ref[...] = add_block(own_ref, text_ref, None, own_out)


def own_next(own_ref, text_ref, own_in, own_out, term_ref):
    term_ref[...] = add_block(own_ref, text_ref, own_in, own_out)


def other_two(other_ref, text_ref, near_ref, own_in, near_in, other_out, own_out, near_out):
    own_out[...] = own_in[...] + add_block(other_ref, text_ref, None, other_out)
    near_out[...] = near_in[...] + add_block(other_ref, near_ref, other_out, other_out)


def both(own_ref, other_ref, text_ref, own_in, other_in, own_out, other_out, term_ref):
    term = add_block(own_ref, text_ref, own_in, own_out)
    term = term + add_block(other_ref, text_ref, other_in, other_out)
    term_ref[...] = term.astype(term_ref.dtype)


def ahead_last(ahead_ref, text_ref, term_in, ahead_out, term_ref):
    term = term_in[...] + add_block(ahead_ref, text_ref, None, ahead_out)
    term_ref[...] = term.astype(term_ref.dtype)


def gather(own_sum, other_back, own_term, second_back, sum_ref, term_ref):
    sum_ref[...] = own_sum[...] + other_back[...]
    term_ref[...] = own_term[...] + second_back[...].astype(F32)


def finish_images(own_ref, ahead_ref, grad_ref, loss_ref):
    rows, width = grad_ref.shape
    scale = SOFTMAX_TEMP_VALUE / float(width) ** 0.5
    total = own_ref[...] + ahead_ref[...].astype(F32)
    grad_ref[...] = total[:, :width] * scale
    folded = jnp.transpose(total[:, width:])
    loss_ref[...] = jnp.sum(folded, axis=0, keepdims=True) / float(WINDOW * rows)


def finish_text(own_ref, near_ref, out_ref):
    scale = SOFTMAX_TEMP_VALUE / float(out_ref.shape[1]) ** 0.5
    out_ref[...] = (own_ref[...] + near_ref[...].astype(F32)) * scale


def shards(student_image_vectors, teacher_emb, text_emb, species):
    rows, width = text_emb.shape
    dot = 2 * rows * rows * width

    def spec(n, m, dtype):
        return jax.ShapeDtypeStruct((n, m), dtype)

    sums = spec(rows, width + LANES, F32)
    term = spec(rows, width, F32)
    sent = spec(rows, width, BF16)
    packed = spec(rows + EXTRA, width, BF16)
    (text,) = call(pack_text, [packed], 0, text_emb, species)
    near = across(text)
    (images,) = call(
        pack_images,
        [spec(2 * rows + EXTRA, width, BF16)],
        0,
        student_image_vectors,
        teacher_emb,
        species,
        after=(text,),
    )
    other = within(images)
    ahead = back(images)
    second = onward(text)
    own_sum, own_term = call(own_first, [sums, term], 4 * dot, images, text)
    own_sum, near_term = call(own_next, [sums, term], 4 * dot, images, near, own_sum)
    other_sum, own_term, near_term = call(
        other_two, [sums, term, term], 8 * dot, other, text, near, own_term, near_term
    )
    ahead_sum, near_term = call(
        ahead_last,
        [spec(rows, width + LANES, BF16), sent],
        4 * dot,
        ahead,
        near,
        near_term,
    )
    near_back = across(near_term)
    ahead_back = onward(ahead_sum)
    own_sum, other_sum, second_term = call(
        both, [sums, sums, sent], 8 * dot, images, other, second, own_sum, other_sum
    )
    second_back = back(second_term)
    other_back = within(other_sum)
    own_sum, own_term = call(
        gather, [sums, term], 16 * dot, own_sum, other_back, own_term, second_back
    )
    grad_student, loss = call(
        finish_images,
        [spec(rows, width, F32), spec(1, rows, F32)],
        0,
        own_sum,
        ahead_back,
    )
    loss = loss.reshape(rows)
    (grad_text,) = call(finish_text, [term], 0, own_term, near_back, after=(loss,))
    return grad_student, grad_text, loss


def solution(mesh):
    return jax.shard_map(
        shards,
        mesh=mesh,
        in_specs=(P("dp", None), P("dp", None), P("dp", None), P("dp")),
        out_specs=(P("dp", None), P("dp", None), P("dp")),
        check_vma=False,
    )
```

time: 89.1 us -> 79.1 us (0.89)
  waiting for transfers between devices: 26.4 us -> 16 us
  starting transfers between devices: 44.3 us -> 45.3 us
    ppermute x8, waiting for transfers between devices: 26.4 us -> 16 us  [moved(): lax.ppermute(value, 'dp', [(i, (i + (odd if i % 2 else even)) % length) f...]
    ppermute x8, starting transfers between devices: 44.3 us -> 45.3 us  [moved(): lax.ppermute(value, 'dp', [(i, (i + (odd if i % 2 else even)) % length) f...]
    unnamed x6 -> x10, local copies, waits for them, and re-layouts: 2.13 us -> 2.81 us
    pallas_call x9 -> x10, Pallas kernels: 13.8 us -> 13.8 us  [call(): pl.pallas_call(ordered, out_shape=out_shape, in_specs=[pl.BlockSpec(memor...]
  transfers between devices with their start and end apart: 8 -> 8, of which waited for: 4 -> 4; matrix products, arithmetic and copies ran while one was open for 0% -> 0% of each run, Pallas kernels for 14% -> 16%
where the time goes in v2:
time: 79.1 us; the launch traced here: 78.7 us
  starting transfers between devices  45.3 us (57%)
  waiting for transfers between devices  16 us (20%)
  Pallas kernels  13.8 us (17%)
  local copies, waits for them, and re-layouts  2.81 us (4%)
    ppermute x8, starting transfers between devices, moved(): lax.ppermute(value, 'dp', [(i, (i + (odd if i % 2 else even)) % length) f...  45.3 us
    ppermute x8, waiting for transfers between devices, moved(): lax.ppermute(value, 'dp', [(i, (i + (odd if i % 2 else even)) % length) f...  16 us
    pallas_call x10, Pallas kernels, call(): pl.pallas_call(ordered, out_shape=out_shape, in_specs=[pl.BlockSpec(memor...  13.8 us
    unnamed x10, local copies, waits for them, and re-layouts  2.81 us
  transfers between devices with their start and end apart: 8, of which 4 were waited for; matrix products, arithmetic and copies ran while one was open for 0% of the time, Pallas kernels for 16%

profile of v2, /device:TPU:1, one launch (start us, length us, event | category | flops | bytes accessed | tf_op | source)
XLA Modules:
  0.0 78.7 jit_solution(7133879844035874894)
XLA Ops:
  0.7 1.1 %copy-done.2 = bf16[384,768]{1,0:T(8,128)(2,1)S(1)} copy-done((bf16[384,768]{1,0:T(8,128)(2,1)S(1)}, bf16[384,768]{1,0:T(8,128)(2,1)}, u32[]{:S(2)}) %copy-start.2) | copy-done | bytes 589848
  1.8 0.7 copy-done.3
  2.5 1.0 %copy-done.1 = bf16[384,768]{1,0:T(8,128)(2,1)S(1)} copy-done((bf16[384,768]{1,0:T(8,128)(2,1)S(1)}, bf16[384,768]{1,0:T(8,128)(2,1)}, u32[]{:S(2)}) %copy-start.1) | copy-done | bytes 589848
  3.5 0.1 shard_map.68.refs_0_
  3.6 8.8 %collective-permute-start = (bf16[784,768]{1,0:T(8,128)(2,1)S(1)}, bf16[784,768]{1,0:T(8,128)(2,1)S(1)}, u32[]{:S(2)}, u32[]{:S(2)}) collective-permute-start(bf16[784,768]{1,0:T(8,128)(2,1)S(1)} %shard_map.68.refs_0_), channel_id=1, source_target_pairs={{0,1},{1,0},{2,3},{3,2},{4,5},{5,4},{6,7},{7,6},{8,9},{9,8},{10,11... | collective-permute-start | bytes 3612680 | tf_op jit(solution)/shard_map/ppermute | solution.py:21
  12.4 1.9 %collective-permute-start.2 = (bf16[400,768]{1,0:T(8,128)(2,1)S(1)}, bf16[400,768]{1,0:T(8,128)(2,1)S(1)}, u32[]{:S(2)}, u32[]{:S(2)}) collective-permute-start(bf16[400,768]{1,0:T(8,128)(2,1)S(1)} %shard_map.67.refs_3_.refs_1_), channel_id=1, source_target_pairs={{0,511},{1,2},{2,1},{3,4},{4,3},{5,6},{6,5},{7,8},{8,7},{9,10},{10... | collective-permute-start | bytes 1843208 | tf_op jit(solution)/shard_map/ppermute | solution.py:21
  14.3 10.4 %collective-permute-start.1 = (bf16[400,768]{1,0:T(8,128)(2,1)S(1)}, bf16[400,768]{1,0:T(8,128)(2,1)S(1)}, u32[]{:S(2)}, u32[]{:S(2)}) collective-permute-start(bf16[400,768]{1,0:T(8,128)(2,1)S(1)} %shard_map.67.refs_3_.refs_1_), channel_id=1, source_target_pairs={{0,2},{1,511},{2,4},{3,1},{4,6},{5,3},{6,8},{7,5},{8,10},{9,7},{10... | collective-permute-start | bytes 1843208 | tf_op jit(solution)/shard_map/ppermute | solution.py:21
  24.7 1.9 %collective-permute-start.5 = (bf16[784,768]{1,0:T(8,128)(2,1)S(1)}, bf16[784,768]{1,0:T(8,128)(2,1)S(1)}, u32[]{:S(2)}, u32[]{:S(2)}) collective-permute-start(bf16[784,768]{1,0:T(8,128)(2,1)S(1)} %shard_map.68.refs_0_), channel_id=1, source_target_pairs={{0,510},{1,3},{2,0},{3,5},{4,2},{5,7},{6,4},{7,9},{8,6},{9,11},{10... | collective-permute-start | bytes 3612680 | tf_op jit(solution)/shard_map/ppermute | solution.py:21
  26.7 1.6 %shard_map.69 = (f32[384,896]{1,0:T(8,128)S(1)}, f32[384,768]{1,0:T(8,128)S(1)}) custom-call(bf16[784,768]{1,0:T(8,128)(2,1)S(1)} %shard_map.68.refs_0_, bf16[400,768]{1,0:T(8,128)(2,1)S(1)} %shard_map.67.refs_3_.refs_1_), custom_call_target="tpu_custom_call" | custom-call | flops 905969664 | bytes 4374528 | tf_op jit(solution)/shard_map/pallas_call | solution.py:50
  28.2 1.1 %collective-permute-done.2.refs_1_.refs_2_ = bf16[400,768]{1,0:T(8,128)(2,1)S(1)} collective-permute-done((bf16[400,768]{1,0:T(8,128)(2,1)S(1)}, bf16[400,768]{1,0:T(8,128)(2,1)S(1)}, u32[]{:S(2)}, u32[]{:S(2)}) %collective-permute-start.2) | collective-permute-done | bytes 614432 | tf_op jit(solution)/shard_map/ppermute | solution.py:21
  29.3 1.6 %shard_map.70 = (f32[384,896]{1,0:T(8,128)S(1)}, f32[384,768]{1,0:T(8,128)S(1)}) custom-call(bf16[784,768]{1,0:T(8,128)(2,1)S(1)} %shard_map.68.refs_0_, bf16[400,768]{1,0:T(8,128)(2,1)S(1)} %collective-permute-done.2.refs_1_.refs_2_, f32[384,896]{1,0:T(8,128)S(1)} %get-tuple-element.19.refs_2_), custom_call_target="tpu_custom_call" | custom-call | flops 905969664 | bytes 5750784 | tf_op jit(solution)/shard_map/pallas_call | solution.py:50
  31.0 3.0 %shard_map.71 = (f32[384,896]{1,0:T(8,128)S(1)}, f32[384,768]{1,0:T(8,128)S(1)}, f32[384,768]{1,0:T(8,128)S(1)}) custom-call(bf16[784,768]{1,0:T(8,128)(2,1)S(1)} %collective-permute-done.refs_0_.refs_1_, bf16[400,768]{1,0:T(8,128)(2,1)S(1)} %shard_map.67.refs_3_.refs_1_, bf16[400,768]{1,0:T(8,128)(2,1)S(1)} %collective-permute-done.2.refs_1_.refs_2_, ...), custom_call_target="tpu_custom_call" | custom-call | flops 1811939328 | bytes 8527872 | tf_op jit(solution)/shard_map/pallas_call | solution.py:50
  34.0 4.4 %collective-permute-done.1.refs_2_ = bf16[400,768]{1,0:T(8,128)(2,1)S(1)} collective-permute-done((bf16[400,768]{1,0:T(8,128)(2,1)S(1)}, bf16[400,768]{1,0:T(8,128)(2,1)S(1)}, u32[]{:S(2)}, u32[]{:S(2)}) %collective-permute-start.1) | collective-permute-done | bytes 614432 | tf_op jit(solution)/shard_map/ppermute | solution.py:21
  38.4 3.1 %shard_map.72 = (f32[384,896]{1,0:T(8,128)S(1)}, f32[384,896]{1,0:T(8,128)S(1)}, bf16[384,768]{1,0:T(8,128)(2,1)S(1)}) custom-call(bf16[784,768]{1,0:T(8,128)(2,1)S(1)} %shard_map.68.refs_0_, bf16[784,768]{1,0:T(8,128)(2,1)S(1)} %collective-permute-done.refs_0_.refs_1_, bf16[400,768]{1,0:T(8,128)(2,1)S(1)} %collective-permute-done.1.refs_2_, ...), custom_call_target="tpu_custom_call" | custom-call | flops 1811939328 | bytes 9117696 | tf_op jit(solution)/shard_map/pallas_call | solution.py:50
  41.5 9.6 %collective-permute-start.3 = (f32[384,896]{1,0:T(8,128)S(1)}, f32[384,896]{1,0:T(8,128)S(1)}, u32[]{:S(2)}, u32[]{:S(2)}) collective-permute-start(f32[384,896]{1,0:T(8,128)S(1)} %get-tuple-element.25), channel_id=1, source_target_pairs={{0,1},{1,0},{2,3},{3,2},{4,5},{5,4},{6,7},{7,6},{8,9},{9,8},{10,11... | collective-permute-start | bytes 4128776 | tf_op jit(solution)/shard_map/ppermute | solution.py:21
  51.2 1.9 %collective-permute-start.4 = (bf16[384,768]{1,0:T(8,128)(2,1)S(1)}, bf16[384,768]{1,0:T(8,128)(2,1)S(1)}, u32[]{:S(2)}, u32[]{:S(2)}) collective-permute-start(bf16[384,768]{1,0:T(8,128)(2,1)S(1)} %get-tuple-element.27), channel_id=1, source_target_pairs={{0,510},{1,3},{2,0},{3,5},{4,2},{5,7},{6,4},{7,9},{8,6},{9,11},{10... | collective-permute-start | bytes 1769480 | tf_op jit(solution)/shard_map/ppermute | solution.py:21
  53.1 1.6 %shard_map.74 = (bf16[384,896]{1,0:T(8,128)(2,1)S(1)}, bf16[384,768]{1,0:T(8,128)(2,1)S(1)}) custom-call(bf16[784,768]{1,0:T(8,128)(2,1)S(1)} %collective-permute-done.5.refs_0_, bf16[400,768]{1,0:T(8,128)(2,1)S(1)} %collective-permute-done.2.refs_1_.refs_2_, f32[384,768]{1,0:T(8,128)S(1)} %get-tuple-element.29.refs_2_), custom_call_target="tpu_custom_call" | custom-call | flops 905969664 | bytes 4276224 | tf_op jit(solution)/shard_map/pallas_call | solution.py:50
  54.7 8.8 %collective-permute-start.6 = (bf16[384,896]{1,0:T(8,128)(2,1)S(1)}, bf16[384,896]{1,0:T(8,128)(2,1)S(1)}, u32[]{:S(2)}, u32[]{:S(2)}) collective-permute-start(bf16[384,896]{1,0:T(8,128)(2,1)S(1)} %get-tuple-element.30), channel_id=1, source_target_pairs={{0,2},{1,511},{2,4},{3,1},{4,6},{5,3},{6,8},{7,5},{8,10},{9,7},{10... | collective-permute-start | bytes 2064392 | tf_op jit(solution)/shard_map/ppermute | solution.py:21
  63.5 1.9 %collective-permute-start.7 = (bf16[384,768]{1,0:T(8,128)(2,1)S(1)}, bf16[384,768]{1,0:T(8,128)(2,1)S(1)}, u32[]{:S(2)}, u32[]{:S(2)}) collective-permute-start(bf16[384,768]{1,0:T(8,128)(2,1)S(1)} %get-tuple-element.33), channel_id=1, source_target_pairs={{0,511},{1,2},{2,1},{3,4},{4,3},{5,6},{6,5},{7,8},{8,7},{9,10},{10... | collective-permute-start | bytes 1769480 | tf_op jit(solution)/shard_map/ppermute | solution.py:21
  65.5 1.8 %collective-permute-done.4.refs_3_ = bf16[384,768]{1,0:T(8,128)(2,1)S(1)} collective-permute-done((bf16[384,768]{1,0:T(8,128)(2,1)S(1)}, bf16[384,768]{1,0:T(8,128)(2,1)S(1)}, u32[]{:S(2)}, u32[]{:S(2)}) %collective-permute-start.4) | collective-permute-done | bytes 589856 | tf_op jit(solution)/shard_map/ppermute | solution.py:21
  67.3 0.2 shard_map.73
  67.5 8.7 %collective-permute-done.6.refs_1_ = bf16[384,896]{1,0:T(8,128)(2,1)S(1)} collective-permute-done((bf16[384,896]{1,0:T(8,128)(2,1)S(1)}, bf16[384,896]{1,0:T(8,128)(2,1)S(1)}, u32[]{:S(2)}, u32[]{:S(2)}) %collective-permute-start.6) | collective-permute-done | bytes 688160 | tf_op jit(solution)/shard_map/ppermute | solution.py:21
  76.2 1.3 %shard_map.75 = (f32[384,768]{1,0:T(8,128)}, f32[1,384]{1,0:T(1,128)S(1)}) custom-call(f32[384,896]{1,0:T(8,128)S(1)} %get-tuple-element.28.refs_0_, bf16[384,896]{1,0:T(8,128)(2,1)S(1)} %collective-permute-done.6.refs_1_), custom_call_target="tpu_custom_call" | custom-call | bytes 3245568 | tf_op jit(solution)/shard_map/pallas_call | solution.py:50
  77.6 1.1 %shard_map.76 = f32[384,768]{1,0:T(8,128)} custom-call(f32[384,768]{1,0:T(8,128)S(1)} %get-tuple-element.32.refs_0_, bf16[384,768]{1,0:T(8,128)(2,1)S(1)} %collective-permute-done.7.refs_1_, f32[384]{0:T(512)S(1)} %reduce.refs_2_), custom_call_target="tpu_custom_call" | custom-call | bytes 2949120 | tf_op jit(solution)/shard_map/pallas_call | solution.py:50
  (13 shorter events, 0.1 us)
Async XLA Ops:
  0.6 1.9 %copy-start = (bf16[384,768]{1,0:T(8,128)(2,1)S(1)}, bf16[384,768]{1,0:T(8,128)(2,1)}, u32[]{:S(2)}) copy-start(bf16[384,768]{1,0:T(8,128)(2,1)} %refs_0_.3) | copy-start | bytes 1769476
  0.6 1.1 %copy-start.2 = (bf16[384,768]{1,0:T(8,128)(2,1)S(1)}, bf16[384,768]{1,0:T(8,128)(2,1)}, u32[]{:S(2)}) copy-start(bf16[384,768]{1,0:T(8,128)(2,1)} %refs_0_.2) | copy-start | bytes 1769476
  1.8 0.7 copy-start.3
  2.4 1.1 %copy-start.1 = (bf16[384,768]{1,0:T(8,128)(2,1)S(1)}, bf16[384,768]{1,0:T(8,128)(2,1)}, u32[]{:S(2)}) copy-start(bf16[384,768]{1,0:T(8,128)(2,1)} %refs_1_.3) | copy-start | bytes 1769476
  3.6 27.4 %collective-permute-start = (bf16[784,768]{1,0:T(8,128)(2,1)S(1)}, bf16[784,768]{1,0:T(8,128)(2,1)S(1)}, u32[]{:S(2)}, u32[]{:S(2)}) collective-permute-start(bf16[784,768]{1,0:T(8,128)(2,1)S(1)} %shard_map.68.refs_0_), channel_id=1, source_target_pairs={{0,1},{1,0},{2,3},{3,2},{4,5},{5,4},{6,7},{7,6},{8,9},{9,8},{10,11... | collective-permute-start | bytes 3612680 | tf_op jit(solution)/shard_map/ppermute | solution.py:21
  12.4 16.9 %collective-permute-start.2 = (bf16[400,768]{1,0:T(8,128)(2,1)S(1)}, bf16[400,768]{1,0:T(8,128)(2,1)S(1)}, u32[]{:S(2)}, u32[]{:S(2)}) collective-permute-start(bf16[400,768]{1,0:T(8,128)(2,1)S(1)} %shard_map.67.refs_3_.refs_1_), channel_id=1, source_target_pairs={{0,511},{1,2},{2,1},{3,4},{4,3},{5,6},{6,5},{7,8},{8,7},{9,10},{10... | collective-permute-start | bytes 1843208 | tf_op jit(solution)/shard_map/ppermute | solution.py:21
  14.3 24.1 %collective-permute-start.1 = (bf16[400,768]{1,0:T(8,128)(2,1)S(1)}, bf16[400,768]{1,0:T(8,128)(2,1)S(1)}, u32[]{:S(2)}, u32[]{:S(2)}) collective-permute-start(bf16[400,768]{1,0:T(8,128)(2,1)S(1)} %shard_map.67.refs_3_.refs_1_), channel_id=1, source_target_pairs={{0,2},{1,511},{2,4},{3,1},{4,6},{5,3},{6,8},{7,5},{8,10},{9,7},{10... | collective-permute-start | bytes 1843208 | tf_op jit(solution)/shard_map/ppermute | solution.py:21
  24.7 28.4 %collective-permute-start.5 = (bf16[784,768]{1,0:T(8,128)(2,1)S(1)}, bf16[784,768]{1,0:T(8,128)(2,1)S(1)}, u32[]{:S(2)}, u32[]{:S(2)}) collective-permute-start(bf16[784,768]{1,0:T(8,128)(2,1)S(1)} %shard_map.68.refs_0_), channel_id=1, source_target_pairs={{0,510},{1,3},{2,0},{3,5},{4,2},{5,7},{6,4},{7,9},{8,6},{9,11},{10... | collective-permute-start | bytes 3612680 | tf_op jit(solution)/shard_map/ppermute | solution.py:21
  41.5 25.7 %collective-permute-start.3 = (f32[384,896]{1,0:T(8,128)S(1)}, f32[384,896]{1,0:T(8,128)S(1)}, u32[]{:S(2)}, u32[]{:S(2)}) collective-permute-start(f32[384,896]{1,0:T(8,128)S(1)} %get-tuple-element.25), channel_id=1, source_target_pairs={{0,1},{1,0},{2,3},{3,2},{4,5},{5,4},{6,7},{7,6},{8,9},{9,8},{10,11... | collective-permute-start | bytes 4128776 | tf_op jit(solution)/shard_map/ppermute | solution.py:21
  51.2 16.1 %collective-permute-start.4 = (bf16[384,768]{1,0:T(8,128)(2,1)S(1)}, bf16[384,768]{1,0:T(8,128)(2,1)S(1)}, u32[]{:S(2)}, u32[]{:S(2)}) collective-permute-start(bf16[384,768]{1,0:T(8,128)(2,1)S(1)} %get-tuple-element.27), channel_id=1, source_target_pairs={{0,510},{1,3},{2,0},{3,5},{4,2},{5,7},{6,4},{7,9},{8,6},{9,11},{10... | collective-permute-start | bytes 1769480 | tf_op jit(solution)/shard_map/ppermute | solution.py:21
  54.7 21.5 %collective-permute-start.6 = (bf16[384,896]{1,0:T(8,128)(2,1)S(1)}, bf16[384,896]{1,0:T(8,128)(2,1)S(1)}, u32[]{:S(2)}, u32[]{:S(2)}) collective-permute-start(bf16[384,896]{1,0:T(8,128)(2,1)S(1)} %get-tuple-element.30), channel_id=1, source_target_pairs={{0,2},{1,511},{2,4},{3,1},{4,6},{5,3},{6,8},{7,5},{8,10},{9,7},{10... | collective-permute-start | bytes 2064392 | tf_op jit(solution)/shard_map/ppermute | solution.py:21
  63.5 14.0 %collective-permute-start.7 = (bf16[384,768]{1,0:T(8,128)(2,1)S(1)}, bf16[384,768]{1,0:T(8,128)(2,1)S(1)}, u32[]{:S(2)}, u32[]{:S(2)}) collective-permute-start(bf16[384,768]{1,0:T(8,128)(2,1)S(1)} %get-tuple-element.33), channel_id=1, source_target_pairs={{0,511},{1,2},{2,1},{3,4},{4,3},{5,6},{6,5},{7,8},{8,7},{9,10},{10... | collective-permute-start | bytes 1769480 | tf_op jit(solution)/shard_map/ppermute | solution.py:21
  77.6 1.2 %copy-start.4 = (f32[384]{0:T(512)}, f32[384]{0:T(512)S(1)}, u32[]{:S(2)}) copy-start(f32[384]{0:T(512)S(1)} %reduce.refs_2_) | copy-start | bytes 4612

commit v3 on v2

v3 whole, which is shorter than its diff:
```python
import jax
import jax.numpy as jnp
from jax import lax
from jax.experimental import pallas as pl
from jax.experimental.pallas import tpu as pltpu
from jax.sharding import PartitionSpec as P

SOFTMAX_TEMP_VALUE = 4.0
LOGIT_BIAS = -3.0
WINDOW = 7
DIGIT = 32.0
LANES = 128
EXTRA = 16

BF16 = jnp.bfloat16
F32 = jnp.float32


def moved(value, even, odd):
    length = lax.axis_size("dp")
    return lax.ppermute(
        value, "dp", [(i, (i + (odd if i % 2 else even)) % length) for i in range(length)]
    )


def within(value):
    return moved(value, 1, -1)


def across(value):
    return moved(value, -1, 1)


def onward(value):
    return moved(value, 2, -2)


def back(value):
    return moved(value, -2, 2)


def call(body, out_shape, flops, *args, after=()):
    count = len(args)

    def ordered(*refs):
        body(*refs[:count], *refs[count + len(after) :])

    in_bytes = sum(a.size * a.dtype.itemsize for a in args)
    out_bytes = sum(o.size * o.dtype.itemsize for o in out_shape)
    return pl.pallas_call(
        ordered,
        out_shape=out_shape,
        in_specs=[pl.BlockSpec(memory_space=pltpu.VMEM)] * count
        + [pl.BlockSpec(memory_space=pl.ANY)] * len(after),
        out_specs=[pl.BlockSpec(memory_space=pltpu.VMEM)] * len(out_shape),
        compiler_params=pltpu.CompilerParams(vmem_limit_bytes=40 * 1024 * 1024),
        cost_estimate=pl.CostEstimate(
            flops=flops, bytes_accessed=in_bytes + out_bytes, transcendentals=0
        ),
    )(*args, *after)


def spread(first, second):
    tiles = [
        row[:, k : k + LANES] for row in (first, second) for k in range(0, row.shape[1], LANES)
    ]
    place = lax.broadcasted_iota(jnp.int32, (EXTRA, LANES), 0)
    out = jnp.zeros((EXTRA, LANES), F32)
    for k, tile in enumerate(tiles):
        out = jnp.where(place == k, tile, out)
    return out.astype(BF16)


def gathered(ref, start, rows):
    tiles = ref[start:, :].astype(F32)
    count = rows // LANES
    first = jnp.concatenate([tiles[k : k + 1, :] for k in range(count)], axis=1)
    second = jnp.concatenate([tiles[k : k + 1, :] for k in range(count, 2 * count)], axis=1)
    return first, second


def digits(species):
    ids = species.reshape(1, species.shape[0]).astype(F32)
    high = jnp.floor(ids / DIGIT)
    return spread(high, ids - high * DIGIT)


def ids_of(ref, rows):
    high, low = gathered(ref, ref.shape[0] - EXTRA, rows)
    return high * DIGIT + low


def put(out_ref, start, value):
    rows = value.shape[0]
    for k in range(value.shape[1] // LANES):
        out_ref[start + k * rows : start + (k + 1) * rows, :] = value[:, k * LANES : (k + 1) * LANES]


def taken(ref, start, rows, width):
    count = width // LANES
    tiles = [ref[start + k * rows : start + (k + 1) * rows, :] for k in range(count)]
    return jnp.concatenate(tiles, axis=1)


def pack_text(text_ref, species_ref, out_ref):
    put(out_ref, 0, text_ref[...])
    out_ref[out_ref.shape[0] - EXTRA :, :] = digits(species_ref[...])


def pack_images(student_ref, teacher_ref, species_ref, out_ref):
    rows, width = student_ref.shape
    put(out_ref, 0, student_ref[...])
    put(out_ref, rows * width // LANES, teacher_ref[...])
    out_ref[out_ref.shape[0] - EXTRA :, :] = digits(species_ref[...])


def pair(student, teacher, ids, text, text_ids):
    rows, width = student.shape
    half_scale = 0.5 * SOFTMAX_TEMP_VALUE / float(width) ** 0.5
    contract = (((1,), (1,)), ((), ()))
    half_z = (
        lax.dot_general(student, text, contract, preferred_element_type=F32) * half_scale
        + 0.5 * LOGIT_BIAS
    )
    half_w = (
        lax.dot_general(teacher, text, contract, preferred_element_type=F32) * half_scale
        + 0.5 * LOGIT_BIAS
    )
    column = jnp.transpose(jnp.broadcast_to(ids, (LANES, rows)))
    column = jnp.concatenate([column] * (rows // LANES), axis=1)
    shift = jnp.where(column == text_ids, 0.75, 0.25)
    target = 0.25 * jnp.tanh(half_w) + shift
    tanh_z = jnp.tanh(half_z)
    slope = (0.5 * tanh_z + 0.5) - target
    z = half_z + half_z
    loss = (jnp.maximum(z, 0.0) - target * z) - jnp.log(0.5 * jnp.abs(tanh_z) + 0.5)
    folded = sum(loss[:, k : k + LANES] for k in range(0, rows, LANES))
    return slope.astype(BF16), folded


def text_term(slope, student):
    return lax.dot_general(slope, student, (((0,), (0,)), ((), ())), preferred_element_type=F32)


def block(images_ref, text_ref, rows):
    width = (text_ref.shape[0] - EXTRA) * LANES // rows
    text = taken(text_ref, 0, rows, width)
    student = taken(images_ref, 0, rows, width)
    teacher = taken(images_ref, rows * width // LANES, rows, width)
    slope, folded = pair(student, teacher, ids_of(images_ref, rows), text, ids_of(text_ref, rows))
    return jnp.dot(slope, text, preferred_element_type=F32), folded, text_term(slope, student)


def own_first(own_ref, text_ref, sums_ref, term_ref):
    rows, width = term_ref.shape
    sums_ref[:, :width], sums_ref[:, width:], term_ref[...] = block(own_ref, text_ref, rows)


def own_next(own_ref, text_ref, sums_in, sums_ref, term_ref):
    rows, width = term_ref.shape
    grad, folded, term_ref[...] = block(own_ref, text_ref, rows)
    sums_ref[:, :width] = sums_in[:, :width] + grad
    sums_ref[:, width:] = sums_in[:, width:] + folded


def other_all(
    other_ref,
    text_ref,
    near_ref,
    second_ref,
    own_in,
    near_in,
    second_in,
    sums_ref,
    own_out,
    near_out,
    second_out,
):
    rows, width = own_in.shape
    texts = (
        (second_ref, second_in, second_out),
        (near_ref, near_in, near_out),
        (text_ref, own_in, own_out),
    )
    for count, (ref, term_in, term_out) in enumerate(texts):
        grad, folded, term = block(other_ref, ref, rows)
        term_out[...] = (term_in[...] + term).astype(term_out.dtype)
        if count:
            grad = sums_ref[:, :width] + grad
            folded = sums_ref[:, width:] + folded
        sums_ref[:, :width] = grad
        sums_ref[:, width:] = folded


def loss_row(folded):
    return jnp.sum(jnp.transpose(folded), axis=0, keepdims=True)


def ahead_last(ahead_ref, text_ref, term_in, ahead_out, term_ref):
    rows, width = term_ref.shape
    grad, folded, term = block(ahead_ref, text_ref, rows)
    term_ref[...] = (term_in[...] + term).astype(term_ref.dtype)
    put(ahead_out, 0, grad.astype(BF16))
    loss = loss_row(folded)
    high = loss.astype(BF16).astype(F32)
    ahead_out[ahead_out.shape[0] - EXTRA :, :] = spread(high, loss - high)


def gather_text(own_ref, second_ref, term_ref):
    term_ref[...] = own_ref[...] + second_ref[...].astype(F32)


def gather_images(own_ref, ahead_ref, sums_ref, loss_ref):
    rows, width = own_ref.shape[0], own_ref.shape[1] - LANES
    sums_ref[...] = own_ref[:, :width] + taken(ahead_ref, 0, rows, width).astype(F32)
    high, low = gathered(ahead_ref, ahead_ref.shape[0] - EXTRA, rows)
    loss_ref[...] = loss_row(own_ref[:, width:]) + high + low


def finish_images(sums_in, loss_in, other_ref, grad_ref, loss_ref, done_ref):
    rows, width = grad_ref.shape
    scale = SOFTMAX_TEMP_VALUE / float(width) ** 0.5
    grad_ref[...] = (sums_in[...] + other_ref[:, :width]) * scale
    loss = loss_in[...] + loss_row(other_ref[:, width:])
    loss_ref[...] = (loss / float(WINDOW * rows)).reshape(rows)
    done_ref[...] = jnp.zeros_like(done_ref)


def finish_text(own_ref, near_ref, out_ref):
    scale = SOFTMAX_TEMP_VALUE / float(out_ref.shape[1]) ** 0.5
    out_ref[...] = (own_ref[...] + near_ref[...].astype(F32)) * scale


def shards(student_image_vectors, teacher_emb, text_emb, species):
    rows, width = text_emb.shape
    dot = 2 * rows * rows * width

    def spec(n, m, dtype):
        return jax.ShapeDtypeStruct((n, m), dtype)

    sums = spec(rows, width + LANES, F32)
    term = spec(rows, width, F32)
    sent = spec(rows, width, BF16)
    packed = spec(rows * width // LANES + EXTRA, LANES, BF16)
    (text,) = call(pack_text, [packed], 0, text_emb, species)
    near = across(text)
    second = onward(text)
    (images,) = call(
        pack_images,
        [spec(2 * rows * width // LANES + EXTRA, LANES, BF16)],
        0,
        student_image_vectors,
        teacher_emb,
        species,
        after=(text,),
    )
    ahead = back(images)
    other = within(images)
    own_sum, own_term = call(own_first, [sums, term], 4 * dot, images, text)
    own_sum, near_term = call(own_next, [sums, term], 32 * dot, images, near, own_sum)
    own_sum, second_term = call(own_next, [sums, term], 32 * dot, images, second, own_sum)
    other_sum, own_term, near_term, second_term = call(
        other_all,
        [sums, term, term, sent],
        12 * dot,
        other,
        text,
        near,
        second,
        own_term,
        near_term,
        second_term,
    )
    second_back = back(second_term)
    other_back = within(other_sum)
    ahead_sum, near_term = call(
        ahead_last, [packed, sent], 4 * dot, ahead, near, near_term
    )
    near_back = across(near_term)
    ahead_back = onward(ahead_sum)
    (own_term,) = call(gather_text, [term], 64 * dot, own_term, second_back)
    own_sum, loss = call(
        gather_images, [term, spec(1, rows, F32)], 32 * dot, own_sum, ahead_back, after=(own_term,)
    )
    grad_student, loss, done = call(
        finish_images,
        [term, jax.ShapeDtypeStruct((rows,), F32), spec(8, LANES, F32)],
        0,
        own_sum,
        loss,
        other_back,
    )
    (grad_text,) = call(finish_text, [term], 0, own_term, near_back, after=(done,))
    return grad_student, grad_text, loss


def solution(mesh):
    return jax.shard_map(
        shards,
        mesh=mesh,
        in_specs=(P("dp", None), P("dp", None), P("dp", None), P("dp")),
        out_specs=(P("dp", None), P("dp", None), P("dp")),
        check_vma=False,
    )
```

time: 79.1 us -> 73.6 us (0.930)
  starting transfers between devices: 45.3 us -> 41.1 us
  local copies, waits for them, and re-layouts: 2.81 us -> 1.81 us
    ppermute x8, starting transfers between devices: 45.3 us -> 41.1 us  [moved(): lax.ppermute(value, 'dp', [(i, (i + (odd if i % 2 else even)) % length) f...]
    unnamed x10 -> x8, local copies, waits for them, and re-layouts: 2.81 us -> 1.81 us
    pallas_call x10 -> x11, Pallas kernels: 13.8 us -> 13.8 us  [call(): pl.pallas_call(ordered, out_shape=out_shape, in_specs=[pl.BlockSpec(memor...]
  transfers between devices with their start and end apart: 8 -> 8, of which waited for: 4 -> 3; matrix products, arithmetic and copies ran while one was open for 0% -> 0% of each run, Pallas kernels for 16% -> 17%
where the time goes in v3:
time: 73.6 us; the launch traced here: 73.3 us
  starting transfers between devices  41.1 us (56%)
  waiting for transfers between devices  15.8 us (21%)
  Pallas kernels  13.8 us (19%)
  local copies, waits for them, and re-layouts  1.81 us (2%)
  between operations  0.81 us (1%)
    ppermute x8, starting transfers between devices, moved(): lax.ppermute(value, 'dp', [(i, (i + (odd if i % 2 else even)) % length) f...  41.1 us
    ppermute x8, waiting for transfers between devices, moved(): lax.ppermute(value, 'dp', [(i, (i + (odd if i % 2 else even)) % length) f...  15.8 us
    pallas_call x11, Pallas kernels, call(): pl.pallas_call(ordered, out_shape=out_shape, in_specs=[pl.BlockSpec(memor...  13.8 us
    unnamed x8, local copies, waits for them, and re-layouts  1.81 us
  transfers between devices with their start and end apart: 8, of which 3 were waited for; matrix products, arithmetic and copies ran while one was open for 0% of the time, Pallas kernels for 17%

profile of v3, /device:TPU:1, one launch (start us, length us, event | category | flops | bytes accessed | tf_op | source)
XLA Modules:
  0.0 73.3 jit_solution(15851462458666234334)
XLA Ops:
  0.7 1.1 %copy-done.2 = bf16[384,768]{1,0:T(8,128)(2,1)S(1)} copy-done((bf16[384,768]{1,0:T(8,128)(2,1)S(1)}, bf16[384,768]{1,0:T(8,128)(2,1)}, u32[]{:S(2)}) %copy-start.2) | copy-done | bytes 589848
  1.8 0.7 copy-done.3
  2.5 0.1 shard_map.67.refs_3_.refs_1_
  2.5 4.7 %collective-permute-start.1 = (bf16[2320,128]{1,0:T(8,128)(2,1)S(1)}, bf16[2320,128]{1,0:T(8,128)(2,1)S(1)}, u32[]{:S(2)}, u32[]{:S(2)}) collective-permute-start(bf16[2320,128]{1,0:T(8,128)(2,1)S(1)} %shard_map.67.refs_3_.refs_1_), channel_id=1, source_target_pairs={{0,511},{1,2},{2,1},{3,4},{4,3},{5,6},{6,5},{7,8},{8,7},{9,10},{10... | collective-permute-start | bytes 1781768 | tf_op jit(solution)/shard_map/ppermute | solution.py:21
  7.3 13.9 %collective-permute-start = (bf16[2320,128]{1,0:T(8,128)(2,1)S(1)}, bf16[2320,128]{1,0:T(8,128)(2,1)S(1)}, u32[]{:S(2)}, u32[]{:S(2)}) collective-permute-start(bf16[2320,128]{1,0:T(8,128)(2,1)S(1)} %shard_map.67.refs_3_.refs_1_), channel_id=1, source_target_pairs={{0,2},{1,511},{2,4},{3,1},{4,6},{5,3},{6,8},{7,5},{8,10},{9,7},{10... | collective-permute-start | bytes 1781768 | tf_op jit(solution)/shard_map/ppermute | solution.py:21
  21.2 0.2 shard_map.68.refs_0_
  21.4 1.9 %collective-permute-start.2 = (bf16[4624,128]{1,0:T(8,128)(2,1)S(1)}, bf16[4624,128]{1,0:T(8,128)(2,1)S(1)}, u32[]{:S(2)}, u32[]{:S(2)}) collective-permute-start(bf16[4624,128]{1,0:T(8,128)(2,1)S(1)} %shard_map.68.refs_0_), channel_id=1, source_target_pairs={{0,510},{1,3},{2,0},{3,5},{4,2},{5,7},{6,4},{7,9},{8,6},{9,11},{10... | collective-permute-start | bytes 3551240 | tf_op jit(solution)/shard_map/ppermute | solution.py:21
  23.3 9.7 %collective-permute-start.3 = (bf16[4624,128]{1,0:T(8,128)(2,1)S(1)}, bf16[4624,128]{1,0:T(8,128)(2,1)S(1)}, u32[]{:S(2)}, u32[]{:S(2)}) collective-permute-start(bf16[4624,128]{1,0:T(8,128)(2,1)S(1)} %shard_map.68.refs_0_), channel_id=1, source_target_pairs={{0,1},{1,0},{2,3},{3,2},{4,5},{5,4},{6,7},{7,6},{8,9},{9,8},{10,11... | collective-permute-start | bytes 3551240 | tf_op jit(solution)/shard_map/ppermute | solution.py:21
  33.1 1.6 %shard_map.69 = (f32[384,896]{1,0:T(8,128)S(1)}, f32[384,768]{1,0:T(8,128)S(1)}) custom-call(bf16[4624,128]{1,0:T(8,128)(2,1)S(1)} %shard_map.68.refs_0_, bf16[2320,128]{1,0:T(8,128)(2,1)S(1)} %shard_map.67.refs_3_.refs_1_), custom_call_target="tpu_custom_call" | custom-call | flops 905969664 | bytes 4333568 | tf_op jit(solution)/shard_map/pallas_call | solution.py:50
  34.6 1.6 %shard_map.70 = (f32[384,896]{1,0:T(8,128)S(1)}, f32[384,768]{1,0:T(8,128)S(1)}) custom-call(bf16[4624,128]{1,0:T(8,128)(2,1)S(1)} %shard_map.68.refs_0_, bf16[2320,128]{1,0:T(8,128)(2,1)S(1)} %collective-permute-done.1.refs_1_.refs_2_, f32[384,896]{1,0:T(8,128)S(1)} %get-tuple-element.20.refs_2_), custom_call_target="tpu_custom_call" | custom-call | flops 7247757312 | bytes 5709824 | tf_op jit(solution)/shard_map/pallas_call | solution.py:50
  36.2 1.6 %shard_map.71 = (f32[384,896]{1,0:T(8,128)S(1)}, f32[384,768]{1,0:T(8,128)S(1)}) custom-call(bf16[4624,128]{1,0:T(8,128)(2,1)S(1)} %shard_map.68.refs_0_, bf16[2320,128]{1,0:T(8,128)(2,1)S(1)} %collective-permute-done.refs_1_.refs_3_, f32[384,896]{1,0:T(8,128)S(1)} %get-tuple-element.21.refs_2_), custom_call_target="tpu_custom_call" | custom-call | flops 7247757312 | bytes 5709824 | tf_op jit(solution)/shard_map/pallas_call | solution.py:50
  37.9 4.4 %shard_map.72 = (f32[384,896]{1,0:T(8,128)S(1)}, f32[384,768]{1,0:T(8,128)S(1)}, f32[384,768]{1,0:T(8,128)S(1)}, bf16[384,768]{1,0:T(8,128)(2,1)S(1)}) custom-call(bf16[4624,128]{1,0:T(8,128)(2,1)S(1)} %collective-permute-done.3.refs_0_, bf16[2320,128]{1,0:T(8,128)(2,1)S(1)} %shard_map.67.refs_3_.refs_1_, ...), custom_call_target="tpu_custom_call" | custom-call | flops 2717908992 | bytes 10829824 | tf_op jit(solution)/shard_map/pallas_call | solution.py:50
  42.3 1.9 %collective-permute-start.5 = (bf16[384,768]{1,0:T(8,128)(2,1)S(1)}, bf16[384,768]{1,0:T(8,128)(2,1)S(1)}, u32[]{:S(2)}, u32[]{:S(2)}) collective-permute-start(bf16[384,768]{1,0:T(8,128)(2,1)S(1)} %get-tuple-element.29), channel_id=1, source_target_pairs={{0,510},{1,3},{2,0},{3,5},{4,2},{5,7},{6,4},{7,9},{8,6},{9,11},{10... | collective-permute-start | bytes 1769480 | tf_op jit(solution)/shard_map/ppermute | solution.py:21
  44.2 4.7 %collective-permute-done.2.refs_0_ = bf16[4624,128]{1,0:T(8,128)(2,1)S(1)} collective-permute-done((bf16[4624,128]{1,0:T(8,128)(2,1)S(1)}, bf16[4624,128]{1,0:T(8,128)(2,1)S(1)}, u32[]{:S(2)}, u32[]{:S(2)}) %collective-permute-start.2) | collective-permute-done | bytes 1183776 | tf_op jit(solution)/shard_map/ppermute | solution.py:21
  48.9 1.6 %shard_map.73 = (bf16[2320,128]{1,0:T(8,128)(2,1)S(1)}, bf16[384,768]{1,0:T(8,128)(2,1)S(1)}) custom-call(bf16[4624,128]{1,0:T(8,128)(2,1)S(1)} %collective-permute-done.2.refs_0_, bf16[2320,128]{1,0:T(8,128)(2,1)S(1)} %collective-permute-done.1.refs_1_.refs_2_, f32[384,768]{1,0:T(8,128)S(1)} %get-tuple-element.26.refs_2_), custom_call_target="tpu_custom_call" | custom-call | flops 905969664 | bytes 4141056 | tf_op jit(solution)/shard_map/pallas_call | solution.py:50
  50.5 4.1 %collective-permute-start.4 = (bf16[2320,128]{1,0:T(8,128)(2,1)S(1)}, bf16[2320,128]{1,0:T(8,128)(2,1)S(1)}, u32[]{:S(2)}, u32[]{:S(2)}) collective-permute-start(bf16[2320,128]{1,0:T(8,128)(2,1)S(1)} %get-tuple-element.27), channel_id=1, source_target_pairs={{0,2},{1,511},{2,4},{3,1},{4,6},{5,3},{6,8},{7,5},{8,10},{9,7},{10... | collective-permute-start | bytes 1781768 | tf_op jit(solution)/shard_map/ppermute | solution.py:21
  54.6 2.8 %collective-permute-start.6 = (f32[384,896]{1,0:T(8,128)S(1)}, f32[384,896]{1,0:T(8,128)S(1)}, u32[]{:S(2)}, u32[]{:S(2)}) collective-permute-start(f32[384,896]{1,0:T(8,128)S(1)} %get-tuple-element.32), channel_id=1, source_target_pairs={{0,1},{1,0},{2,3},{3,2},{4,5},{5,4},{6,7},{7,6},{8,9},{9,8},{10,11... | collective-permute-start | bytes 4128776 | tf_op jit(solution)/shard_map/ppermute | solution.py:21
  57.4 1.9 %collective-permute-start.7 = (bf16[384,768]{1,0:T(8,128)(2,1)S(1)}, bf16[384,768]{1,0:T(8,128)(2,1)S(1)}, u32[]{:S(2)}, u32[]{:S(2)}) collective-permute-start(bf16[384,768]{1,0:T(8,128)(2,1)S(1)} %get-tuple-element.34), channel_id=1, source_target_pairs={{0,511},{1,2},{2,1},{3,4},{4,3},{5,6},{6,5},{7,8},{8,7},{9,10},{10... | collective-permute-start | bytes 1769480 | tf_op jit(solution)/shard_map/ppermute | solution.py:21
  59.3 0.1 shard_map.74.refs_2_.refs_0_
  59.5 8.4 %collective-permute-done.4.refs_1_ = bf16[2320,128]{1,0:T(8,128)(2,1)S(1)} collective-permute-done((bf16[2320,128]{1,0:T(8,128)(2,1)S(1)}, bf16[2320,128]{1,0:T(8,128)(2,1)S(1)}, u32[]{:S(2)}, u32[]{:S(2)}) %collective-permute-start.4) | collective-permute-done | bytes 593952 | tf_op jit(solution)/shard_map/ppermute | solution.py:21
  67.9 0.2 shard_map.75
  68.1 1.4 %shard_map.76 = (f32[384,768]{1,0:T(8,128)}, f32[384]{0:T(512)}, f32[8,128]{1,0:T(8,128)S(1)}) custom-call(f32[384,768]{1,0:T(8,128)S(1)} %get-tuple-element.30.refs_0_, f32[1,384]{1,0:T(1,128)S(1)} %get-tuple-element.31.refs_1_, f32[384,896]{1,0:T(8,128)S(1)} %collective-permute-done.6.refs_2_), custom_call_target="tpu_custom_call" | custom-call | bytes 3742720 | tf_op jit(solution)/shard_map/pallas_call | solution.py:50
  69.4 2.7 %collective-permute-done.7.refs_1_ = bf16[384,768]{1,0:T(8,128)(2,1)S(1)} collective-permute-done((bf16[384,768]{1,0:T(8,128)(2,1)S(1)}, bf16[384,768]{1,0:T(8,128)(2,1)S(1)}, u32[]{:S(2)}, u32[]{:S(2)}) %collective-permute-start.7) | collective-permute-done | bytes 589856 | tf_op jit(solution)/shard_map/ppermute | solution.py:21
  72.1 1.1 %shard_map.77 = f32[384,768]{1,0:T(8,128)} custom-call(f32[384,768]{1,0:T(8,128)S(1)} %shard_map.74.refs_2_.refs_0_, bf16[384,768]{1,0:T(8,128)(2,1)S(1)} %collective-permute-done.7.refs_1_, f32[8,128]{1,0:T(8,128)S(1)} %get-tuple-element.35.refs_2_), custom_call_target="tpu_custom_call" | custom-call | bytes 2949120 | tf_op jit(solution)/shard_map/pallas_call | solution.py:50
  (11 shorter events, 0.0 us)
Async XLA Ops:
  0.6 20.6 %copy-start = (bf16[384,768]{1,0:T(8,128)(2,1)S(1)}, bf16[384,768]{1,0:T(8,128)(2,1)}, u32[]{:S(2)}) copy-start(bf16[384,768]{1,0:T(8,128)(2,1)} %refs_0_.3) | copy-start | bytes 1769476
  0.6 1.1 %copy-start.2 = (bf16[384,768]{1,0:T(8,128)(2,1)S(1)}, bf16[384,768]{1,0:T(8,128)(2,1)}, u32[]{:S(2)}) copy-start(bf16[384,768]{1,0:T(8,128)(2,1)} %refs_0_.2) | copy-start | bytes 1769476
  1.8 0.7 copy-start.3
  2.4 18.8 %copy-start.1 = (bf16[384,768]{1,0:T(8,128)(2,1)S(1)}, bf16[384,768]{1,0:T(8,128)(2,1)}, u32[]{:S(2)}) copy-start(bf16[384,768]{1,0:T(8,128)(2,1)} %refs_1_.3) | copy-start | bytes 1769476
  2.5 32.1 %collective-permute-start.1 = (bf16[2320,128]{1,0:T(8,128)(2,1)S(1)}, bf16[2320,128]{1,0:T(8,128)(2,1)S(1)}, u32[]{:S(2)}, u32[]{:S(2)}) collective-permute-start(bf16[2320,128]{1,0:T(8,128)(2,1)S(1)} %shard_map.67.refs_3_.refs_1_), channel_id=1, source_target_pairs={{0,511},{1,2},{2,1},{3,4},{4,3},{5,6},{6,5},{7,8},{8,7},{9,10},{10... | collective-permute-start | bytes 1781768 | tf_op jit(solution)/shard_map/ppermute | solution.py:21
  7.3 29.0 %collective-permute-start = (bf16[2320,128]{1,0:T(8,128)(2,1)S(1)}, bf16[2320,128]{1,0:T(8,128)(2,1)S(1)}, u32[]{:S(2)}, u32[]{:S(2)}) collective-permute-start(bf16[2320,128]{1,0:T(8,128)(2,1)S(1)} %shard_map.67.refs_3_.refs_1_), channel_id=1, source_target_pairs={{0,2},{1,511},{2,4},{3,1},{4,6},{5,3},{6,8},{7,5},{8,10},{9,7},{10... | collective-permute-start | bytes 1781768 | tf_op jit(solution)/shard_map/ppermute | solution.py:21
  21.4 27.5 %collective-permute-start.2 = (bf16[4624,128]{1,0:T(8,128)(2,1)S(1)}, bf16[4624,128]{1,0:T(8,128)(2,1)S(1)}, u32[]{:S(2)}, u32[]{:S(2)}) collective-permute-start(bf16[4624,128]{1,0:T(8,128)(2,1)S(1)} %shard_map.68.refs_0_), channel_id=1, source_target_pairs={{0,510},{1,3},{2,0},{3,5},{4,2},{5,7},{6,4},{7,9},{8,6},{9,11},{10... | collective-permute-start | bytes 3551240 | tf_op jit(solution)/shard_map/ppermute | solution.py:21
  23.3 14.5 %collective-permute-start.3 = (bf16[4624,128]{1,0:T(8,128)(2,1)S(1)}, bf16[4624,128]{1,0:T(8,128)(2,1)S(1)}, u32[]{:S(2)}, u32[]{:S(2)}) collective-permute-start(bf16[4624,128]{1,0:T(8,128)(2,1)S(1)} %shard_map.68.refs_0_), channel_id=1, source_target_pairs={{0,1},{1,0},{2,3},{3,2},{4,5},{5,4},{6,7},{7,6},{8,9},{9,8},{10,11... | collective-permute-start | bytes 3551240 | tf_op jit(solution)/shard_map/ppermute | solution.py:21
  42.3 17.0 %collective-permute-start.5 = (bf16[384,768]{1,0:T(8,128)(2,1)S(1)}, bf16[384,768]{1,0:T(8,128)(2,1)S(1)}, u32[]{:S(2)}, u32[]{:S(2)}) collective-permute-start(bf16[384,768]{1,0:T(8,128)(2,1)S(1)} %get-tuple-element.29), channel_id=1, source_target_pairs={{0,510},{1,3},{2,0},{3,5},{4,2},{5,7},{6,4},{7,9},{8,6},{9,11},{10... | collective-permute-start | bytes 1769480 | tf_op jit(solution)/shard_map/ppermute | solution.py:21
  50.5 17.4 %collective-permute-start.4 = (bf16[2320,128]{1,0:T(8,128)(2,1)S(1)}, bf16[2320,128]{1,0:T(8,128)(2,1)S(1)}, u32[]{:S(2)}, u32[]{:S(2)}) collective-permute-start(bf16[2320,128]{1,0:T(8,128)(2,1)S(1)} %get-tuple-element.27), channel_id=1, source_target_pairs={{0,2},{1,511},{2,4},{3,1},{4,6},{5,3},{6,8},{7,5},{8,10},{9,7},{10... | collective-permute-start | bytes 1781768 | tf_op jit(solution)/shard_map/ppermute | solution.py:21
  54.6 13.5 %collective-permute-start.6 = (f32[384,896]{1,0:T(8,128)S(1)}, f32[384,896]{1,0:T(8,128)S(1)}, u32[]{:S(2)}, u32[]{:S(2)}) collective-permute-start(f32[384,896]{1,0:T(8,128)S(1)} %get-tuple-element.32), channel_id=1, source_target_pairs={{0,1},{1,0},{2,3},{3,2},{4,5},{5,4},{6,7},{7,6},{8,9},{9,8},{10,11... | collective-permute-start | bytes 4128776 | tf_op jit(solution)/shard_map/ppermute | solution.py:21
  57.4 14.7 %collective-permute-start.7 = (bf16[384,768]{1,0:T(8,128)(2,1)S(1)}, bf16[384,768]{1,0:T(8,128)(2,1)S(1)}, u32[]{:S(2)}, u32[]{:S(2)}) collective-permute-start(bf16[384,768]{1,0:T(8,128)(2,1)S(1)} %get-tuple-element.34), channel_id=1, source_target_pairs={{0,511},{1,2},{2,1},{3,4},{4,3},{5,6},{6,5},{7,8},{8,7},{9,10},{10... | collective-permute-start | bytes 1769480 | tf_op jit(solution)/shard_map/ppermute | solution.py:21

commit v4 on v3

--- a/solution.py
+++ b/solution.py
@@ -107,11 +107,14 @@
     out_ref[out_ref.shape[0] - EXTRA :, :] = digits(species_ref[...])
 
 
-def pack_images(student_ref, teacher_ref, species_ref, out_ref):
+def pack_images(student_ref, teacher_ref, species_ref, out_ref, teacher_out):
     rows, width = student_ref.shape
+    ids = digits(species_ref[...])
     put(out_ref, 0, student_ref[...])
     put(out_ref, rows * width // LANES, teacher_ref[...])
-    out_ref[out_ref.shape[0] - EXTRA :, :] = digits(species_ref[...])
+    out_ref[out_ref.shape[0] - EXTRA :, :] = ids
+    put(teacher_out, 0, teacher_ref[...])
+    teacher_out[teacher_out.shape[0] - EXTRA :, :] = ids
 
 
 def pair(student, teacher, ids, text, text_ids):
@@ -142,63 +145,84 @@
     return lax.dot_general(slope, student, (((0,), (0,)), ((), ())), preferred_element_type=F32)
 
 
-def block(images_ref, text_ref, rows):
-    width = (text_ref.shape[0] - EXTRA) * LANES // rows
-    text = taken(text_ref, 0, rows, width)
-    student = taken(images_ref, 0, rows, width)
-    teacher = taken(images_ref, rows * width // LANES, rows, width)
-    slope, folded = pair(student, teacher, ids_of(images_ref, rows), text, ids_of(text_ref, rows))
-    return jnp.dot(slope, text, preferred_element_type=F32), folded, text_term(slope, student)
+def unpacked(ref, rows):
+    width = (ref.shape[0] - EXTRA) * LANES // rows
+    return taken(ref, 0, rows, width), ids_of(ref, rows)
+
+
+def both_images(ref, rows):
+    size = (ref.shape[0] - EXTRA) // 2
+    width = size * LANES // rows
+    return taken(ref, 0, rows, width), taken(ref, size, rows, width), ids_of(ref, rows)
+
+
+def block(images, texts):
+    student, teacher, ids = images
+    slope, folded = pair(student, teacher, ids, *texts)
+    grad = jnp.dot(slope, texts[0], preferred_element_type=F32)
+    return grad, folded, text_term(slope, student)
+
+
+def add_to(sums_ref, sums_in, grad, folded):
+    width = grad.shape[1]
+    sums_ref[:, :width] = sums_in[:, :width] + grad
+    sums_ref[:, width:] = sums_in[:, width:] + folded
 
 
 def own_first(own_ref, text_ref, sums_ref, term_ref):
     rows, width = term_ref.shape
-    sums_ref[:, :width], sums_ref[:, width:], term_ref[...] = block(own_ref, text_ref, rows)
-
-
-def own_next(own_ref, text_ref, sums_in, sums_ref, term_ref):
+    images = both_images(own_ref, rows)
+    sums_ref[:, :width], sums_ref[:, width:], term_ref[...] = block(images, unpacked(text_ref, rows))
+
+
+def own_second(own_ref, text_ref, sums_in, sums_ref, term_ref):
+    rows = term_ref.shape[0]
+    grad, folded, term_ref[...] = block(both_images(own_ref, rows), unpacked(text_ref, rows))
+    add_to(sums_ref, sums_in, grad, folded)
+
+
+def other_second(other_ref, text_ref, term_in, sums_ref, term_ref):
     rows, width = term_ref.shape
-    grad, folded, term_ref[...] = block(own_ref, text_ref, rows)
-    sums_ref[:, :width] = sums_in[:, :width] + grad
-    sums_ref[:, width:] = sums_in[:, width:] + folded
-
-
-def other_all(
+    grad, folded, term = block(both_images(other_ref, rows), unpacked(text_ref, rows))
+    sums_ref[:, :width] = grad
+    sums_ref[:, width:] = folded
+    term_ref[...] = (term_in[...] + term).astype(term_ref.dtype)
+
+
+def near_and_text(
+    own_ref,
     other_ref,
     text_ref,
     near_ref,
-    second_ref,
     own_in,
-    near_in,
-    second_in,
-    sums_ref,
+    other_in,
+    term_in,
     own_out,
-    near_out,
-    second_out,
+    other_out,
+    near_term,
+    own_term,
 ):
-    rows, width = own_in.shape
-    texts = (
-        (second_ref, second_in, second_out),
-        (near_ref, near_in, near_out),
-        (text_ref, own_in, own_out),
-    )
-    for count, (ref, term_in, term_out) in enumerate(texts):
-        grad, folded, term = block(other_ref, ref, rows)
-        term_out[...] = (term_in[...] + term).astype(term_out.dtype)
-        if count:
-            grad = sums_ref[:, :width] + grad
-            folded = sums_ref[:, width:] + folded
-        sums_ref[:, :width] = grad
-        sums_ref[:, width:] = folded
+    rows = term_in.shape[0]
+    near = unpacked(near_ref, rows)
+    grad, folded, term = block(both_images(own_ref, rows), near)
+    add_to(own_out, own_in, grad, folded)
+    other = both_images(other_ref, rows)
+    grad, folded, more = block(other, near)
+    near_term[...] = term + more
+    add_to(other_out, other_in, grad, folded)
+    grad, folded, term = block(other, unpacked(text_ref, rows))
+    own_term[...] = term_in[...] + term
+    add_to(other_out, other_out, grad, folded)
 
 
 def loss_row(folded):
     return jnp.sum(jnp.transpose(folded), axis=0, keepdims=True)
 
 
-def ahead_last(ahead_ref, text_ref, term_in, ahead_out, term_ref):
-    rows, width = term_ref.shape
-    grad, folded, term = block(ahead_ref, text_ref, rows)
+def ahead_last(student_ref, teacher_ref, near_ref, term_in, ahead_out, term_ref):
+    rows = term_ref.shape[0]
+    images = (student_ref[...], *unpacked(teacher_ref, rows))
+    grad, folded, term = block(images, unpacked(near_ref, rows))
     term_ref[...] = (term_in[...] + term).astype(term_ref.dtype)
     put(ahead_out, 0, grad.astype(BF16))
     loss = loss_row(folded)
@@ -242,39 +266,44 @@
     term = spec(rows, width, F32)
     sent = spec(rows, width, BF16)
     packed = spec(rows * width // LANES + EXTRA, LANES, BF16)
+    ahead_student = back(student_image_vectors)
     (text,) = call(pack_text, [packed], 0, text_emb, species)
+    second = onward(text)
     near = across(text)
-    second = onward(text)
-    (images,) = call(
+    images, teacher = call(
         pack_images,
-        [spec(2 * rows * width // LANES + EXTRA, LANES, BF16)],
+        [spec(2 * rows * width // LANES + EXTRA, LANES, BF16), packed],
         0,
         student_image_vectors,
         teacher_emb,
         species,
         after=(text,),
     )
-    ahead = back(images)
     other = within(images)
-    own_sum, own_term = call(own_first, [sums, term], 4 * dot, images, text)
-    own_sum, near_term = call(own_next, [sums, term], 32 * dot, images, near, own_sum)
-    own_sum, second_term = call(own_next, [sums, term], 32 * dot, images, second, own_sum)
-    other_sum, own_term, near_term, second_term = call(
-        other_all,
-        [sums, term, term, sent],
-        12 * dot,
+    ahead_teacher = back(teacher)
+    own_sum, own_term = call(
+        own_first, [sums, term], 64 * dot, images, text, after=(ahead_student,)
+    )
+    own_sum, second_term = call(own_second, [sums, term], 16 * dot, images, second, own_sum)
+    other_sum, second_term = call(
+        other_second, [sums, sent], 16 * dot, other, second, second_term
+    )
+    second_back = back(second_term)
+    own_sum, other_sum, near_term, own_term = call(
+        near_and_text,
+        [sums, sums, term, term],
+        4 * dot,
+        images,
         other,
         text,
         near,
-        second,
+        own_sum,
+        other_sum,
         own_term,
-        near_term,
-        second_term,
-    )
-    second_back = back(second_term)
+    )
     other_back = within(other_sum)
     ahead_sum, near_term = call(
-        ahead_last, [packed, sent], 4 * dot, ahead, near, near_term
+        ahead_last, [packed, sent], 4 * dot, ahead_student, ahead_teacher, near, near_term
     )
     near_back = across(near_term)
     ahead_back = onward(ahead_sum)

time: 73.6 us -> 74.5 us (1.012)
  starting transfers between devices: 41.1 us -> 49.9 us
  waiting for transfers between devices: 15.8 us -> 7.7 us
    ppermute x8 -> x9, starting transfers between devices: 41.1 us -> 49.9 us  [moved(): lax.ppermute(value, 'dp', [(i, (i + (odd if i % 2 else even)) % length) f...]
    ppermute x8 -> x9, waiting for transfers between devices: 15.8 us -> 7.7 us  [moved(): lax.ppermute(value, 'dp', [(i, (i + (odd if i % 2 else even)) % length) f...]
  transfers between devices with their start and end apart: 8 -> 9, of which waited for: 3 -> 2; matrix products, arithmetic and copies ran while one was open for 0% -> 0% of each run, Pallas kernels for 17% -> 17%
where the time goes in v4:
time: 74.5 us; the launch traced here: 74.1 us
  starting transfers between devices  49.9 us (67%)
  Pallas kernels  14 us (19%)
  waiting for transfers between devices  7.7 us (10%)
  local copies, waits for them, and re-layouts  1.75 us (2%)
  between operations  0.82 us (1%)
    ppermute x9, starting transfers between devices, moved(): lax.ppermute(value, 'dp', [(i, (i + (odd if i % 2 else even)) % length) f...  49.9 us
    pallas_call x11, Pallas kernels, call(): pl.pallas_call(ordered, out_shape=out_shape, in_specs=[pl.BlockSpec(memor...  14 us
    ppermute x9, waiting for transfers between devices, moved(): lax.ppermute(value, 'dp', [(i, (i + (odd if i % 2 else even)) % length) f...  7.7 us
    unnamed x8, local copies, waits for them, and re-layouts  1.75 us
  transfers between devices with their start and end apart: 9, of which 2 were waited for; matrix products, arithmetic and copies ran while one was open for 0% of the time, Pallas kernels for 17%

profile of v4, /device:TPU:1, one launch (start us, length us, event | category | flops | bytes accessed | tf_op | source)
XLA Modules:
  0.0 74.1 jit_solution(4548746282088131181)
XLA Ops:
  0.6 4.0 %collective-permute-start.3 = (bf16[384,768]{1,0:T(8,128)(2,1)}, bf16[384,768]{1,0:T(8,128)(2,1)S(1)}, u32[]{:S(2)}, u32[]{:S(2)}) collective-permute-start(bf16[384,768]{1,0:T(8,128)(2,1)} %refs_0_.3), channel_id=1, source_target_pairs={{0,510},{1,3},{2,0},{3,5},{4,2},{5,7},{6,4},{7,9},{8,6},{9,11},{10... | collective-permute-start | bytes 1769480 | tf_op jit(solution)/shard_map/ppermute | solution.py:21
  4.7 1.1 %copy-done = bf16[384,768]{1,0:T(8,128)(2,1)S(1)} copy-done((bf16[384,768]{1,0:T(8,128)(2,1)S(1)}, bf16[384,768]{1,0:T(8,128)(2,1)}, u32[]{:S(2)}) %copy-start) | copy-done | bytes 589848
  5.7 0.7 copy-done.3
  6.4 0.1 shard_map.67.refs_3_.refs_1_.refs_2_
  6.5 14.6 %collective-permute-start.2 = (bf16[2320,128]{1,0:T(8,128)(2,1)S(1)}, bf16[2320,128]{1,0:T(8,128)(2,1)S(1)}, u32[]{:S(2)}, u32[]{:S(2)}) collective-permute-start(bf16[2320,128]{1,0:T(8,128)(2,1)S(1)} %shard_map.67.refs_3_.refs_1_.refs_2_), channel_id=1, source_target_pairs={{0,2},{1,511},{2,4},{3,1},{4,6},{5,3},{6,8},{7,5},{8,10},{9,7},{10... | collective-permute-start | bytes 1781768 | tf_op jit(solution)/shard_map/ppermute | solution.py:21
  21.1 1.9 %collective-permute-start.1 = (bf16[2320,128]{1,0:T(8,128)(2,1)S(1)}, bf16[2320,128]{1,0:T(8,128)(2,1)S(1)}, u32[]{:S(2)}, u32[]{:S(2)}) collective-permute-start(bf16[2320,128]{1,0:T(8,128)(2,1)S(1)} %shard_map.67.refs_3_.refs_1_.refs_2_), channel_id=1, source_target_pairs={{0,511},{1,2},{2,1},{3,4},{4,3},{5,6},{6,5},{7,8},{8,7},{9,10},{10... | collective-permute-start | bytes 1781768 | tf_op jit(solution)/shard_map/ppermute | solution.py:21
  23.1 0.2 shard_map.68
  23.3 1.9 %collective-permute-start.4 = (bf16[2320,128]{1,0:T(8,128)(2,1)S(1)}, bf16[2320,128]{1,0:T(8,128)(2,1)S(1)}, u32[]{:S(2)}, u32[]{:S(2)}) collective-permute-start(bf16[2320,128]{1,0:T(8,128)(2,1)S(1)} %get-tuple-element.29), channel_id=1, source_target_pairs={{0,510},{1,3},{2,0},{3,5},{4,2},{5,7},{6,4},{7,9},{8,6},{9,11},{10... | collective-permute-start | bytes 1781768 | tf_op jit(solution)/shard_map/ppermute | solution.py:21
  25.3 10.3 %collective-permute-start = (bf16[4624,128]{1,0:T(8,128)(2,1)S(1)}, bf16[4624,128]{1,0:T(8,128)(2,1)S(1)}, u32[]{:S(2)}, u32[]{:S(2)}) collective-permute-start(bf16[4624,128]{1,0:T(8,128)(2,1)S(1)} %get-tuple-element.22.refs_0_), channel_id=1, source_target_pairs={{0,1},{1,0},{2,3},{3,2},{4,5},{5,4},{6,7},{7,6},{8,9},{9,8},{10,11... | collective-permute-start | bytes 3551240 | tf_op jit(solution)/shard_map/ppermute | solution.py:21
  35.6 1.6 %shard_map.69 = (f32[384,896]{1,0:T(8,128)S(1)}, f32[384,768]{1,0:T(8,128)S(1)}) custom-call(bf16[4624,128]{1,0:T(8,128)(2,1)S(1)} %get-tuple-element.22.refs_0_, bf16[2320,128]{1,0:T(8,128)(2,1)S(1)} %shard_map.67.refs_3_.refs_1_.refs_2_, bf16[384,768]{1,0:T(8,128)(2,1)S(1)} %collective-permute-done.3.refs_2_.refs_0_), custom_call_target="tpu_custom_call" | custom-call | flops 14495514624 | bytes 4333568 | tf_op jit(solution)/shard_map/pallas_call | solution.py:50
  37.1 1.6 %shard_map.70 = (f32[384,896]{1,0:T(8,128)S(1)}, f32[384,768]{1,0:T(8,128)S(1)}) custom-call(bf16[4624,128]{1,0:T(8,128)(2,1)S(1)} %get-tuple-element.22.refs_0_, bf16[2320,128]{1,0:T(8,128)(2,1)S(1)} %collective-permute-done.2.refs_1_, f32[384,896]{1,0:T(8,128)S(1)} %get-tuple-element.23.refs_2_), custom_call_target="tpu_custom_call" | custom-call | flops 3623878656 | bytes 5709824 | tf_op jit(solution)/shard_map/pallas_call | solution.py:50
  38.7 1.6 %shard_map.71 = (f32[384,896]{1,0:T(8,128)S(1)}, bf16[384,768]{1,0:T(8,128)(2,1)S(1)}) custom-call(bf16[4624,128]{1,0:T(8,128)(2,1)S(1)} %collective-permute-done.refs_0_.refs_1_, bf16[2320,128]{1,0:T(8,128)(2,1)S(1)} %collective-permute-done.2.refs_1_, f32[384,768]{1,0:T(8,128)S(1)} %get-tuple-element.25.refs_2_), custom_call_target="tpu_custom_call" | custom-call | flops 3623878656 | bytes 4923392 | tf_op jit(solution)/shard_map/pallas_call | solution.py:50
  40.3 1.9 %collective-permute-start.6 = (bf16[384,768]{1,0:T(8,128)(2,1)S(1)}, bf16[384,768]{1,0:T(8,128)(2,1)S(1)}, u32[]{:S(2)}, u32[]{:S(2)}) collective-permute-start(bf16[384,768]{1,0:T(8,128)(2,1)S(1)} %get-tuple-element.33), channel_id=1, source_target_pairs={{0,510},{1,3},{2,0},{3,5},{4,2},{5,7},{6,4},{7,9},{8,6},{9,11},{10... | collective-permute-start | bytes 1769480 | tf_op jit(solution)/shard_map/ppermute | solution.py:21
  42.3 4.6 %shard_map.72 = (f32[384,896]{1,0:T(8,128)S(1)}, f32[384,896]{1,0:T(8,128)S(1)}, f32[384,768]{1,0:T(8,128)S(1)}, f32[384,768]{1,0:T(8,128)S(1)}) custom-call(bf16[4624,128]{1,0:T(8,128)(2,1)S(1)} %get-tuple-element.22.refs_0_, bf16[4624,128]{1,0:T(8,128)(2,1)S(1)} %collective-permute-done.refs_0_.refs_1_, ...), custom_call_target="tpu_custom_call" | custom-call | flops 905969664 | bytes 12599296 | tf_op jit(solution)/shard_map/pallas_call | solution.py:50
  46.9 2.6 %collective-permute-done.4.refs_1_ = bf16[2320,128]{1,0:T(8,128)(2,1)S(1)} collective-permute-done((bf16[2320,128]{1,0:T(8,128)(2,1)S(1)}, bf16[2320,128]{1,0:T(8,128)(2,1)S(1)}, u32[]{:S(2)}, u32[]{:S(2)}) %collective-permute-start.4) | collective-permute-done | bytes 593952 | tf_op jit(solution)/shard_map/ppermute | solution.py:21
  49.4 1.6 %shard_map.73 = (bf16[2320,128]{1,0:T(8,128)(2,1)S(1)}, bf16[384,768]{1,0:T(8,128)(2,1)S(1)}) custom-call(bf16[384,768]{1,0:T(8,128)(2,1)S(1)} %collective-permute-done.3.refs_2_.refs_0_, bf16[2320,128]{1,0:T(8,128)(2,1)S(1)} %collective-permute-done.4.refs_1_, bf16[2320,128]{1,0:T(8,128)(2,1)S(1)} %collective-permute-done.1.refs_3_.refs_2_, ...), custom_call_target="tpu_custom_call" | custom-call | flops 905969664 | bytes 4141056 | tf_op jit(solution)/shard_map/pallas_call | solution.py:50
  51.0 6.2 %collective-permute-start.8 = (bf16[384,768]{1,0:T(8,128)(2,1)S(1)}, bf16[384,768]{1,0:T(8,128)(2,1)S(1)}, u32[]{:S(2)}, u32[]{:S(2)}) collective-permute-start(bf16[384,768]{1,0:T(8,128)(2,1)S(1)} %get-tuple-element.38), channel_id=1, source_target_pairs={{0,511},{1,2},{2,1},{3,4},{4,3},{5,6},{6,5},{7,8},{8,7},{9,10},{10... | collective-permute-start | bytes 1769480 | tf_op jit(solution)/shard_map/ppermute | solution.py:21
  57.2 7.1 %collective-permute-start.5 = (bf16[2320,128]{1,0:T(8,128)(2,1)S(1)}, bf16[2320,128]{1,0:T(8,128)(2,1)S(1)}, u32[]{:S(2)}, u32[]{:S(2)}) collective-permute-start(bf16[2320,128]{1,0:T(8,128)(2,1)S(1)} %get-tuple-element.31), channel_id=1, source_target_pairs={{0,2},{1,511},{2,4},{3,1},{4,6},{5,3},{6,8},{7,5},{8,10},{9,7},{10... | collective-permute-start | bytes 1781768 | tf_op jit(solution)/shard_map/ppermute | solution.py:21
  64.3 1.9 %collective-permute-start.7 = (f32[384,896]{1,0:T(8,128)S(1)}, f32[384,896]{1,0:T(8,128)S(1)}, u32[]{:S(2)}, u32[]{:S(2)}) collective-permute-start(f32[384,896]{1,0:T(8,128)S(1)} %get-tuple-element.36), channel_id=1, source_target_pairs={{0,1},{1,0},{2,3},{3,2},{4,5},{5,4},{6,7},{7,6},{8,9},{9,8},{10,11... | collective-permute-start | bytes 4128776 | tf_op jit(solution)/shard_map/ppermute | solution.py:21
  66.2 0.1 shard_map.74.refs_2_.refs_0_
  66.3 5.1 %collective-permute-done.5.refs_1_ = bf16[2320,128]{1,0:T(8,128)(2,1)S(1)} collective-permute-done((bf16[2320,128]{1,0:T(8,128)(2,1)S(1)}, bf16[2320,128]{1,0:T(8,128)(2,1)S(1)}, u32[]{:S(2)}, u32[]{:S(2)}) %collective-permute-start.5) | collective-permute-done | bytes 593952 | tf_op jit(solution)/shard_map/ppermute | solution.py:21
  71.4 0.2 shard_map.75
  71.6 1.4 %shard_map.76 = (f32[384,768]{1,0:T(8,128)}, f32[384]{0:T(512)}, f32[8,128]{1,0:T(8,128)S(1)}) custom-call(f32[384,768]{1,0:T(8,128)S(1)} %get-tuple-element.34.refs_0_, f32[1,384]{1,0:T(1,128)S(1)} %get-tuple-element.35.refs_1_, f32[384,896]{1,0:T(8,128)S(1)} %collective-permute-done.7.refs_2_), custom_call_target="tpu_custom_call" | custom-call | bytes 3742720 | tf_op jit(solution)/shard_map/pallas_call | solution.py:50
  73.0 1.1 %shard_map.77 = f32[384,768]{1,0:T(8,128)} custom-call(f32[384,768]{1,0:T(8,128)S(1)} %shard_map.74.refs_2_.refs_0_, bf16[384,768]{1,0:T(8,128)(2,1)S(1)} %collective-permute-done.8.refs_1_, f32[8,128]{1,0:T(8,128)S(1)} %get-tuple-element.39.refs_2_), custom_call_target="tpu_custom_call" | custom-call | bytes 2949120 | tf_op jit(solution)/shard_map/pallas_call | solution.py:50
  (13 shorter events, 0.0 us)
Async XLA Ops:
  0.6 34.9 %collective-permute-start.3 = (bf16[384,768]{1,0:T(8,128)(2,1)}, bf16[384,768]{1,0:T(8,128)(2,1)S(1)}, u32[]{:S(2)}, u32[]{:S(2)}) collective-permute-start(bf16[384,768]{1,0:T(8,128)(2,1)} %refs_0_.3), channel_id=1, source_target_pairs={{0,510},{1,3},{2,0},{3,5},{4,2},{5,7},{6,4},{7,9},{8,6},{9,11},{10... | collective-permute-start | bytes 1769480 | tf_op jit(solution)/shard_map/ppermute | solution.py:21
  4.7 1.1 %copy-start = (bf16[384,768]{1,0:T(8,128)(2,1)S(1)}, bf16[384,768]{1,0:T(8,128)(2,1)}, u32[]{:S(2)}) copy-start(bf16[384,768]{1,0:T(8,128)(2,1)} %refs_0_.2) | copy-start | bytes 1769476
  5.7 0.7 copy-start.3
  6.4 16.6 %copy-start.1 = (bf16[384,768]{1,0:T(8,128)(2,1)S(1)}, bf16[384,768]{1,0:T(8,128)(2,1)}, u32[]{:S(2)}) copy-start(bf16[384,768]{1,0:T(8,128)(2,1)} %refs_1_.3) | copy-start | bytes 1769476
  6.4 16.7 %copy-start.2 = (bf16[384,768]{1,0:T(8,128)(2,1)S(1)}, bf16[384,768]{1,0:T(8,128)(2,1)}, u32[]{:S(2)}) copy-start(bf16[384,768]{1,0:T(8,128)(2,1)} %refs_0_.3) | copy-start | bytes 1769476
  6.5 30.6 %collective-permute-start.2 = (bf16[2320,128]{1,0:T(8,128)(2,1)S(1)}, bf16[2320,128]{1,0:T(8,128)(2,1)S(1)}, u32[]{:S(2)}, u32[]{:S(2)}) collective-permute-start(bf16[2320,128]{1,0:T(8,128)(2,1)S(1)} %shard_map.67.refs_3_.refs_1_.refs_2_), channel_id=1, source_target_pairs={{0,2},{1,511},{2,4},{3,1},{4,6},{5,3},{6,8},{7,5},{8,10},{9,7},{10... | collective-permute-start | bytes 1781768 | tf_op jit(solution)/shard_map/ppermute | solution.py:21
  21.1 21.1 %collective-permute-start.1 = (bf16[2320,128]{1,0:T(8,128)(2,1)S(1)}, bf16[2320,128]{1,0:T(8,128)(2,1)S(1)}, u32[]{:S(2)}, u32[]{:S(2)}) collective-permute-start(bf16[2320,128]{1,0:T(8,128)(2,1)S(1)} %shard_map.67.refs_3_.refs_1_.refs_2_), channel_id=1, source_target_pairs={{0,511},{1,2},{2,1},{3,4},{4,3},{5,6},{6,5},{7,8},{8,7},{9,10},{10... | collective-permute-start | bytes 1781768 | tf_op jit(solution)/shard_map/ppermute | solution.py:21
  23.3 26.1 %collective-permute-start.4 = (bf16[2320,128]{1,0:T(8,128)(2,1)S(1)}, bf16[2320,128]{1,0:T(8,128)(2,1)S(1)}, u32[]{:S(2)}, u32[]{:S(2)}) collective-permute-start(bf16[2320,128]{1,0:T(8,128)(2,1)S(1)} %get-tuple-element.29), channel_id=1, source_target_pairs={{0,510},{1,3},{2,0},{3,5},{4,2},{5,7},{6,4},{7,9},{8,6},{9,11},{10... | collective-permute-start | bytes 1781768 | tf_op jit(solution)/shard_map/ppermute | solution.py:21
  25.3 13.5 %collective-permute-start = (bf16[4624,128]{1,0:T(8,128)(2,1)S(1)}, bf16[4624,128]{1,0:T(8,128)(2,1)S(1)}, u32[]{:S(2)}, u32[]{:S(2)}) collective-permute-start(bf16[4624,128]{1,0:T(8,128)(2,1)S(1)} %get-tuple-element.22.refs_0_), channel_id=1, source_target_pairs={{0,1},{1,0},{2,3},{3,2},{4,5},{5,4},{6,7},{7,6},{8,9},{9,8},{10,11... | collective-permute-start | bytes 3551240 | tf_op jit(solution)/shard_map/ppermute | solution.py:21
  40.3 25.9 %collective-permute-start.6 = (bf16[384,768]{1,0:T(8,128)(2,1)S(1)}, bf16[384,768]{1,0:T(8,128)(2,1)S(1)}, u32[]{:S(2)}, u32[]{:S(2)}) collective-permute-start(bf16[384,768]{1,0:T(8,128)(2,1)S(1)} %get-tuple-element.33), channel_id=1, source_target_pairs={{0,510},{1,3},{2,0},{3,5},{4,2},{5,7},{6,4},{7,9},{8,6},{9,11},{10... | collective-permute-start | bytes 1769480 | tf_op jit(solution)/shard_map/ppermute | solution.py:21
  51.0 22.0 %collective-permute-start.8 = (bf16[384,768]{1,0:T(8,128)(2,1)S(1)}, bf16[384,768]{1,0:T(8,128)(2,1)S(1)}, u32[]{:S(2)}, u32[]{:S(2)}) collective-permute-start(bf16[384,768]{1,0:T(8,128)(2,1)S(1)} %get-tuple-element.38), channel_id=1, source_target_pairs={{0,511},{1,2},{2,1},{3,4},{4,3},{5,6},{6,5},{7,8},{8,7},{9,10},{10... | collective-permute-start | bytes 1769480 | tf_op jit(solution)/shard_map/ppermute | solution.py:21
  57.2 14.2 %collective-permute-start.5 = (bf16[2320,128]{1,0:T(8,128)(2,1)S(1)}, bf16[2320,128]{1,0:T(8,128)(2,1)S(1)}, u32[]{:S(2)}, u32[]{:S(2)}) collective-permute-start(bf16[2320,128]{1,0:T(8,128)(2,1)S(1)} %get-tuple-element.31), channel_id=1, source_target_pairs={{0,2},{1,511},{2,4},{3,1},{4,6},{5,3},{6,8},{7,5},{8,10},{9,7},{10... | collective-permute-start | bytes 1781768 | tf_op jit(solution)/shard_map/ppermute | solution.py:21
  64.3 7.4 %collective-permute-start.7 = (f32[384,896]{1,0:T(8,128)S(1)}, f32[384,896]{1,0:T(8,128)S(1)}, u32[]{:S(2)}, u32[]{:S(2)}) collective-permute-start(f32[384,896]{1,0:T(8,128)S(1)} %get-tuple-element.36), channel_id=1, source_target_pairs={{0,1},{1,0},{2,3},{3,2},{4,5},{5,4},{6,7},{7,6},{8,9},{9,8},{10,11... | collective-permute-start | bytes 4128776 | tf_op jit(solution)/shard_map/ppermute | solution.py:21

commit v5 on v4

--- a/solution.py
+++ b/solution.py
@@ -175,55 +175,43 @@
     sums_ref[:, :width], sums_ref[:, width:], term_ref[...] = block(images, unpacked(text_ref, rows))
 
 
-def own_second(own_ref, text_ref, sums_in, sums_ref, term_ref):
+def other_first(other_ref, text_ref, term_in, sums_ref, term_ref):
+    rows, width = term_ref.shape
+    images = both_images(other_ref, rows)
+    sums_ref[:, :width], sums_ref[:, width:], term = block(images, unpacked(text_ref, rows))
+    term_ref[...] = term_in[...] + term
+
+
+def both_second(own_ref, other_ref, text_ref, own_in, other_in, own_out, other_out, term_ref):
     rows = term_ref.shape[0]
-    grad, folded, term_ref[...] = block(both_images(own_ref, rows), unpacked(text_ref, rows))
-    add_to(sums_ref, sums_in, grad, folded)
-
-
-def other_second(other_ref, text_ref, term_in, sums_ref, term_ref):
-    rows, width = term_ref.shape
-    grad, folded, term = block(both_images(other_ref, rows), unpacked(text_ref, rows))
-    sums_ref[:, :width] = grad
-    sums_ref[:, width:] = folded
-    term_ref[...] = (term_in[...] + term).astype(term_ref.dtype)
-
-
-def near_and_text(
-    own_ref,
-    other_ref,
-    text_ref,
-    near_ref,
-    own_in,
-    other_in,
-    term_in,
-    own_out,
-    other_out,
-    near_term,
-    own_term,
+    text = unpacked(text_ref, rows)
+    grad, folded, term = block(both_images(own_ref, rows), text)
+    add_to(own_out, own_in, grad, folded)
+    grad, folded, more = block(both_images(other_ref, rows), text)
+    add_to(other_out, other_in, grad, folded)
+    term_ref[...] = (term + more).astype(term_ref.dtype)
+
+
+def both_near(
+    own_ref, other_ref, text_ref, own_in, other_in, term_in, own_out, other_out, term_ref
 ):
-    rows = term_in.shape[0]
-    near = unpacked(near_ref, rows)
-    grad, folded, term = block(both_images(own_ref, rows), near)
+    rows = term_ref.shape[0]
+    text = unpacked(text_ref, rows)
+    grad, folded, term = block(both_images(own_ref, rows), text)
     add_to(own_out, own_in, grad, folded)
-    other = both_images(other_ref, rows)
-    grad, folded, more = block(other, near)
-    near_term[...] = term + more
+    grad, folded, more = block(both_images(other_ref, rows), text)
     add_to(other_out, other_in, grad, folded)
-    grad, folded, term = block(other, unpacked(text_ref, rows))
-    own_term[...] = term_in[...] + term
-    add_to(other_out, other_out, grad, folded)
+    term_ref[...] = (term_in[...] + term + more).astype(term_ref.dtype)
 
 
 def loss_row(folded):
     return jnp.sum(jnp.transpose(folded), axis=0, keepdims=True)
 
 
-def ahead_last(student_ref, teacher_ref, near_ref, term_in, ahead_out, term_ref):
+def ahead_near(student_ref, teacher_ref, near_ref, ahead_out, term_ref):
     rows = term_ref.shape[0]
     images = (student_ref[...], *unpacked(teacher_ref, rows))
-    grad, folded, term = block(images, unpacked(near_ref, rows))
-    term_ref[...] = (term_in[...] + term).astype(term_ref.dtype)
+    grad, folded, term_ref[...] = block(images, unpacked(near_ref, rows))
     put(ahead_out, 0, grad.astype(BF16))
     loss = loss_row(folded)
     high = loss.astype(BF16).astype(F32)
@@ -241,18 +229,13 @@
     loss_ref[...] = loss_row(own_ref[:, width:]) + high + low
 
 
-def finish_images(sums_in, loss_in, other_ref, grad_ref, loss_ref, done_ref):
+def finish(sums_in, loss_in, term_in, other_ref, grad_ref, text_ref, loss_ref):
     rows, width = grad_ref.shape
     scale = SOFTMAX_TEMP_VALUE / float(width) ** 0.5
+    text_ref[...] = term_in[...] * scale
     grad_ref[...] = (sums_in[...] + other_ref[:, :width]) * scale
     loss = loss_in[...] + loss_row(other_ref[:, width:])
     loss_ref[...] = (loss / float(WINDOW * rows)).reshape(rows)
-    done_ref[...] = jnp.zeros_like(done_ref)
-
-
-def finish_text(own_ref, near_ref, out_ref):
-    scale = SOFTMAX_TEMP_VALUE / float(out_ref.shape[1]) ** 0.5
-    out_ref[...] = (own_ref[...] + near_ref[...].astype(F32)) * scale
 
 
 def shards(student_image_vectors, teacher_emb, text_emb, species):
@@ -284,42 +267,50 @@
     own_sum, own_term = call(
         own_first, [sums, term], 64 * dot, images, text, after=(ahead_student,)
     )
-    own_sum, second_term = call(own_second, [sums, term], 16 * dot, images, second, own_sum)
-    other_sum, second_term = call(
-        other_second, [sums, sent], 16 * dot, other, second, second_term
+    other_sum, own_term = call(other_first, [sums, term], 16 * dot, other, text, own_term)
+    own_sum, other_sum, second_term = call(
+        both_second, [sums, sums, sent], 16 * dot, images, other, second, own_sum, other_sum
     )
     second_back = back(second_term)
-    own_sum, other_sum, near_term, own_term = call(
-        near_and_text,
-        [sums, sums, term, term],
+    ahead_sum, far_term = call(
+        ahead_near,
+        [packed, term],
         4 * dot,
+        ahead_student,
+        ahead_teacher,
+        near,
+        after=(second_term,),
+    )
+    ahead_back = onward(ahead_sum)
+    own_sum, other_sum, near_term = call(
+        both_near,
+        [sums, sums, sent],
+        0 * dot,
         images,
         other,
-        text,
         near,
         own_sum,
         other_sum,
-        own_term,
-    )
+        far_term,
+    )
+    near_back = across(near_term)
     other_back = within(other_sum)
-    ahead_sum, near_term = call(
-        ahead_last, [packed, sent], 4 * dot, ahead_student, ahead_teacher, near, near_term
-    )
-    near_back = across(near_term)
-    ahead_back = onward(ahead_sum)
-    (own_term,) = call(gather_text, [term], 64 * dot, own_term, second_back)
+    (own_term,) = call(gather_text, [term], 128 * dot, own_term, second_back)
     own_sum, loss = call(
-        gather_images, [term, spec(1, rows, F32)], 32 * dot, own_sum, ahead_back, after=(own_term,)
-    )
-    grad_student, loss, done = call(
-        finish_images,
-        [term, jax.ShapeDtypeStruct((rows,), F32), spec(8, LANES, F32)],
+        gather_images, [term, spec(1, rows, F32)], 64 * dot, own_sum, ahead_back, after=(own_term,)
+    )
+    (own_term,) = call(
+        gather_text, [term], 32 * dot, own_term, near_back, after=(own_sum,)
+    )
+    grad_student, grad_text, loss = call(
+        finish,
+        [term, term, jax.ShapeDtypeStruct((rows,), F32)],
         0,
         own_sum,
         loss,
+        own_term,
         other_back,
     )
-    (grad_text,) = call(finish_text, [term], 0, own_term, near_back, after=(done,))
     return grad_student, grad_text, loss
 
 

time: 74.5 us -> 71.7 us (0.962)
  starting transfers between devices: 49.9 us -> 33.9 us
  waiting for transfers between devices: 7.7 us -> 21.6 us
    ppermute x9, starting transfers between devices: 49.9 us -> 33.9 us  [moved(): lax.ppermute(value, 'dp', [(i, (i + (odd if i % 2 else even)) % length) f...]
    ppermute x9, waiting for transfers between devices: 7.7 us -> 21.6 us  [moved(): lax.ppermute(value, 'dp', [(i, (i + (odd if i % 2 else even)) % length) f...]
  transfers between devices with their start and end apart: 9 -> 9, of which waited for: 2 -> 4; matrix products, arithmetic and copies ran while one was open for 0% -> 0% of each run, Pallas kernels for 17% -> 16%
where the time goes in v5:
time: 71.7 us; the launch traced here: 71.3 us
  starting transfers between devices  33.9 us (47%)
  waiting for transfers between devices  21.6 us (30%)
  Pallas kernels  13.3 us (19%)
  local copies, waits for them, and re-layouts  1.75 us (2%)
  between operations  0.81 us (1%)
    ppermute x9, starting transfers between devices, moved(): lax.ppermute(value, 'dp', [(i, (i + (odd if i % 2 else even)) % length) f...  33.9 us
    ppermute x9, waiting for transfers between devices, moved(): lax.ppermute(value, 'dp', [(i, (i + (odd if i % 2 else even)) % length) f...  21.6 us
    pallas_call x11, Pallas kernels, call(): pl.pallas_call(ordered, out_shape=out_shape, in_specs=[pl.BlockSpec(memor...  13.3 us
    unnamed x8, local copies, waits for them, and re-layouts  1.75 us
  transfers between devices with their start and end apart: 9, of which 4 were waited for; matrix products, arithmetic and copies ran while one was open for 0% of the time, Pallas kernels for 16%

profile of v5, /device:TPU:1, one launch (start us, length us, event | category | flops | bytes accessed | tf_op | source)
XLA Modules:
  0.0 71.3 jit_solution(10016083694668261551)
XLA Ops:
  0.6 4.0 %collective-permute-start.3 = (bf16[384,768]{1,0:T(8,128)(2,1)}, bf16[384,768]{1,0:T(8,128)(2,1)S(1)}, u32[]{:S(2)}, u32[]{:S(2)}) collective-permute-start(bf16[384,768]{1,0:T(8,128)(2,1)} %refs_0_.3), channel_id=1, source_target_pairs={{0,510},{1,3},{2,0},{3,5},{4,2},{5,7},{6,4},{7,9},{8,6},{9,11},{10... | collective-permute-start | bytes 1769480 | tf_op jit(solution)/shard_map/ppermute | solution.py:21
  4.7 1.1 %copy-done = bf16[384,768]{1,0:T(8,128)(2,1)S(1)} copy-done((bf16[384,768]{1,0:T(8,128)(2,1)S(1)}, bf16[384,768]{1,0:T(8,128)(2,1)}, u32[]{:S(2)}) %copy-start) | copy-done | bytes 589848
  5.7 0.7 copy-done.3
  6.5 14.6 %collective-permute-start.2 = (bf16[2320,128]{1,0:T(8,128)(2,1)S(1)}, bf16[2320,128]{1,0:T(8,128)(2,1)S(1)}, u32[]{:S(2)}, u32[]{:S(2)}) collective-permute-start(bf16[2320,128]{1,0:T(8,128)(2,1)S(1)} %shard_map.67.refs_3_.refs_1_), channel_id=1, source_target_pairs={{0,2},{1,511},{2,4},{3,1},{4,6},{5,3},{6,8},{7,5},{8,10},{9,7},{10... | collective-permute-start | bytes 1781768 | tf_op jit(solution)/shard_map/ppermute | solution.py:21
  21.1 1.9 %collective-permute-start.1 = (bf16[2320,128]{1,0:T(8,128)(2,1)S(1)}, bf16[2320,128]{1,0:T(8,128)(2,1)S(1)}, u32[]{:S(2)}, u32[]{:S(2)}) collective-permute-start(bf16[2320,128]{1,0:T(8,128)(2,1)S(1)} %shard_map.67.refs_3_.refs_1_), channel_id=1, source_target_pairs={{0,511},{1,2},{2,1},{3,4},{4,3},{5,6},{6,5},{7,8},{8,7},{9,10},{10... | collective-permute-start | bytes 1781768 | tf_op jit(solution)/shard_map/ppermute | solution.py:21
  23.1 0.2 shard_map.68
  23.3 3.7 %collective-permute-start = (bf16[4624,128]{1,0:T(8,128)(2,1)S(1)}, bf16[4624,128]{1,0:T(8,128)(2,1)S(1)}, u32[]{:S(2)}, u32[]{:S(2)}) collective-permute-start(bf16[4624,128]{1,0:T(8,128)(2,1)S(1)} %get-tuple-element.19.refs_0_), channel_id=1, source_target_pairs={{0,1},{1,0},{2,3},{3,2},{4,5},{5,4},{6,7},{7,6},{8,9},{9,8},{10,11... | collective-permute-start | bytes 3551240 | tf_op jit(solution)/shard_map/ppermute | solution.py:21
  27.1 1.9 %collective-permute-start.4 = (bf16[2320,128]{1,0:T(8,128)(2,1)S(1)}, bf16[2320,128]{1,0:T(8,128)(2,1)S(1)}, u32[]{:S(2)}, u32[]{:S(2)}) collective-permute-start(bf16[2320,128]{1,0:T(8,128)(2,1)S(1)} %get-tuple-element.25), channel_id=1, source_target_pairs={{0,510},{1,3},{2,0},{3,5},{4,2},{5,7},{6,4},{7,9},{8,6},{9,11},{10... | collective-permute-start | bytes 1781768 | tf_op jit(solution)/shard_map/ppermute | solution.py:21
  29.0 1.6 %shard_map.69 = (f32[384,896]{1,0:T(8,128)S(1)}, f32[384,768]{1,0:T(8,128)S(1)}) custom-call(bf16[4624,128]{1,0:T(8,128)(2,1)S(1)} %get-tuple-element.19.refs_0_, bf16[2320,128]{1,0:T(8,128)(2,1)S(1)} %shard_map.67.refs_3_.refs_1_, bf16[384,768]{1,0:T(8,128)(2,1)S(1)} %collective-permute-done.3.refs_2_.refs_0_), custom_call_target="tpu_custom_call" | custom-call | flops 14495514624 | bytes 4333568 | tf_op jit(solution)/shard_map/pallas_call | solution.py:50
  30.6 1.6 %shard_map.70 = (f32[384,896]{1,0:T(8,128)S(1)}, f32[384,768]{1,0:T(8,128)S(1)}) custom-call(bf16[4624,128]{1,0:T(8,128)(2,1)S(1)} %collective-permute-done.refs_0_.refs_1_, bf16[2320,128]{1,0:T(8,128)(2,1)S(1)} %shard_map.67.refs_3_.refs_1_, f32[384,768]{1,0:T(8,128)S(1)} %get-tuple-element.21.refs_2_), custom_call_target="tpu_custom_call" | custom-call | flops 3623878656 | bytes 5513216 | tf_op jit(solution)/shard_map/pallas_call | solution.py:50
  32.2 2.3 %collective-permute-done.2.refs_2_ = bf16[2320,128]{1,0:T(8,128)(2,1)S(1)} collective-permute-done((bf16[2320,128]{1,0:T(8,128)(2,1)S(1)}, bf16[2320,128]{1,0:T(8,128)(2,1)S(1)}, u32[]{:S(2)}, u32[]{:S(2)}) %collective-permute-start.2) | collective-permute-done | bytes 593952 | tf_op jit(solution)/shard_map/ppermute | solution.py:21
  34.4 3.2 %shard_map.71 = (f32[384,896]{1,0:T(8,128)S(1)}, f32[384,896]{1,0:T(8,128)S(1)}, bf16[384,768]{1,0:T(8,128)(2,1)S(1)}) custom-call(bf16[4624,128]{1,0:T(8,128)(2,1)S(1)} %get-tuple-element.19.refs_0_, bf16[4624,128]{1,0:T(8,128)(2,1)S(1)} %collective-permute-done.refs_0_.refs_1_, bf16[2320,128]{1,0:T(8,128)(2,1)S(1)} %collective-permute-done.2.refs_2_, ...), custom_call_target="tpu_custom_call" | custom-call | flops 3623878656 | bytes 9056256 | tf_op jit(solution)/shard_map/pallas_call | solution.py:50
  37.6 1.9 %collective-permute-start.6 = (bf16[384,768]{1,0:T(8,128)(2,1)S(1)}, bf16[384,768]{1,0:T(8,128)(2,1)S(1)}, u32[]{:S(2)}, u32[]{:S(2)}) collective-permute-start(bf16[384,768]{1,0:T(8,128)(2,1)S(1)} %get-tuple-element.26.refs_3_), channel_id=1, source_target_pairs={{0,510},{1,3},{2,0},{3,5},{4,2},{5,7},{6,4},{7,9},{8,6},{9,11},{10... | collective-permute-start | bytes 1769480 | tf_op jit(solution)/shard_map/ppermute | solution.py:21
  39.5 9.9 %collective-permute-done.4.refs_1_ = bf16[2320,128]{1,0:T(8,128)(2,1)S(1)} collective-permute-done((bf16[2320,128]{1,0:T(8,128)(2,1)S(1)}, bf16[2320,128]{1,0:T(8,128)(2,1)S(1)}, u32[]{:S(2)}, u32[]{:S(2)}) %collective-permute-start.4) | collective-permute-done | bytes 593952 | tf_op jit(solution)/shard_map/ppermute | solution.py:21
  49.5 1.6 %shard_map.72 = (bf16[2320,128]{1,0:T(8,128)(2,1)S(1)}, f32[384,768]{1,0:T(8,128)S(1)}) custom-call(bf16[384,768]{1,0:T(8,128)(2,1)S(1)} %collective-permute-done.3.refs_2_.refs_0_, bf16[2320,128]{1,0:T(8,128)(2,1)S(1)} %collective-permute-done.4.refs_1_, bf16[2320,128]{1,0:T(8,128)(2,1)S(1)} %collective-permute-done.1.refs_2_, ...), custom_call_target="tpu_custom_call" | custom-call | flops 905969664 | bytes 3551232 | tf_op jit(solution)/shard_map/pallas_call | solution.py:50
  51.0 1.9 %collective-permute-start.5 = (bf16[2320,128]{1,0:T(8,128)(2,1)S(1)}, bf16[2320,128]{1,0:T(8,128)(2,1)S(1)}, u32[]{:S(2)}, u32[]{:S(2)}) collective-permute-start(bf16[2320,128]{1,0:T(8,128)(2,1)S(1)} %get-tuple-element.29), channel_id=1, source_target_pairs={{0,2},{1,511},{2,4},{3,1},{4,6},{5,3},{6,8},{7,5},{8,10},{9,7},{10... | collective-permute-start | bytes 1781768 | tf_op jit(solution)/shard_map/ppermute | solution.py:21
  53.0 3.0 %shard_map.73 = (f32[384,896]{1,0:T(8,128)S(1)}, f32[384,896]{1,0:T(8,128)S(1)}, bf16[384,768]{1,0:T(8,128)(2,1)S(1)}) custom-call(bf16[4624,128]{1,0:T(8,128)(2,1)S(1)} %get-tuple-element.19.refs_0_, bf16[4624,128]{1,0:T(8,128)(2,1)S(1)} %collective-permute-done.refs_0_.refs_1_, bf16[2320,128]{1,0:T(8,128)(2,1)S(1)} %collective-permute-done.1.refs_2_, ...), custom_call_target="tpu_custom_call" | custom-call | bytes 10235904 | tf_op jit(solution)/shard_map/pallas_call | solution.py:50
  56.0 1.9 %collective-permute-start.7 = (bf16[384,768]{1,0:T(8,128)(2,1)S(1)}, bf16[384,768]{1,0:T(8,128)(2,1)S(1)}, u32[]{:S(2)}, u32[]{:S(2)}) collective-permute-start(bf16[384,768]{1,0:T(8,128)(2,1)S(1)} %get-tuple-element.33), channel_id=1, source_target_pairs={{0,511},{1,2},{2,1},{3,4},{4,3},{5,6},{6,5},{7,8},{8,7},{9,10},{10... | collective-permute-start | bytes 1769480 | tf_op jit(solution)/shard_map/ppermute | solution.py:21
  57.9 1.9 %collective-permute-start.8 = (f32[384,896]{1,0:T(8,128)S(1)}, f32[384,896]{1,0:T(8,128)S(1)}, u32[]{:S(2)}, u32[]{:S(2)}) collective-permute-start(f32[384,896]{1,0:T(8,128)S(1)} %get-tuple-element.34), channel_id=1, source_target_pairs={{0,1},{1,0},{2,3},{3,2},{4,5},{5,4},{6,7},{7,6},{8,9},{9,8},{10,11... | collective-permute-start | bytes 4128776 | tf_op jit(solution)/shard_map/ppermute | solution.py:21
  59.9 0.1 shard_map.74.refs_2_.refs_0_
  60.0 5.3 %collective-permute-done.5.refs_1_ = bf16[2320,128]{1,0:T(8,128)(2,1)S(1)} collective-permute-done((bf16[2320,128]{1,0:T(8,128)(2,1)S(1)}, bf16[2320,128]{1,0:T(8,128)(2,1)S(1)}, u32[]{:S(2)}, u32[]{:S(2)}) %collective-permute-start.5) | collective-permute-done | bytes 593952 | tf_op jit(solution)/shard_map/ppermute | solution.py:21
  65.3 0.2 shard_map.75
  65.5 4.1 %collective-permute-done.7.refs_1_ = bf16[384,768]{1,0:T(8,128)(2,1)S(1)} collective-permute-done((bf16[384,768]{1,0:T(8,128)(2,1)S(1)}, bf16[384,768]{1,0:T(8,128)(2,1)S(1)}, u32[]{:S(2)}, u32[]{:S(2)}) %collective-permute-start.7) | collective-permute-done | bytes 589856 | tf_op jit(solution)/shard_map/ppermute | solution.py:21
  69.8 1.6 %shard_map.77 = (f32[384,768]{1,0:T(8,128)}, f32[384,768]{1,0:T(8,128)}, f32[384]{0:T(512)}) custom-call(f32[384,768]{1,0:T(8,128)S(1)} %get-tuple-element.31.refs_2_.refs_0_, f32[1,384]{1,0:T(1,128)S(1)} %get-tuple-element.32.refs_1_, f32[384,768]{1,0:T(8,128)S(1)} %shard_map.76.refs_2_, f32[384,896]{1,0:T(8,128)S(1)} %collective-permute-done.8.refs_3_), custom_call_target="tpu_custom_call" | custom-call | bytes 6097920 | tf_op jit(solution)/shard_map/pallas_call | solution.py:50
  (13 shorter events, 0.2 us)
Async XLA Ops:
  0.6 28.4 %collective-permute-start.3 = (bf16[384,768]{1,0:T(8,128)(2,1)}, bf16[384,768]{1,0:T(8,128)(2,1)S(1)}, u32[]{:S(2)}, u32[]{:S(2)}) collective-permute-start(bf16[384,768]{1,0:T(8,128)(2,1)} %refs_0_.3), channel_id=1, source_target_pairs={{0,510},{1,3},{2,0},{3,5},{4,2},{5,7},{6,4},{7,9},{8,6},{9,11},{10... | collective-permute-start | bytes 1769480 | tf_op jit(solution)/shard_map/ppermute | solution.py:21
  4.7 1.1 %copy-start = (bf16[384,768]{1,0:T(8,128)(2,1)S(1)}, bf16[384,768]{1,0:T(8,128)(2,1)}, u32[]{:S(2)}) copy-start(bf16[384,768]{1,0:T(8,128)(2,1)} %refs_0_.2) | copy-start | bytes 1769476
  5.7 0.7 copy-start.3
  6.4 16.6 %copy-start.1 = (bf16[384,768]{1,0:T(8,128)(2,1)S(1)}, bf16[384,768]{1,0:T(8,128)(2,1)}, u32[]{:S(2)}) copy-start(bf16[384,768]{1,0:T(8,128)(2,1)} %refs_1_.3) | copy-start | bytes 1769476
  6.4 16.7 %copy-start.2 = (bf16[384,768]{1,0:T(8,128)(2,1)S(1)}, bf16[384,768]{1,0:T(8,128)(2,1)}, u32[]{:S(2)}) copy-start(bf16[384,768]{1,0:T(8,128)(2,1)} %refs_0_.3) | copy-start | bytes 1769476
  6.5 27.9 %collective-permute-start.2 = (bf16[2320,128]{1,0:T(8,128)(2,1)S(1)}, bf16[2320,128]{1,0:T(8,128)(2,1)S(1)}, u32[]{:S(2)}, u32[]{:S(2)}) collective-permute-start(bf16[2320,128]{1,0:T(8,128)(2,1)S(1)} %shard_map.67.refs_3_.refs_1_), channel_id=1, source_target_pairs={{0,2},{1,511},{2,4},{3,1},{4,6},{5,3},{6,8},{7,5},{8,10},{9,7},{10... | collective-permute-start | bytes 1781768 | tf_op jit(solution)/shard_map/ppermute | solution.py:21
  21.1 28.3 %collective-permute-start.1 = (bf16[2320,128]{1,0:T(8,128)(2,1)S(1)}, bf16[2320,128]{1,0:T(8,128)(2,1)S(1)}, u32[]{:S(2)}, u32[]{:S(2)}) collective-permute-start(bf16[2320,128]{1,0:T(8,128)(2,1)S(1)} %shard_map.67.refs_3_.refs_1_), channel_id=1, source_target_pairs={{0,511},{1,2},{2,1},{3,4},{4,3},{5,6},{6,5},{7,8},{8,7},{9,10},{10... | collective-permute-start | bytes 1781768 | tf_op jit(solution)/shard_map/ppermute | solution.py:21
  23.3 7.3 %collective-permute-start = (bf16[4624,128]{1,0:T(8,128)(2,1)S(1)}, bf16[4624,128]{1,0:T(8,128)(2,1)S(1)}, u32[]{:S(2)}, u32[]{:S(2)}) collective-permute-start(bf16[4624,128]{1,0:T(8,128)(2,1)S(1)} %get-tuple-element.19.refs_0_), channel_id=1, source_target_pairs={{0,1},{1,0},{2,3},{3,2},{4,5},{5,4},{6,7},{7,6},{8,9},{9,8},{10,11... | collective-permute-start | bytes 3551240 | tf_op jit(solution)/shard_map/ppermute | solution.py:21
  27.1 22.4 %collective-permute-start.4 = (bf16[2320,128]{1,0:T(8,128)(2,1)S(1)}, bf16[2320,128]{1,0:T(8,128)(2,1)S(1)}, u32[]{:S(2)}, u32[]{:S(2)}) collective-permute-start(bf16[2320,128]{1,0:T(8,128)(2,1)S(1)} %get-tuple-element.25), channel_id=1, source_target_pairs={{0,510},{1,3},{2,0},{3,5},{4,2},{5,7},{6,4},{7,9},{8,6},{9,11},{10... | collective-permute-start | bytes 1781768 | tf_op jit(solution)/shard_map/ppermute | solution.py:21
  37.6 22.3 %collective-permute-start.6 = (bf16[384,768]{1,0:T(8,128)(2,1)S(1)}, bf16[384,768]{1,0:T(8,128)(2,1)S(1)}, u32[]{:S(2)}, u32[]{:S(2)}) collective-permute-start(bf16[384,768]{1,0:T(8,128)(2,1)S(1)} %get-tuple-element.26.refs_3_), channel_id=1, source_target_pairs={{0,510},{1,3},{2,0},{3,5},{4,2},{5,7},{6,4},{7,9},{8,6},{9,11},{10... | collective-permute-start | bytes 1769480 | tf_op jit(solution)/shard_map/ppermute | solution.py:21
  51.0 14.3 %collective-permute-start.5 = (bf16[2320,128]{1,0:T(8,128)(2,1)S(1)}, bf16[2320,128]{1,0:T(8,128)(2,1)S(1)}, u32[]{:S(2)}, u32[]{:S(2)}) collective-permute-start(bf16[2320,128]{1,0:T(8,128)(2,1)S(1)} %get-tuple-element.29), channel_id=1, source_target_pairs={{0,2},{1,511},{2,4},{3,1},{4,6},{5,3},{6,8},{7,5},{8,10},{9,7},{10... | collective-permute-start | bytes 1781768 | tf_op jit(solution)/shard_map/ppermute | solution.py:21
  56.0 13.6 %collective-permute-start.7 = (bf16[384,768]{1,0:T(8,128)(2,1)S(1)}, bf16[384,768]{1,0:T(8,128)(2,1)S(1)}, u32[]{:S(2)}, u32[]{:S(2)}) collective-permute-start(bf16[384,768]{1,0:T(8,128)(2,1)S(1)} %get-tuple-element.33), channel_id=1, source_target_pairs={{0,511},{1,2},{2,1},{3,4},{4,3},{5,6},{6,5},{7,8},{8,7},{9,10},{10... | collective-permute-start | bytes 1769480 | tf_op jit(solution)/shard_map/ppermute | solution.py:21
  57.9 11.8 %collective-permute-start.8 = (f32[384,896]{1,0:T(8,128)S(1)}, f32[384,896]{1,0:T(8,128)S(1)}, u32[]{:S(2)}, u32[]{:S(2)}) collective-permute-start(f32[384,896]{1,0:T(8,128)S(1)} %get-tuple-element.34), channel_id=1, source_target_pairs={{0,1},{1,0},{2,3},{3,2},{4,5},{5,4},{6,7},{7,6},{8,9},{9,8},{10,11... | collective-permute-start | bytes 4128776 | tf_op jit(solution)/shard_map/ppermute | solution.py:21

commit v6 on v5

--- a/solution.py
+++ b/solution.py
@@ -192,26 +192,25 @@
     term_ref[...] = (term + more).astype(term_ref.dtype)
 
 
-def both_near(
-    own_ref, other_ref, text_ref, own_in, other_in, term_in, own_out, other_out, term_ref
-):
+def both_near(own_ref, other_ref, text_ref, own_in, other_in, own_out, other_out, term_ref):
     rows = term_ref.shape[0]
     text = unpacked(text_ref, rows)
     grad, folded, term = block(both_images(own_ref, rows), text)
     add_to(own_out, own_in, grad, folded)
     grad, folded, more = block(both_images(other_ref, rows), text)
     add_to(other_out, other_in, grad, folded)
-    term_ref[...] = (term_in[...] + term + more).astype(term_ref.dtype)
+    term_ref[...] = term + more
 
 
 def loss_row(folded):
     return jnp.sum(jnp.transpose(folded), axis=0, keepdims=True)
 
 
-def ahead_near(student_ref, teacher_ref, near_ref, ahead_out, term_ref):
+def ahead_near(student_ref, teacher_ref, near_ref, term_in, ahead_out, term_ref):
     rows = term_ref.shape[0]
     images = (student_ref[...], *unpacked(teacher_ref, rows))
-    grad, folded, term_ref[...] = block(images, unpacked(near_ref, rows))
+    grad, folded, term = block(images, unpacked(near_ref, rows))
+    term_ref[...] = (term_in[...] + term).astype(term_ref.dtype)
     put(ahead_out, 0, grad.astype(BF16))
     loss = loss_row(folded)
     high = loss.astype(BF16).astype(F32)
@@ -272,27 +271,13 @@
         both_second, [sums, sums, sent], 16 * dot, images, other, second, own_sum, other_sum
     )
     second_back = back(second_term)
-    ahead_sum, far_term = call(
-        ahead_near,
-        [packed, term],
-        4 * dot,
-        ahead_student,
-        ahead_teacher,
-        near,
-        after=(second_term,),
+    own_sum, other_sum, near_term = call(
+        both_near, [sums, sums, term], 0 * dot, images, other, near, own_sum, other_sum
+    )
+    ahead_sum, near_term = call(
+        ahead_near, [packed, sent], 0 * dot, ahead_student, ahead_teacher, near, near_term
     )
     ahead_back = onward(ahead_sum)
-    own_sum, other_sum, near_term = call(
-        both_near,
-        [sums, sums, sent],
-        0 * dot,
-        images,
-        other,
-        near,
-        own_sum,
-        other_sum,
-        far_term,
-    )
     near_back = across(near_term)
     other_back = within(other_sum)
     (own_term,) = call(gather_text, [term], 128 * dot, own_term, second_back)

time: 71.7 us -> 71.9 us (level)
  starting transfers between devices: 33.9 us -> 37.1 us
  waiting for transfers between devices: 21.6 us -> 18.4 us
    ppermute x9, waiting for transfers between devices: 21.6 us -> 18.4 us  [moved(): lax.ppermute(value, 'dp', [(i, (i + (odd if i % 2 else even)) % length) f...]
    ppermute x9, starting transfers between devices: 33.9 us -> 37.1 us  [moved(): lax.ppermute(value, 'dp', [(i, (i + (odd if i % 2 else even)) % length) f...]
where the time goes in v6:
time: 71.9 us; the launch traced here: 71.3 us
  starting transfers between devices  37.1 us (52%)
  waiting for transfers between devices  18.4 us (26%)
  Pallas kernels  13.3 us (18%)
  local copies, waits for them, and re-layouts  1.75 us (2%)
  between operations  0.83 us (1%)
    ppermute x9, starting transfers between devices, moved(): lax.ppermute(value, 'dp', [(i, (i + (odd if i % 2 else even)) % length) f...  37.1 us
    ppermute x9, waiting for transfers between devices, moved(): lax.ppermute(value, 'dp', [(i, (i + (odd if i % 2 else even)) % length) f...  18.4 us
    pallas_call x11, Pallas kernels, call(): pl.pallas_call(ordered, out_shape=out_shape, in_specs=[pl.BlockSpec(memor...  13.3 us
    unnamed x8, local copies, waits for them, and re-layouts  1.75 us
  transfers between devices with their start and end apart: 9, of which 4 were waited for; matrix products, arithmetic and copies ran while one was open for 0% of the time, Pallas kernels for 16%

profile of v6, /device:TPU:1, one launch (start us, length us, event | category | flops | bytes accessed | tf_op | source)
XLA Modules:
  0.0 71.3 jit_solution(5359858582790222871)
XLA Ops:
  0.6 4.0 %collective-permute-start.3 = (bf16[384,768]{1,0:T(8,128)(2,1)}, bf16[384,768]{1,0:T(8,128)(2,1)S(1)}, u32[]{:S(2)}, u32[]{:S(2)}) collective-permute-start(bf16[384,768]{1,0:T(8,128)(2,1)} %refs_0_.3), channel_id=1, source_target_pairs={{0,510},{1,3},{2,0},{3,5},{4,2},{5,7},{6,4},{7,9},{8,6},{9,11},{10... | collective-permute-start | bytes 1769480 | tf_op jit(solution)/shard_map/ppermute | solution.py:21
  4.7 1.1 %copy-done = bf16[384,768]{1,0:T(8,128)(2,1)S(1)} copy-done((bf16[384,768]{1,0:T(8,128)(2,1)S(1)}, bf16[384,768]{1,0:T(8,128)(2,1)}, u32[]{:S(2)}) %copy-start) | copy-done | bytes 589848
  5.7 0.7 copy-done.3
  6.5 14.6 %collective-permute-start.2 = (bf16[2320,128]{1,0:T(8,128)(2,1)S(1)}, bf16[2320,128]{1,0:T(8,128)(2,1)S(1)}, u32[]{:S(2)}, u32[]{:S(2)}) collective-permute-start(bf16[2320,128]{1,0:T(8,128)(2,1)S(1)} %shard_map.67.refs_3_.refs_1_), channel_id=1, source_target_pairs={{0,2},{1,511},{2,4},{3,1},{4,6},{5,3},{6,8},{7,5},{8,10},{9,7},{10... | collective-permute-start | bytes 1781768 | tf_op jit(solution)/shard_map/ppermute | solution.py:21
  21.1 1.9 %collective-permute-start.1 = (bf16[2320,128]{1,0:T(8,128)(2,1)S(1)}, bf16[2320,128]{1,0:T(8,128)(2,1)S(1)}, u32[]{:S(2)}, u32[]{:S(2)}) collective-permute-start(bf16[2320,128]{1,0:T(8,128)(2,1)S(1)} %shard_map.67.refs_3_.refs_1_), channel_id=1, source_target_pairs={{0,511},{1,2},{2,1},{3,4},{4,3},{5,6},{6,5},{7,8},{8,7},{9,10},{10... | collective-permute-start | bytes 1781768 | tf_op jit(solution)/shard_map/ppermute | solution.py:21
  23.1 0.2 shard_map.68
  23.3 3.7 %collective-permute-start = (bf16[4624,128]{1,0:T(8,128)(2,1)S(1)}, bf16[4624,128]{1,0:T(8,128)(2,1)S(1)}, u32[]{:S(2)}, u32[]{:S(2)}) collective-permute-start(bf16[4624,128]{1,0:T(8,128)(2,1)S(1)} %get-tuple-element.19.refs_0_), channel_id=1, source_target_pairs={{0,1},{1,0},{2,3},{3,2},{4,5},{5,4},{6,7},{7,6},{8,9},{9,8},{10,11... | collective-permute-start | bytes 3551240 | tf_op jit(solution)/shard_map/ppermute | solution.py:21
  27.1 1.9 %collective-permute-start.4 = (bf16[2320,128]{1,0:T(8,128)(2,1)S(1)}, bf16[2320,128]{1,0:T(8,128)(2,1)S(1)}, u32[]{:S(2)}, u32[]{:S(2)}) collective-permute-start(bf16[2320,128]{1,0:T(8,128)(2,1)S(1)} %get-tuple-element.26), channel_id=1, source_target_pairs={{0,510},{1,3},{2,0},{3,5},{4,2},{5,7},{6,4},{7,9},{8,6},{9,11},{10... | collective-permute-start | bytes 1781768 | tf_op jit(solution)/shard_map/ppermute | solution.py:21
  29.0 1.6 %shard_map.69 = (f32[384,896]{1,0:T(8,128)S(1)}, f32[384,768]{1,0:T(8,128)S(1)}) custom-call(bf16[4624,128]{1,0:T(8,128)(2,1)S(1)} %get-tuple-element.19.refs_0_, bf16[2320,128]{1,0:T(8,128)(2,1)S(1)} %shard_map.67.refs_3_.refs_1_, bf16[384,768]{1,0:T(8,128)(2,1)S(1)} %collective-permute-done.3.refs_2_.refs_0_), custom_call_target="tpu_custom_call" | custom-call | flops 14495514624 | bytes 4333568 | tf_op jit(solution)/shard_map/pallas_call | solution.py:50
  30.6 1.6 %shard_map.70 = (f32[384,896]{1,0:T(8,128)S(1)}, f32[384,768]{1,0:T(8,128)S(1)}) custom-call(bf16[4624,128]{1,0:T(8,128)(2,1)S(1)} %collective-permute-done.refs_0_.refs_1_, bf16[2320,128]{1,0:T(8,128)(2,1)S(1)} %shard_map.67.refs_3_.refs_1_, f32[384,768]{1,0:T(8,128)S(1)} %get-tuple-element.21.refs_2_), custom_call_target="tpu_custom_call" | custom-call | flops 3623878656 | bytes 5513216 | tf_op jit(solution)/shard_map/pallas_call | solution.py:50
  32.2 2.2 %collective-permute-done.2.refs_2_ = bf16[2320,128]{1,0:T(8,128)(2,1)S(1)} collective-permute-done((bf16[2320,128]{1,0:T(8,128)(2,1)S(1)}, bf16[2320,128]{1,0:T(8,128)(2,1)S(1)}, u32[]{:S(2)}, u32[]{:S(2)}) %collective-permute-start.2) | collective-permute-done | bytes 593952 | tf_op jit(solution)/shard_map/ppermute | solution.py:21
  34.4 3.1 %shard_map.71 = (f32[384,896]{1,0:T(8,128)S(1)}, f32[384,896]{1,0:T(8,128)S(1)}, bf16[384,768]{1,0:T(8,128)(2,1)S(1)}) custom-call(bf16[4624,128]{1,0:T(8,128)(2,1)S(1)} %get-tuple-element.19.refs_0_, bf16[4624,128]{1,0:T(8,128)(2,1)S(1)} %collective-permute-done.refs_0_.refs_1_, bf16[2320,128]{1,0:T(8,128)(2,1)S(1)} %collective-permute-done.2.refs_2_, ...), custom_call_target="tpu_custom_call" | custom-call | flops 3623878656 | bytes 9056256 | tf_op jit(solution)/shard_map/pallas_call | solution.py:50
  37.5 1.9 %collective-permute-start.6 = (bf16[384,768]{1,0:T(8,128)(2,1)S(1)}, bf16[384,768]{1,0:T(8,128)(2,1)S(1)}, u32[]{:S(2)}, u32[]{:S(2)}) collective-permute-start(bf16[384,768]{1,0:T(8,128)(2,1)S(1)} %get-tuple-element.30), channel_id=1, source_target_pairs={{0,510},{1,3},{2,0},{3,5},{4,2},{5,7},{6,4},{7,9},{8,6},{9,11},{10... | collective-permute-start | bytes 1769480 | tf_op jit(solution)/shard_map/ppermute | solution.py:21
  39.5 3.1 %shard_map.72 = (f32[384,896]{1,0:T(8,128)S(1)}, f32[384,896]{1,0:T(8,128)S(1)}, f32[384,768]{1,0:T(8,128)S(1)}) custom-call(bf16[4624,128]{1,0:T(8,128)(2,1)S(1)} %get-tuple-element.19.refs_0_, bf16[4624,128]{1,0:T(8,128)(2,1)S(1)} %collective-permute-done.refs_0_.refs_1_, bf16[2320,128]{1,0:T(8,128)(2,1)S(1)} %collective-permute-done.1.refs_2_, ...), custom_call_target="tpu_custom_call" | custom-call | bytes 9646080 | tf_op jit(solution)/shard_map/pallas_call | solution.py:50
  42.6 6.8 %collective-permute-done.4.refs_1_ = bf16[2320,128]{1,0:T(8,128)(2,1)S(1)} collective-permute-done((bf16[2320,128]{1,0:T(8,128)(2,1)S(1)}, bf16[2320,128]{1,0:T(8,128)(2,1)S(1)}, u32[]{:S(2)}, u32[]{:S(2)}) %collective-permute-start.4) | collective-permute-done | bytes 593952 | tf_op jit(solution)/shard_map/ppermute | solution.py:21
  49.4 1.5 %shard_map.73 = (bf16[2320,128]{1,0:T(8,128)(2,1)S(1)}, bf16[384,768]{1,0:T(8,128)(2,1)S(1)}) custom-call(bf16[384,768]{1,0:T(8,128)(2,1)S(1)} %collective-permute-done.3.refs_2_.refs_0_, bf16[2320,128]{1,0:T(8,128)(2,1)S(1)} %collective-permute-done.4.refs_1_, bf16[2320,128]{1,0:T(8,128)(2,1)S(1)} %collective-permute-done.1.refs_2_, ...), custom_call_target="tpu_custom_call" | custom-call | bytes 4141056 | tf_op jit(solution)/shard_map/pallas_call | solution.py:50
  51.0 2.4 %collective-permute-start.5 = (bf16[2320,128]{1,0:T(8,128)(2,1)S(1)}, bf16[2320,128]{1,0:T(8,128)(2,1)S(1)}, u32[]{:S(2)}, u32[]{:S(2)}) collective-permute-start(bf16[2320,128]{1,0:T(8,128)(2,1)S(1)} %get-tuple-element.28), channel_id=1, source_target_pairs={{0,2},{1,511},{2,4},{3,1},{4,6},{5,3},{6,8},{7,5},{8,10},{9,7},{10... | collective-permute-start | bytes 1781768 | tf_op jit(solution)/shard_map/ppermute | solution.py:21
  53.4 4.2 %collective-permute-start.7 = (bf16[384,768]{1,0:T(8,128)(2,1)S(1)}, bf16[384,768]{1,0:T(8,128)(2,1)S(1)}, u32[]{:S(2)}, u32[]{:S(2)}) collective-permute-start(bf16[384,768]{1,0:T(8,128)(2,1)S(1)} %get-tuple-element.33), channel_id=1, source_target_pairs={{0,511},{1,2},{2,1},{3,4},{4,3},{5,6},{6,5},{7,8},{8,7},{9,10},{10... | collective-permute-start | bytes 1769480 | tf_op jit(solution)/shard_map/ppermute | solution.py:21
  57.6 2.3 %collective-permute-start.8 = (f32[384,896]{1,0:T(8,128)S(1)}, f32[384,896]{1,0:T(8,128)S(1)}, u32[]{:S(2)}, u32[]{:S(2)}) collective-permute-start(f32[384,896]{1,0:T(8,128)S(1)} %get-tuple-element.34), channel_id=1, source_target_pairs={{0,1},{1,0},{2,3},{3,2},{4,5},{5,4},{6,7},{7,6},{8,9},{9,8},{10,11... | collective-permute-start | bytes 4128776 | tf_op jit(solution)/shard_map/ppermute | solution.py:21
  59.9 0.1 shard_map.74.refs_2_.refs_0_
  60.0 7.3 %collective-permute-done.5.refs_1_ = bf16[2320,128]{1,0:T(8,128)(2,1)S(1)} collective-permute-done((bf16[2320,128]{1,0:T(8,128)(2,1)S(1)}, bf16[2320,128]{1,0:T(8,128)(2,1)S(1)}, u32[]{:S(2)}, u32[]{:S(2)}) %collective-permute-start.5) | collective-permute-done | bytes 593952 | tf_op jit(solution)/shard_map/ppermute | solution.py:21
  67.3 0.2 shard_map.75
  67.5 2.0 %collective-permute-done.7.refs_1_ = bf16[384,768]{1,0:T(8,128)(2,1)S(1)} collective-permute-done((bf16[384,768]{1,0:T(8,128)(2,1)S(1)}, bf16[384,768]{1,0:T(8,128)(2,1)S(1)}, u32[]{:S(2)}, u32[]{:S(2)}) %collective-permute-start.7) | collective-permute-done | bytes 589856 | tf_op jit(solution)/shard_map/ppermute | solution.py:21
  69.7 1.6 %shard_map.77 = (f32[384,768]{1,0:T(8,128)}, f32[384,768]{1,0:T(8,128)}, f32[384]{0:T(512)}) custom-call(f32[384,768]{1,0:T(8,128)S(1)} %get-tuple-element.31.refs_2_.refs_0_, f32[1,384]{1,0:T(1,128)S(1)} %get-tuple-element.32.refs_1_, f32[384,768]{1,0:T(8,128)S(1)} %shard_map.76.refs_2_, f32[384,896]{1,0:T(8,128)S(1)} %collective-permute-done.8.refs_3_), custom_call_target="tpu_custom_call" | custom-call | bytes 6097920 | tf_op jit(solution)/shard_map/pallas_call | solution.py:50
  (13 shorter events, 0.2 us)
Async XLA Ops:
  0.6 28.4 %collective-permute-start.3 = (bf16[384,768]{1,0:T(8,128)(2,1)}, bf16[384,768]{1,0:T(8,128)(2,1)S(1)}, u32[]{:S(2)}, u32[]{:S(2)}) collective-permute-start(bf16[384,768]{1,0:T(8,128)(2,1)} %refs_0_.3), channel_id=1, source_target_pairs={{0,510},{1,3},{2,0},{3,5},{4,2},{5,7},{6,4},{7,9},{8,6},{9,11},{10... | collective-permute-start | bytes 1769480 | tf_op jit(solution)/shard_map/ppermute | solution.py:21
  4.7 1.1 %copy-start = (bf16[384,768]{1,0:T(8,128)(2,1)S(1)}, bf16[384,768]{1,0:T(8,128)(2,1)}, u32[]{:S(2)}) copy-start(bf16[384,768]{1,0:T(8,128)(2,1)} %refs_0_.2) | copy-start | bytes 1769476
  5.7 0.7 copy-start.3
  6.4 16.6 %copy-start.1 = (bf16[384,768]{1,0:T(8,128)(2,1)S(1)}, bf16[384,768]{1,0:T(8,128)(2,1)}, u32[]{:S(2)}) copy-start(bf16[384,768]{1,0:T(8,128)(2,1)} %refs_1_.3) | copy-start | bytes 1769476
  6.4 16.7 %copy-start.2 = (bf16[384,768]{1,0:T(8,128)(2,1)S(1)}, bf16[384,768]{1,0:T(8,128)(2,1)}, u32[]{:S(2)}) copy-start(bf16[384,768]{1,0:T(8,128)(2,1)} %refs_0_.3) | copy-start | bytes 1769476
  6.5 27.9 %collective-permute-start.2 = (bf16[2320,128]{1,0:T(8,128)(2,1)S(1)}, bf16[2320,128]{1,0:T(8,128)(2,1)S(1)}, u32[]{:S(2)}, u32[]{:S(2)}) collective-permute-start(bf16[2320,128]{1,0:T(8,128)(2,1)S(1)} %shard_map.67.refs_3_.refs_1_), channel_id=1, source_target_pairs={{0,2},{1,511},{2,4},{3,1},{4,6},{5,3},{6,8},{7,5},{8,10},{9,7},{10... | collective-permute-start | bytes 1781768 | tf_op jit(solution)/shard_map/ppermute | solution.py:21
  21.1 18.3 %collective-permute-start.1 = (bf16[2320,128]{1,0:T(8,128)(2,1)S(1)}, bf16[2320,128]{1,0:T(8,128)(2,1)S(1)}, u32[]{:S(2)}, u32[]{:S(2)}) collective-permute-start(bf16[2320,128]{1,0:T(8,128)(2,1)S(1)} %shard_map.67.refs_3_.refs_1_), channel_id=1, source_target_pairs={{0,511},{1,2},{2,1},{3,4},{4,3},{5,6},{6,5},{7,8},{8,7},{9,10},{10... | collective-permute-start | bytes 1781768 | tf_op jit(solution)/shard_map/ppermute | solution.py:21
  23.3 7.3 %collective-permute-start = (bf16[4624,128]{1,0:T(8,128)(2,1)S(1)}, bf16[4624,128]{1,0:T(8,128)(2,1)S(1)}, u32[]{:S(2)}, u32[]{:S(2)}) collective-permute-start(bf16[4624,128]{1,0:T(8,128)(2,1)S(1)} %get-tuple-element.19.refs_0_), channel_id=1, source_target_pairs={{0,1},{1,0},{2,3},{3,2},{4,5},{5,4},{6,7},{7,6},{8,9},{9,8},{10,11... | collective-permute-start | bytes 3551240 | tf_op jit(solution)/shard_map/ppermute | solution.py:21
  27.1 22.4 %collective-permute-start.4 = (bf16[2320,128]{1,0:T(8,128)(2,1)S(1)}, bf16[2320,128]{1,0:T(8,128)(2,1)S(1)}, u32[]{:S(2)}, u32[]{:S(2)}) collective-permute-start(bf16[2320,128]{1,0:T(8,128)(2,1)S(1)} %get-tuple-element.26), channel_id=1, source_target_pairs={{0,510},{1,3},{2,0},{3,5},{4,2},{5,7},{6,4},{7,9},{8,6},{9,11},{10... | collective-permute-start | bytes 1781768 | tf_op jit(solution)/shard_map/ppermute | solution.py:21
  37.5 22.4 %collective-permute-start.6 = (bf16[384,768]{1,0:T(8,128)(2,1)S(1)}, bf16[384,768]{1,0:T(8,128)(2,1)S(1)}, u32[]{:S(2)}, u32[]{:S(2)}) collective-permute-start(bf16[384,768]{1,0:T(8,128)(2,1)S(1)} %get-tuple-element.30), channel_id=1, source_target_pairs={{0,510},{1,3},{2,0},{3,5},{4,2},{5,7},{6,4},{7,9},{8,6},{9,11},{10... | collective-permute-start | bytes 1769480 | tf_op jit(solution)/shard_map/ppermute | solution.py:21
  51.0 16.3 %collective-permute-start.5 = (bf16[2320,128]{1,0:T(8,128)(2,1)S(1)}, bf16[2320,128]{1,0:T(8,128)(2,1)S(1)}, u32[]{:S(2)}, u32[]{:S(2)}) collective-permute-start(bf16[2320,128]{1,0:T(8,128)(2,1)S(1)} %get-tuple-element.28), channel_id=1, source_target_pairs={{0,2},{1,511},{2,4},{3,1},{4,6},{5,3},{6,8},{7,5},{8,10},{9,7},{10... | collective-permute-start | bytes 1781768 | tf_op jit(solution)/shard_map/ppermute | solution.py:21
  53.4 16.1 %collective-permute-start.7 = (bf16[384,768]{1,0:T(8,128)(2,1)S(1)}, bf16[384,768]{1,0:T(8,128)(2,1)S(1)}, u32[]{:S(2)}, u32[]{:S(2)}) collective-permute-start(bf16[384,768]{1,0:T(8,128)(2,1)S(1)} %get-tuple-element.33), channel_id=1, source_target_pairs={{0,511},{1,2},{2,1},{3,4},{4,3},{5,6},{6,5},{7,8},{8,7},{9,10},{10... | collective-permute-start | bytes 1769480 | tf_op jit(solution)/shard_map/ppermute | solution.py:21
  57.6 12.1 %collective-permute-start.8 = (f32[384,896]{1,0:T(8,128)S(1)}, f32[384,896]{1,0:T(8,128)S(1)}, u32[]{:S(2)}, u32[]{:S(2)}) collective-permute-start(f32[384,896]{1,0:T(8,128)S(1)} %get-tuple-element.34), channel_id=1, source_target_pairs={{0,1},{1,0},{2,3},{3,2},{4,5},{5,4},{6,7},{7,6},{8,9},{9,8},{10,11... | collective-permute-start | bytes 4128776 | tf_op jit(solution)/shard_map/ppermute | solution.py:21

commit v7 on v5

--- a/solution.py
+++ b/solution.py
@@ -102,19 +102,22 @@
     return jnp.concatenate(tiles, axis=1)
 
 
-def pack_text(text_ref, species_ref, out_ref):
+def write_ids(species_ref, ids_ref):
+    ids_ref[...] = digits(species_ref[...])
+
+
+def pack_text(text_ref, ids_ref, out_ref):
     put(out_ref, 0, text_ref[...])
-    out_ref[out_ref.shape[0] - EXTRA :, :] = digits(species_ref[...])
-
-
-def pack_images(student_ref, teacher_ref, species_ref, out_ref, teacher_out):
+    out_ref[out_ref.shape[0] - EXTRA :, :] = ids_ref[...]
+
+
+def pack_images(student_ref, teacher_ref, ids_ref, out_ref, teacher_out):
     rows, width = student_ref.shape
-    ids = digits(species_ref[...])
     put(out_ref, 0, student_ref[...])
     put(out_ref, rows * width // LANES, teacher_ref[...])
-    out_ref[out_ref.shape[0] - EXTRA :, :] = ids
+    out_ref[out_ref.shape[0] - EXTRA :, :] = ids_ref[...]
     put(teacher_out, 0, teacher_ref[...])
-    teacher_out[teacher_out.shape[0] - EXTRA :, :] = ids
+    teacher_out[teacher_out.shape[0] - EXTRA :, :] = ids_ref[...]
 
 
 def pair(student, teacher, ids, text, text_ids):
@@ -163,10 +166,15 @@
     return grad, folded, text_term(slope, student)
 
 
-def add_to(sums_ref, sums_in, grad, folded):
-    width = grad.shape[1]
-    sums_ref[:, :width] = sums_in[:, :width] + grad
-    sums_ref[:, width:] = sums_in[:, width:] + folded
+def two_blocks(images, texts, sums_in, sums_out):
+    rows, width = texts[0].shape
+    pairs = [pair(student, teacher, ids, *texts) for student, teacher, ids in images]
+    slope = jnp.concatenate([slope for slope, _ in pairs], axis=0)
+    grad = jnp.dot(slope, texts[0], preferred_element_type=F32)
+    for k, (was, out) in enumerate(zip(sums_in, sums_out)):
+        out[:, :width] = was[:, :width] + grad[k * rows : (k + 1) * rows, :]
+        out[:, width:] = was[:, width:] + pairs[k][1]
+    return text_term(slope, jnp.concatenate([student for student, _, _ in images], axis=0))
 
 
 def own_first(own_ref, text_ref, sums_ref, term_ref):
@@ -182,26 +190,25 @@
     term_ref[...] = term_in[...] + term
 
 
-def both_second(own_ref, other_ref, text_ref, own_in, other_in, own_out, other_out, term_ref):
+def both_second(
+    own_ref, other_ref, text_ref, ids_ref, own_in, other_in, own_out, other_out, term_ref
+):
     rows = term_ref.shape[0]
-    text = unpacked(text_ref, rows)
-    grad, folded, term = block(both_images(own_ref, rows), text)
-    add_to(own_out, own_in, grad, folded)
-    grad, folded, more = block(both_images(other_ref, rows), text)
-    add_to(other_out, other_in, grad, folded)
-    term_ref[...] = (term + more).astype(term_ref.dtype)
+    images = [both_images(ref, rows) for ref in (own_ref, other_ref)]
+    sums_in, sums_out = (own_in, other_in), (own_out, other_out)
+    texts = (text_ref[...], ids_of(ids_ref, rows))
+    term = two_blocks(images, texts, sums_in, sums_out)
+    term_ref[...] = term.astype(term_ref.dtype)
 
 
 def both_near(
     own_ref, other_ref, text_ref, own_in, other_in, term_in, own_out, other_out, term_ref
 ):
     rows = term_ref.shape[0]
-    text = unpacked(text_ref, rows)
-    grad, folded, term = block(both_images(own_ref, rows), text)
-    add_to(own_out, own_in, grad, folded)
-    grad, folded, more = block(both_images(other_ref, rows), text)
-    add_to(other_out, other_in, grad, folded)
-    term_ref[...] = (term_in[...] + term + more).astype(term_ref.dtype)
+    images = [both_images(ref, rows) for ref in (own_ref, other_ref)]
+    sums_in, sums_out = (own_in, other_in), (own_out, other_out)
+    term = two_blocks(images, unpacked(text_ref, rows), sums_in, sums_out)
+    term_ref[...] = (term_in[...] + term).astype(term_ref.dtype)
 
 
 def loss_row(folded):
@@ -250,8 +257,10 @@
     sent = spec(rows, width, BF16)
     packed = spec(rows * width // LANES + EXTRA, LANES, BF16)
     ahead_student = back(student_image_vectors)
-    (text,) = call(pack_text, [packed], 0, text_emb, species)
-    second = onward(text)
+    second = onward(text_emb)
+    (ids,) = call(write_ids, [spec(EXTRA, LANES, BF16)], 0, species)
+    second_ids = onward(ids)
+    (text,) = call(pack_text, [packed], 0, text_emb, ids)
     near = across(text)
     images, teacher = call(
         pack_images,
@@ -259,7 +268,7 @@
         0,
         student_image_vectors,
         teacher_emb,
-        species,
+        ids,
         after=(text,),
     )
     other = within(images)
@@ -269,7 +278,7 @@
     )
     other_sum, own_term = call(other_first, [sums, term], 16 * dot, other, text, own_term)
     own_sum, other_sum, second_term = call(
-        both_second, [sums, sums, sent], 16 * dot, images, other, second, own_sum, other_sum
+        both_second, [sums, sums, sent], 16 * dot, images, other, second, second_ids, own_sum, other_sum
     )
     second_back = back(second_term)
     ahead_sum, far_term = call(

time: 71.7 us -> 72.1 us (level)
  starting transfers between devices: 33.9 us -> 39.5 us
  waiting for transfers between devices: 21.6 us -> 17.2 us
  Pallas kernels: 13.3 us -> 12.4 us
    ppermute x9 -> x10, starting transfers between devices: 33.9 us -> 39.5 us  [moved(): lax.ppermute(value, 'dp', [(i, (i + (odd if i % 2 else even)) % length) f...]
    ppermute x9 -> x10, waiting for transfers between devices: 21.6 us -> 17.2 us  [moved(): lax.ppermute(value, 'dp', [(i, (i + (odd if i % 2 else even)) % length) f...]
    pallas_call x11 -> x12, Pallas kernels: 13.3 us -> 12.4 us  [call(): pl.pallas_call(ordered, out_shape=out_shape, in_specs=[pl.BlockSpec(memor...]
  transfers between devices with their start and end apart: 9 -> 10, of which waited for: 4 -> 3; matrix products, arithmetic and copies ran while one was open for 0% -> 0% of each run, Pallas kernels for 16% -> 15%
where the time goes in v7:
time: 72.1 us; the launch traced here: 71.7 us
  starting transfers between devices  39.5 us (55%)
  waiting for transfers between devices  17.2 us (24%)
  Pallas kernels  12.4 us (17%)
  local copies, waits for them, and re-layouts  1.75 us (2%)
  between operations  0.86 us (1%)
    ppermute x10, starting transfers between devices, moved(): lax.ppermute(value, 'dp', [(i, (i + (odd if i % 2 else even)) % length) f...  39.5 us
    ppermute x10, waiting for transfers between devices, moved(): lax.ppermute(value, 'dp', [(i, (i + (odd if i % 2 else even)) % length) f...  17.2 us
    pallas_call x12, Pallas kernels, call(): pl.pallas_call(ordered, out_shape=out_shape, in_specs=[pl.BlockSpec(memor...  12.4 us
    unnamed x8, local copies, waits for them, and re-layouts  1.75 us
  transfers between devices with their start and end apart: 10, of which 3 were waited for; matrix products, arithmetic and copies ran while one was open for 0% of the time, Pallas kernels for 15%

profile of v7, /device:TPU:1, one launch (start us, length us, event | category | flops | bytes accessed | tf_op | source)
XLA Modules:
  0.0 71.7 jit_solution(14592598395154568097)
XLA Ops:
  0.7 4.2 %collective-permute-start.4 = (bf16[384,768]{1,0:T(8,128)(2,1)}, bf16[384,768]{1,0:T(8,128)(2,1)S(1)}, u32[]{:S(2)}, u32[]{:S(2)}) collective-permute-start(bf16[384,768]{1,0:T(8,128)(2,1)} %refs_0_.5), channel_id=1, source_target_pairs={{0,510},{1,3},{2,0},{3,5},{4,2},{5,7},{6,4},{7,9},{8,6},{9,11},{10... | collective-permute-start | bytes 1769480 | tf_op jit(solution)/shard_map/ppermute | solution.py:21
  4.8 0.7 copy-done.3
  5.5 14.5 %collective-permute-start.3 = (bf16[16,128]{1,0:T(8,128)(2,1)S(1)}, bf16[16,128]{1,0:T(8,128)(2,1)S(1)}, u32[]{:S(2)}, u32[]{:S(2)}) collective-permute-start(bf16[16,128]{1,0:T(8,128)(2,1)S(1)} %shard_map.67.refs_1_.refs_2_), channel_id=1, source_target_pairs={{0,2},{1,511},{2,4},{3,1},{4,6},{5,3},{6,8},{7,5},{8,10},{9,7},{10... | collective-permute-start | bytes 12296 | tf_op jit(solution)/shard_map/ppermute | solution.py:21
  20.0 3.4 %collective-permute-start.2 = (bf16[384,768]{1,0:T(8,128)(2,1)}, bf16[384,768]{1,0:T(8,128)(2,1)S(1)}, u32[]{:S(2)}, u32[]{:S(2)}) collective-permute-start(bf16[384,768]{1,0:T(8,128)(2,1)} %refs_0_.4), channel_id=1, source_target_pairs={{0,2},{1,511},{2,4},{3,1},{4,6},{5,3},{6,8},{7,5},{8,10},{9,7},{10... | collective-permute-start | bytes 1769480 | tf_op jit(solution)/shard_map/ppermute | solution.py:21
  23.4 1.1 %copy-done.2 = bf16[384,768]{1,0:T(8,128)(2,1)S(1)} copy-done((bf16[384,768]{1,0:T(8,128)(2,1)S(1)}, bf16[384,768]{1,0:T(8,128)(2,1)}, u32[]{:S(2)}) %copy-start.2) | copy-done | bytes 589848
  24.5 1.9 %collective-permute-start.1 = (bf16[2320,128]{1,0:T(8,128)(2,1)S(1)}, bf16[2320,128]{1,0:T(8,128)(2,1)S(1)}, u32[]{:S(2)}, u32[]{:S(2)}) collective-permute-start(bf16[2320,128]{1,0:T(8,128)(2,1)S(1)} %shard_map.68.refs_3_.refs_1_), channel_id=1, source_target_pairs={{0,511},{1,2},{2,1},{3,4},{4,3},{5,6},{6,5},{7,8},{8,7},{9,10},{10... | collective-permute-start | bytes 1781768 | tf_op jit(solution)/shard_map/ppermute | solution.py:21
  26.5 0.2 shard_map.69
  26.7 3.4 %collective-permute-start = (bf16[4624,128]{1,0:T(8,128)(2,1)S(1)}, bf16[4624,128]{1,0:T(8,128)(2,1)S(1)}, u32[]{:S(2)}, u32[]{:S(2)}) collective-permute-start(bf16[4624,128]{1,0:T(8,128)(2,1)S(1)} %get-tuple-element.19.refs_0_), channel_id=1, source_target_pairs={{0,1},{1,0},{2,3},{3,2},{4,5},{5,4},{6,7},{7,6},{8,9},{9,8},{10,11... | collective-permute-start | bytes 3551240 | tf_op jit(solution)/shard_map/ppermute | solution.py:21
  30.1 2.3 %collective-permute-start.5 = (bf16[2320,128]{1,0:T(8,128)(2,1)S(1)}, bf16[2320,128]{1,0:T(8,128)(2,1)S(1)}, u32[]{:S(2)}, u32[]{:S(2)}) collective-permute-start(bf16[2320,128]{1,0:T(8,128)(2,1)S(1)} %get-tuple-element.25), channel_id=1, source_target_pairs={{0,510},{1,3},{2,0},{3,5},{4,2},{5,7},{6,4},{7,9},{8,6},{9,11},{10... | collective-permute-start | bytes 1781768 | tf_op jit(solution)/shard_map/ppermute | solution.py:21
  32.4 1.6 %shard_map.70 = (f32[384,896]{1,0:T(8,128)S(1)}, f32[384,768]{1,0:T(8,128)S(1)}) custom-call(bf16[4624,128]{1,0:T(8,128)(2,1)S(1)} %get-tuple-element.19.refs_0_, bf16[2320,128]{1,0:T(8,128)(2,1)S(1)} %shard_map.68.refs_3_.refs_1_, bf16[384,768]{1,0:T(8,128)(2,1)S(1)} %collective-permute-done.4.refs_2_.refs_0_), custom_call_target="tpu_custom_call" | custom-call | flops 14495514624 | bytes 4333568 | tf_op jit(solution)/shard_map/pallas_call | solution.py:50
  34.0 1.6 %shard_map.71 = (f32[384,896]{1,0:T(8,128)S(1)}, f32[384,768]{1,0:T(8,128)S(1)}) custom-call(bf16[4624,128]{1,0:T(8,128)(2,1)S(1)} %collective-permute-done.refs_0_.refs_1_, bf16[2320,128]{1,0:T(8,128)(2,1)S(1)} %shard_map.68.refs_3_.refs_1_, f32[384,768]{1,0:T(8,128)S(1)} %get-tuple-element.21.refs_2_), custom_call_target="tpu_custom_call" | custom-call | flops 3623878656 | bytes 5513216 | tf_op jit(solution)/shard_map/pallas_call | solution.py:50
  35.6 2.7 %shard_map.72 = (f32[384,896]{1,0:T(8,128)S(1)}, f32[384,896]{1,0:T(8,128)S(1)}, bf16[384,768]{1,0:T(8,128)(2,1)S(1)}) custom-call(bf16[4624,128]{1,0:T(8,128)(2,1)S(1)} %get-tuple-element.19.refs_0_, bf16[4624,128]{1,0:T(8,128)(2,1)S(1)} %collective-permute-done.refs_0_.refs_1_, bf16[384,768]{1,0:T(8,128)(2,1)S(1)} %collective-permute-done.2.refs_2_, ...), custom_call_target="tpu_custom_call" | custom-call | flops 3623878656 | bytes 9056256 | tf_op jit(solution)/shard_map/pallas_call | solution.py:50
  38.3 1.9 %collective-permute-start.7 = (bf16[384,768]{1,0:T(8,128)(2,1)S(1)}, bf16[384,768]{1,0:T(8,128)(2,1)S(1)}, u32[]{:S(2)}, u32[]{:S(2)}) collective-permute-start(bf16[384,768]{1,0:T(8,128)(2,1)S(1)} %get-tuple-element.26.refs_3_), channel_id=1, source_target_pairs={{0,510},{1,3},{2,0},{3,5},{4,2},{5,7},{6,4},{7,9},{8,6},{9,11},{10... | collective-permute-start | bytes 1769480 | tf_op jit(solution)/shard_map/ppermute | solution.py:21
  40.2 10.2 %collective-permute-done.5.refs_1_ = bf16[2320,128]{1,0:T(8,128)(2,1)S(1)} collective-permute-done((bf16[2320,128]{1,0:T(8,128)(2,1)S(1)}, bf16[2320,128]{1,0:T(8,128)(2,1)S(1)}, u32[]{:S(2)}, u32[]{:S(2)}) %collective-permute-start.5) | collective-permute-done | bytes 593952 | tf_op jit(solution)/shard_map/ppermute | solution.py:21
  50.4 1.6 %shard_map.73 = (bf16[2320,128]{1,0:T(8,128)(2,1)S(1)}, f32[384,768]{1,0:T(8,128)S(1)}) custom-call(bf16[384,768]{1,0:T(8,128)(2,1)S(1)} %collective-permute-done.4.refs_2_.refs_0_, bf16[2320,128]{1,0:T(8,128)(2,1)S(1)} %collective-permute-done.5.refs_1_, bf16[2320,128]{1,0:T(8,128)(2,1)S(1)} %collective-permute-done.1.refs_2_, ...), custom_call_target="tpu_custom_call" | custom-call | flops 905969664 | bytes 3551232 | tf_op jit(solution)/shard_map/pallas_call | solution.py:50
  52.0 3.8 %collective-permute-start.6 = (bf16[2320,128]{1,0:T(8,128)(2,1)S(1)}, bf16[2320,128]{1,0:T(8,128)(2,1)S(1)}, u32[]{:S(2)}, u32[]{:S(2)}) collective-permute-start(bf16[2320,128]{1,0:T(8,128)(2,1)S(1)} %get-tuple-element.29), channel_id=1, source_target_pairs={{0,2},{1,511},{2,4},{3,1},{4,6},{5,3},{6,8},{7,5},{8,10},{9,7},{10... | collective-permute-start | bytes 1781768 | tf_op jit(solution)/shard_map/ppermute | solution.py:21
  55.8 2.7 %shard_map.74 = (f32[384,896]{1,0:T(8,128)S(1)}, f32[384,896]{1,0:T(8,128)S(1)}, bf16[384,768]{1,0:T(8,128)(2,1)S(1)}) custom-call(bf16[4624,128]{1,0:T(8,128)(2,1)S(1)} %get-tuple-element.19.refs_0_, bf16[4624,128]{1,0:T(8,128)(2,1)S(1)} %collective-permute-done.refs_0_.refs_1_, bf16[2320,128]{1,0:T(8,128)(2,1)S(1)} %collective-permute-done.1.refs_2_, ...), custom_call_target="tpu_custom_call" | custom-call | bytes 10235904 | tf_op jit(solution)/shard_map/pallas_call | solution.py:50
  58.5 1.9 %collective-permute-start.8 = (bf16[384,768]{1,0:T(8,128)(2,1)S(1)}, bf16[384,768]{1,0:T(8,128)(2,1)S(1)}, u32[]{:S(2)}, u32[]{:S(2)}) collective-permute-start(bf16[384,768]{1,0:T(8,128)(2,1)S(1)} %get-tuple-element.33), channel_id=1, source_target_pairs={{0,511},{1,2},{2,1},{3,4},{4,3},{5,6},{6,5},{7,8},{8,7},{9,10},{10... | collective-permute-start | bytes 1769480 | tf_op jit(solution)/shard_map/ppermute | solution.py:21
  60.4 2.3 %collective-permute-start.9 = (f32[384,896]{1,0:T(8,128)S(1)}, f32[384,896]{1,0:T(8,128)S(1)}, u32[]{:S(2)}, u32[]{:S(2)}) collective-permute-start(f32[384,896]{1,0:T(8,128)S(1)} %get-tuple-element.34), channel_id=1, source_target_pairs={{0,1},{1,0},{2,3},{3,2},{4,5},{5,4},{6,7},{7,6},{8,9},{9,8},{10,11... | collective-permute-start | bytes 4128776 | tf_op jit(solution)/shard_map/ppermute | solution.py:21
  62.8 0.9 %collective-permute-done.6.refs_1_ = bf16[2320,128]{1,0:T(8,128)(2,1)S(1)} collective-permute-done((bf16[2320,128]{1,0:T(8,128)(2,1)S(1)}, bf16[2320,128]{1,0:T(8,128)(2,1)S(1)}, u32[]{:S(2)}, u32[]{:S(2)}) %collective-permute-start.6) | collective-permute-done | bytes 593952 | tf_op jit(solution)/shard_map/ppermute | solution.py:21
  63.7 0.2 shard_map.76
  64.0 6.0 %collective-permute-done.8.refs_1_ = bf16[384,768]{1,0:T(8,128)(2,1)S(1)} collective-permute-done((bf16[384,768]{1,0:T(8,128)(2,1)S(1)}, bf16[384,768]{1,0:T(8,128)(2,1)S(1)}, u32[]{:S(2)}, u32[]{:S(2)}) %collective-permute-start.8) | collective-permute-done | bytes 589856 | tf_op jit(solution)/shard_map/ppermute | solution.py:21
  70.0 0.1 shard_map.77.refs_2_
  70.1 1.6 %shard_map.78 = (f32[384,768]{1,0:T(8,128)}, f32[384,768]{1,0:T(8,128)}, f32[384]{0:T(512)}) custom-call(f32[384,768]{1,0:T(8,128)S(1)} %get-tuple-element.31.refs_2_.refs_0_, f32[1,384]{1,0:T(1,128)S(1)} %get-tuple-element.32.refs_1_, f32[384,768]{1,0:T(8,128)S(1)} %shard_map.77.refs_2_, f32[384,896]{1,0:T(8,128)S(1)} %collective-permute-done.9.refs_3_), custom_call_target="tpu_custom_call" | custom-call | bytes 6097920 | tf_op jit(solution)/shard_map/pallas_call | solution.py:50
  (16 shorter events, 0.2 us)
Async XLA Ops:
  0.6 25.8 %copy-start.1 = (bf16[384,768]{1,0:T(8,128)(2,1)S(1)}, bf16[384,768]{1,0:T(8,128)(2,1)}, u32[]{:S(2)}) copy-start(bf16[384,768]{1,0:T(8,128)(2,1)} %refs_0_.5) | copy-start | bytes 1769476
  0.6 25.8 %copy-start = (bf16[384,768]{1,0:T(8,128)(2,1)S(1)}, bf16[384,768]{1,0:T(8,128)(2,1)}, u32[]{:S(2)}) copy-start(bf16[384,768]{1,0:T(8,128)(2,1)} %refs_1_.1) | copy-start | bytes 1769476
  0.7 29.4 %collective-permute-start.4 = (bf16[384,768]{1,0:T(8,128)(2,1)}, bf16[384,768]{1,0:T(8,128)(2,1)S(1)}, u32[]{:S(2)}, u32[]{:S(2)}) collective-permute-start(bf16[384,768]{1,0:T(8,128)(2,1)} %refs_0_.5), channel_id=1, source_target_pairs={{0,510},{1,3},{2,0},{3,5},{4,2},{5,7},{6,4},{7,9},{8,6},{9,11},{10... | collective-permute-start | bytes 1769480 | tf_op jit(solution)/shard_map/ppermute | solution.py:21
  4.8 0.7 copy-start.3
  5.5 30.1 %collective-permute-start.3 = (bf16[16,128]{1,0:T(8,128)(2,1)S(1)}, bf16[16,128]{1,0:T(8,128)(2,1)S(1)}, u32[]{:S(2)}, u32[]{:S(2)}) collective-permute-start(bf16[16,128]{1,0:T(8,128)(2,1)S(1)} %shard_map.67.refs_1_.refs_2_), channel_id=1, source_target_pairs={{0,2},{1,511},{2,4},{3,1},{4,6},{5,3},{6,8},{7,5},{8,10},{9,7},{10... | collective-permute-start | bytes 12296 | tf_op jit(solution)/shard_map/ppermute | solution.py:21
  20.0 15.6 %collective-permute-start.2 = (bf16[384,768]{1,0:T(8,128)(2,1)}, bf16[384,768]{1,0:T(8,128)(2,1)S(1)}, u32[]{:S(2)}, u32[]{:S(2)}) collective-permute-start(bf16[384,768]{1,0:T(8,128)(2,1)} %refs_0_.4), channel_id=1, source_target_pairs={{0,2},{1,511},{2,4},{3,1},{4,6},{5,3},{6,8},{7,5},{8,10},{9,7},{10... | collective-permute-start | bytes 1769480 | tf_op jit(solution)/shard_map/ppermute | solution.py:21
  23.4 1.1 %copy-start.2 = (bf16[384,768]{1,0:T(8,128)(2,1)S(1)}, bf16[384,768]{1,0:T(8,128)(2,1)}, u32[]{:S(2)}) copy-start(bf16[384,768]{1,0:T(8,128)(2,1)} %refs_0_.4) | copy-start | bytes 1769476
  24.5 25.9 %collective-permute-start.1 = (bf16[2320,128]{1,0:T(8,128)(2,1)S(1)}, bf16[2320,128]{1,0:T(8,128)(2,1)S(1)}, u32[]{:S(2)}, u32[]{:S(2)}) collective-permute-start(bf16[2320,128]{1,0:T(8,128)(2,1)S(1)} %shard_map.68.refs_3_.refs_1_), channel_id=1, source_target_pairs={{0,511},{1,2},{2,1},{3,4},{4,3},{5,6},{6,5},{7,8},{8,7},{9,10},{10... | collective-permute-start | bytes 1781768 | tf_op jit(solution)/shard_map/ppermute | solution.py:21
  26.7 7.3 %collective-permute-start = (bf16[4624,128]{1,0:T(8,128)(2,1)S(1)}, bf16[4624,128]{1,0:T(8,128)(2,1)S(1)}, u32[]{:S(2)}, u32[]{:S(2)}) collective-permute-start(bf16[4624,128]{1,0:T(8,128)(2,1)S(1)} %get-tuple-element.19.refs_0_), channel_id=1, source_target_pairs={{0,1},{1,0},{2,3},{3,2},{4,5},{5,4},{6,7},{7,6},{8,9},{9,8},{10,11... | collective-permute-start | bytes 3551240 | tf_op jit(solution)/shard_map/ppermute | solution.py:21
  30.1 20.3 %collective-permute-start.5 = (bf16[2320,128]{1,0:T(8,128)(2,1)S(1)}, bf16[2320,128]{1,0:T(8,128)(2,1)S(1)}, u32[]{:S(2)}, u32[]{:S(2)}) collective-permute-start(bf16[2320,128]{1,0:T(8,128)(2,1)S(1)} %get-tuple-element.25), channel_id=1, source_target_pairs={{0,510},{1,3},{2,0},{3,5},{4,2},{5,7},{6,4},{7,9},{8,6},{9,11},{10... | collective-permute-start | bytes 1781768 | tf_op jit(solution)/shard_map/ppermute | solution.py:21
  38.3 24.4 %collective-permute-start.7 = (bf16[384,768]{1,0:T(8,128)(2,1)S(1)}, bf16[384,768]{1,0:T(8,128)(2,1)S(1)}, u32[]{:S(2)}, u32[]{:S(2)}) collective-permute-start(bf16[384,768]{1,0:T(8,128)(2,1)S(1)} %get-tuple-element.26.refs_3_), channel_id=1, source_target_pairs={{0,510},{1,3},{2,0},{3,5},{4,2},{5,7},{6,4},{7,9},{8,6},{9,11},{10... | collective-permute-start | bytes 1769480 | tf_op jit(solution)/shard_map/ppermute | solution.py:21
  52.0 11.8 %collective-permute-start.6 = (bf16[2320,128]{1,0:T(8,128)(2,1)S(1)}, bf16[2320,128]{1,0:T(8,128)(2,1)S(1)}, u32[]{:S(2)}, u32[]{:S(2)}) collective-permute-start(bf16[2320,128]{1,0:T(8,128)(2,1)S(1)} %get-tuple-element.29), channel_id=1, source_target_pairs={{0,2},{1,511},{2,4},{3,1},{4,6},{5,3},{6,8},{7,5},{8,10},{9,7},{10... | collective-permute-start | bytes 1781768 | tf_op jit(solution)/shard_map/ppermute | solution.py:21
  58.5 11.5 %collective-permute-start.8 = (bf16[384,768]{1,0:T(8,128)(2,1)S(1)}, bf16[384,768]{1,0:T(8,128)(2,1)S(1)}, u32[]{:S(2)}, u32[]{:S(2)}) collective-permute-start(bf16[384,768]{1,0:T(8,128)(2,1)S(1)} %get-tuple-element.33), channel_id=1, source_target_pairs={{0,511},{1,2},{2,1},{3,4},{4,3},{5,6},{6,5},{7,8},{8,7},{9,10},{10... | collective-permute-start | bytes 1769480 | tf_op jit(solution)/shard_map/ppermute | solution.py:21
  60.4 9.7 %collective-permute-start.9 = (f32[384,896]{1,0:T(8,128)S(1)}, f32[384,896]{1,0:T(8,128)S(1)}, u32[]{:S(2)}, u32[]{:S(2)}) collective-permute-start(f32[384,896]{1,0:T(8,128)S(1)} %get-tuple-element.34), channel_id=1, source_target_pairs={{0,1},{1,0},{2,3},{3,2},{4,5},{5,4},{6,7},{7,6},{8,9},{9,8},{10,11... | collective-permute-start | bytes 4128776 | tf_op jit(solution)/shard_map/ppermute | solution.py:21

commit v8 on v6

--- a/solution.py
+++ b/solution.py
@@ -37,6 +37,10 @@
 
 def back(value):
     return moved(value, -2, 2)
+
+
+def far_back(value):
+    return moved(value, -3, 3)
 
 
 def call(body, out_shape, flops, *args, after=()):
@@ -107,14 +111,11 @@
     out_ref[out_ref.shape[0] - EXTRA :, :] = digits(species_ref[...])
 
 
-def pack_images(student_ref, teacher_ref, species_ref, out_ref, teacher_out):
+def pack_images(student_ref, teacher_ref, species_ref, out_ref):
     rows, width = student_ref.shape
-    ids = digits(species_ref[...])
     put(out_ref, 0, student_ref[...])
     put(out_ref, rows * width // LANES, teacher_ref[...])
-    out_ref[out_ref.shape[0] - EXTRA :, :] = ids
-    put(teacher_out, 0, teacher_ref[...])
-    teacher_out[teacher_out.shape[0] - EXTRA :, :] = ids
+    out_ref[out_ref.shape[0] - EXTRA :, :] = digits(species_ref[...])
 
 
 def pair(student, teacher, ids, text, text_ids):
@@ -163,77 +164,72 @@
     return grad, folded, text_term(slope, student)
 
 
+def two_blocks(images, texts, sums_in, sums_out):
+    rows, width = texts[0].shape
+    pairs = [pair(student, teacher, ids, *texts) for student, teacher, ids in images]
+    slope = jnp.concatenate([slope for slope, _ in pairs], axis=0)
+    grad = jnp.dot(slope, texts[0], preferred_element_type=F32)
+    for k, (was, out) in enumerate(zip(sums_in, sums_out)):
+        out[:, :width] = was[:, :width] + grad[k * rows : (k + 1) * rows, :]
+        out[:, width:] = was[:, width:] + pairs[k][1]
+    return text_term(slope, jnp.concatenate([student for student, _, _ in images], axis=0))
+
+
+def own_first(own_ref, text_ref, sums_ref, term_ref):
+    rows, width = term_ref.shape
+    images = both_images(own_ref, rows)
+    sums_ref[:, :width], sums_ref[:, width:], term_ref[...] = block(images, unpacked(text_ref, rows))
+
+
 def add_to(sums_ref, sums_in, grad, folded):
     width = grad.shape[1]
     sums_ref[:, :width] = sums_in[:, :width] + grad
     sums_ref[:, width:] = sums_in[:, width:] + folded
 
 
-def own_first(own_ref, text_ref, sums_ref, term_ref):
-    rows, width = term_ref.shape
-    images = both_images(own_ref, rows)
-    sums_ref[:, :width], sums_ref[:, width:], term_ref[...] = block(images, unpacked(text_ref, rows))
-
-
-def other_first(other_ref, text_ref, term_in, sums_ref, term_ref):
-    rows, width = term_ref.shape
-    images = both_images(other_ref, rows)
-    sums_ref[:, :width], sums_ref[:, width:], term = block(images, unpacked(text_ref, rows))
-    term_ref[...] = term_in[...] + term
-
-
-def both_second(own_ref, other_ref, text_ref, own_in, other_in, own_out, other_out, term_ref):
+def own_next(own_ref, text_ref, sums_in, sums_ref, term_ref):
     rows = term_ref.shape[0]
-    text = unpacked(text_ref, rows)
-    grad, folded, term = block(both_images(own_ref, rows), text)
-    add_to(own_out, own_in, grad, folded)
-    grad, folded, more = block(both_images(other_ref, rows), text)
-    add_to(other_out, other_in, grad, folded)
-    term_ref[...] = (term + more).astype(term_ref.dtype)
-
-
-def both_near(own_ref, other_ref, text_ref, own_in, other_in, own_out, other_out, term_ref):
+    grad, folded, term = block(both_images(own_ref, rows), unpacked(text_ref, rows))
+    add_to(sums_ref, sums_in, grad, folded)
+    term_ref[...] = term.astype(term_ref.dtype)
+
+
+def other_two(
+    other_ref, text_ref, near_ref, own_in, near_in, sums_ref, near_out, own_out
+):
+    rows, width = own_in.shape
+    other = both_images(other_ref, rows)
+    grad, folded, term = block(other, unpacked(near_ref, rows))
+    near_out[...] = (near_in[...] + term).astype(near_out.dtype)
+    sums_ref[:, :width] = grad
+    sums_ref[:, width:] = folded
+    grad, folded, term = block(other, unpacked(text_ref, rows))
+    own_out[...] = own_in[...] + term
+    add_to(sums_ref, sums_ref, grad, folded)
+
+
+def both(own_ref, other_ref, text_ref, own_in, other_in, own_out, other_out, term_ref):
     rows = term_ref.shape[0]
-    text = unpacked(text_ref, rows)
-    grad, folded, term = block(both_images(own_ref, rows), text)
-    add_to(own_out, own_in, grad, folded)
-    grad, folded, more = block(both_images(other_ref, rows), text)
-    add_to(other_out, other_in, grad, folded)
-    term_ref[...] = term + more
+    images = [both_images(ref, rows) for ref in (own_ref, other_ref)]
+    sums_in, sums_out = (own_in, other_in), (own_out, other_out)
+    term = two_blocks(images, unpacked(text_ref, rows), sums_in, sums_out)
+    term_ref[...] = term.astype(term_ref.dtype)
 
 
 def loss_row(folded):
     return jnp.sum(jnp.transpose(folded), axis=0, keepdims=True)
 
 
-def ahead_near(student_ref, teacher_ref, near_ref, term_in, ahead_out, term_ref):
-    rows = term_ref.shape[0]
-    images = (student_ref[...], *unpacked(teacher_ref, rows))
-    grad, folded, term = block(images, unpacked(near_ref, rows))
-    term_ref[...] = (term_in[...] + term).astype(term_ref.dtype)
-    put(ahead_out, 0, grad.astype(BF16))
-    loss = loss_row(folded)
-    high = loss.astype(BF16).astype(F32)
-    ahead_out[ahead_out.shape[0] - EXTRA :, :] = spread(high, loss - high)
-
-
-def gather_text(own_ref, second_ref, term_ref):
-    term_ref[...] = own_ref[...] + second_ref[...].astype(F32)
-
-
-def gather_images(own_ref, ahead_ref, sums_ref, loss_ref):
-    rows, width = own_ref.shape[0], own_ref.shape[1] - LANES
-    sums_ref[...] = own_ref[:, :width] + taken(ahead_ref, 0, rows, width).astype(F32)
-    high, low = gathered(ahead_ref, ahead_ref.shape[0] - EXTRA, rows)
-    loss_ref[...] = loss_row(own_ref[:, width:]) + high + low
-
-
-def finish(sums_in, loss_in, term_in, other_ref, grad_ref, text_ref, loss_ref):
+def gather(own_ref, back_ref, term_ref):
+    term_ref[...] = own_ref[...] + back_ref[...].astype(F32)
+
+
+def finish(own_ref, other_ref, term_in, grad_ref, text_ref, loss_ref):
     rows, width = grad_ref.shape
     scale = SOFTMAX_TEMP_VALUE / float(width) ** 0.5
     text_ref[...] = term_in[...] * scale
-    grad_ref[...] = (sums_in[...] + other_ref[:, :width]) * scale
-    loss = loss_in[...] + loss_row(other_ref[:, width:])
+    grad_ref[...] = (own_ref[:, :width] + other_ref[:, :width]) * scale
+    loss = loss_row(own_ref[:, width:] + other_ref[:, width:])
     loss_ref[...] = (loss / float(WINDOW * rows)).reshape(rows)
 
 
@@ -248,13 +244,12 @@
     term = spec(rows, width, F32)
     sent = spec(rows, width, BF16)
     packed = spec(rows * width // LANES + EXTRA, LANES, BF16)
-    ahead_student = back(student_image_vectors)
     (text,) = call(pack_text, [packed], 0, text_emb, species)
+    near = across(text)
     second = onward(text)
-    near = across(text)
-    images, teacher = call(
+    (images,) = call(
         pack_images,
-        [spec(2 * rows * width // LANES + EXTRA, LANES, BF16), packed],
+        [spec(2 * rows * width // LANES + EXTRA, LANES, BF16)],
         0,
         student_image_vectors,
         teacher_emb,
@@ -262,39 +257,29 @@
         after=(text,),
     )
     other = within(images)
-    ahead_teacher = back(teacher)
-    own_sum, own_term = call(
-        own_first, [sums, term], 64 * dot, images, text, after=(ahead_student,)
-    )
-    other_sum, own_term = call(other_first, [sums, term], 16 * dot, other, text, own_term)
+    far = onward(near)
+    own_sum, own_term = call(own_first, [sums, term], 16 * dot, images, text)
+    own_sum, near_term = call(own_next, [sums, term], 32 * dot, images, near, own_sum)
+    other_sum, near_term, own_term = call(
+        other_two, [sums, sent, term], 0 * dot, other, text, near, own_term, near_term
+    )
+    near_back = across(near_term)
     own_sum, other_sum, second_term = call(
-        both_second, [sums, sums, sent], 16 * dot, images, other, second, own_sum, other_sum
+        both, [sums, sums, sent], 0 * dot, images, other, second, own_sum, other_sum
     )
     second_back = back(second_term)
-    own_sum, other_sum, near_term = call(
-        both_near, [sums, sums, term], 0 * dot, images, other, near, own_sum, other_sum
-    )
-    ahead_sum, near_term = call(
-        ahead_near, [packed, sent], 0 * dot, ahead_student, ahead_teacher, near, near_term
-    )
-    ahead_back = onward(ahead_sum)
-    near_back = across(near_term)
+    own_sum, far_term = call(own_next, [sums, sent], 0 * dot, images, far, own_sum)
+    last_back = far_back(far_term)
     other_back = within(other_sum)
-    (own_term,) = call(gather_text, [term], 128 * dot, own_term, second_back)
-    own_sum, loss = call(
-        gather_images, [term, spec(1, rows, F32)], 64 * dot, own_sum, ahead_back, after=(own_term,)
-    )
-    (own_term,) = call(
-        gather_text, [term], 32 * dot, own_term, near_back, after=(own_sum,)
-    )
+    for value, weight in ((near_back, 64 * dot), (second_back, 64 * dot), (last_back, 32 * dot)):
+        (own_term,) = call(gather, [term], weight, own_term, value)
     grad_student, grad_text, loss = call(
         finish,
         [term, term, jax.ShapeDtypeStruct((rows,), F32)],
         0,
         own_sum,
-        loss,
+        other_back,
         own_term,
-        other_back,
     )
     return grad_student, grad_text, loss
 

time: 71.9 us -> 74.9 us (1.042)
  starting transfers between devices: 37.1 us -> 43.8 us
  waiting for transfers between devices: 18.4 us -> 14.8 us
    ppermute x9 -> x8, starting transfers between devices: 37.1 us -> 43.8 us  [moved(): lax.ppermute(value, 'dp', [(i, (i + (odd if i % 2 else even)) % length) f...]
    ppermute x9 -> x8, waiting for transfers between devices: 18.4 us -> 14.8 us  [moved(): lax.ppermute(value, 'dp', [(i, (i + (odd if i % 2 else even)) % length) f...]
  transfers between devices with their start and end apart: 9 -> 8, of which waited for: 4 -> 2; matrix products, arithmetic and copies ran while one was open for 0% -> 0% of each run, Pallas kernels for 16% -> 15%
where the time goes in v8:
time: 74.9 us; the launch traced here: 74 us
  starting transfers between devices  43.8 us (58%)
  waiting for transfers between devices  14.8 us (20%)
  Pallas kernels  12.8 us (17%)
  local copies, waits for them, and re-layouts  1.81 us (2%)
  between operations  0.82 us (1%)
    ppermute x8, starting transfers between devices, moved(): lax.ppermute(value, 'dp', [(i, (i + (odd if i % 2 else even)) % length) f...  43.8 us
    ppermute x8, waiting for transfers between devices, moved(): lax.ppermute(value, 'dp', [(i, (i + (odd if i % 2 else even)) % length) f...  14.8 us
    pallas_call x11, Pallas kernels, call(): pl.pallas_call(ordered, out_shape=out_shape, in_specs=[pl.BlockSpec(memor...  12.8 us
    unnamed x8, local copies, waits for them, and re-layouts  1.81 us
  transfers between devices with their start and end apart: 8, of which 2 were waited for; matrix products, arithmetic and copies ran while one was open for 0% of the time, Pallas kernels for 15%

profile of v8, /device:TPU:1, one launch (start us, length us, event | category | flops | bytes accessed | tf_op | source)
XLA Modules:
  0.0 74.0 jit_solution(8150477900544045388)
XLA Ops:
  0.7 1.1 %copy-done.2 = bf16[384,768]{1,0:T(8,128)(2,1)S(1)} copy-done((bf16[384,768]{1,0:T(8,128)(2,1)S(1)}, bf16[384,768]{1,0:T(8,128)(2,1)}, u32[]{:S(2)}) %copy-start.2) | copy-done | bytes 589848
  1.8 0.7 copy-done.3
  2.5 0.1 shard_map.67.refs_3_.refs_1_
  2.5 4.7 %collective-permute-start = (bf16[2320,128]{1,0:T(8,128)(2,1)S(1)}, bf16[2320,128]{1,0:T(8,128)(2,1)S(1)}, u32[]{:S(2)}, u32[]{:S(2)}) collective-permute-start(bf16[2320,128]{1,0:T(8,128)(2,1)S(1)} %shard_map.67.refs_3_.refs_1_), channel_id=1, source_target_pairs={{0,511},{1,2},{2,1},{3,4},{4,3},{5,6},{6,5},{7,8},{8,7},{9,10},{10... | collective-permute-start | bytes 1781768 | tf_op jit(solution)/shard_map/ppermute | solution.py:21
  7.3 0.2 shard_map.68.refs_0_
  7.5 14.3 %collective-permute-start.2 = (bf16[4624,128]{1,0:T(8,128)(2,1)S(1)}, bf16[4624,128]{1,0:T(8,128)(2,1)S(1)}, u32[]{:S(2)}, u32[]{:S(2)}) collective-permute-start(bf16[4624,128]{1,0:T(8,128)(2,1)S(1)} %shard_map.68.refs_0_), channel_id=1, source_target_pairs={{0,1},{1,0},{2,3},{3,2},{4,5},{5,4},{6,7},{7,6},{8,9},{9,8},{10,11... | collective-permute-start | bytes 3551240 | tf_op jit(solution)/shard_map/ppermute | solution.py:21
  21.8 3.0 %collective-permute-start.3 = (bf16[2320,128]{1,0:T(8,128)(2,1)S(1)}, bf16[2320,128]{1,0:T(8,128)(2,1)S(1)}, u32[]{:S(2)}, u32[]{:S(2)}) collective-permute-start(bf16[2320,128]{1,0:T(8,128)(2,1)S(1)} %shard_map.67.refs_3_.refs_1_), channel_id=1, source_target_pairs={{0,2},{1,511},{2,4},{3,1},{4,6},{5,3},{6,8},{7,5},{8,10},{9,7},{10... | collective-permute-start | bytes 1781768 | tf_op jit(solution)/shard_map/ppermute | solution.py:21
  24.8 1.6 %shard_map.69 = (f32[384,896]{1,0:T(8,128)S(1)}, f32[384,768]{1,0:T(8,128)S(1)}) custom-call(bf16[4624,128]{1,0:T(8,128)(2,1)S(1)} %shard_map.68.refs_0_, bf16[2320,128]{1,0:T(8,128)(2,1)S(1)} %shard_map.67.refs_3_.refs_1_), custom_call_target="tpu_custom_call" | custom-call | flops 3623878656 | bytes 4333568 | tf_op jit(solution)/shard_map/pallas_call | solution.py:54
  26.3 0.0 collective-permute-done.refs_1_.refs_2_
  26.3 11.0 %collective-permute-start.1 = (bf16[2320,128]{1,0:T(8,128)(2,1)S(1)}, bf16[2320,128]{1,0:T(8,128)(2,1)S(1)}, u32[]{:S(2)}, u32[]{:S(2)}) collective-permute-start(bf16[2320,128]{1,0:T(8,128)(2,1)S(1)} %collective-permute-done.refs_1_.refs_2_), channel_id=1, source_target_pairs={{0,2},{1,511},{2,4},{3,1},{4,6},{5,3},{6,8},{7,5},{8,10},{9,7},{10... | collective-permute-start | bytes 1781768 | tf_op jit(solution)/shard_map/ppermute | solution.py:21
  37.3 1.6 %shard_map.70 = (f32[384,896]{1,0:T(8,128)S(1)}, f32[384,768]{1,0:T(8,128)S(1)}) custom-call(bf16[4624,128]{1,0:T(8,128)(2,1)S(1)} %shard_map.68.refs_0_, bf16[2320,128]{1,0:T(8,128)(2,1)S(1)} %collective-permute-done.refs_1_.refs_2_, f32[384,896]{1,0:T(8,128)S(1)} %get-tuple-element.15.refs_2_), custom_call_target="tpu_custom_call" | custom-call | flops 7247757312 | bytes 5709824 | tf_op jit(solution)/shard_map/pallas_call | solution.py:54
  38.9 3.1 %shard_map.71 = (f32[384,896]{1,0:T(8,128)S(1)}, bf16[384,768]{1,0:T(8,128)(2,1)S(1)}, f32[384,768]{1,0:T(8,128)S(1)}) custom-call(bf16[4624,128]{1,0:T(8,128)(2,1)S(1)} %collective-permute-done.2.refs_0_.refs_1_, bf16[2320,128]{1,0:T(8,128)(2,1)S(1)} %shard_map.67.refs_3_.refs_1_, bf16[2320,128]{1,0:T(8,128)(2,1)S(1)} %collective-permute-done.refs_1_.refs_2_, ...), custom_call_target="tpu_custom_call" | custom-call | bytes 7876608 | tf_op jit(solution)/shard_map/pallas_call | solution.py:54
  42.0 1.9 %collective-permute-start.5 = (bf16[384,768]{1,0:T(8,128)(2,1)S(1)}, bf16[384,768]{1,0:T(8,128)(2,1)S(1)}, u32[]{:S(2)}, u32[]{:S(2)}) collective-permute-start(bf16[384,768]{1,0:T(8,128)(2,1)S(1)} %get-tuple-element.24), channel_id=1, source_target_pairs={{0,511},{1,2},{2,1},{3,4},{4,3},{5,6},{6,5},{7,8},{8,7},{9,10},{10... | collective-permute-start | bytes 1769480 | tf_op jit(solution)/shard_map/ppermute | solution.py:21
  43.9 2.7 %shard_map.72 = (f32[384,896]{1,0:T(8,128)S(1)}, f32[384,896]{1,0:T(8,128)S(1)}, bf16[384,768]{1,0:T(8,128)(2,1)S(1)}) custom-call(bf16[4624,128]{1,0:T(8,128)(2,1)S(1)} %shard_map.68.refs_0_, bf16[4624,128]{1,0:T(8,128)(2,1)S(1)} %collective-permute-done.2.refs_0_.refs_1_, bf16[2320,128]{1,0:T(8,128)(2,1)S(1)} %collective-permute-done.3.refs_2_, ...), custom_call_target="tpu_custom_call" | custom-call | bytes 9056256 | tf_op jit(solution)/shard_map/pallas_call | solution.py:54
  46.6 1.9 %collective-permute-start.6 = (bf16[384,768]{1,0:T(8,128)(2,1)S(1)}, bf16[384,768]{1,0:T(8,128)(2,1)S(1)}, u32[]{:S(2)}, u32[]{:S(2)}) collective-permute-start(bf16[384,768]{1,0:T(8,128)(2,1)S(1)} %get-tuple-element.25), channel_id=1, source_target_pairs={{0,510},{1,3},{2,0},{3,5},{4,2},{5,7},{6,4},{7,9},{8,6},{9,11},{10... | collective-permute-start | bytes 1769480 | tf_op jit(solution)/shard_map/ppermute | solution.py:21
  48.6 2.4 %collective-permute-start.4 = (f32[384,896]{1,0:T(8,128)S(1)}, f32[384,896]{1,0:T(8,128)S(1)}, u32[]{:S(2)}, u32[]{:S(2)}) collective-permute-start(f32[384,896]{1,0:T(8,128)S(1)} %get-tuple-element.22), channel_id=1, source_target_pairs={{0,1},{1,0},{2,3},{3,2},{4,5},{5,4},{6,7},{7,6},{8,9},{9,8},{10,11... | collective-permute-start | bytes 4128776 | tf_op jit(solution)/shard_map/ppermute | solution.py:21
  51.0 1.6 %shard_map.73 = (f32[384,896]{1,0:T(8,128)S(1)}, bf16[384,768]{1,0:T(8,128)(2,1)S(1)}) custom-call(bf16[4624,128]{1,0:T(8,128)(2,1)S(1)} %shard_map.68.refs_0_, bf16[2320,128]{1,0:T(8,128)(2,1)S(1)} %collective-permute-done.1.refs_1_, f32[384,896]{1,0:T(8,128)S(1)} %get-tuple-element.20.refs_2_), custom_call_target="tpu_custom_call" | custom-call | bytes 5120000 | tf_op jit(solution)/shard_map/pallas_call | solution.py:54
  52.6 4.6 %collective-permute-start.7 = (bf16[384,768]{1,0:T(8,128)(2,1)S(1)}, bf16[384,768]{1,0:T(8,128)(2,1)S(1)}, u32[]{:S(2)}, u32[]{:S(2)}) collective-permute-start(bf16[384,768]{1,0:T(8,128)(2,1)S(1)} %get-tuple-element.26), channel_id=1, source_target_pairs={{0,509},{1,4},{2,511},{3,6},{4,1},{5,8},{6,3},{7,10},{8,5},{9,12},... | collective-permute-start | bytes 1769480 | tf_op jit(solution)/shard_map/ppermute | solution.py:21
  57.2 0.2 shard_map.74.refs_0_
  57.4 6.0 %collective-permute-done.6.refs_1_ = bf16[384,768]{1,0:T(8,128)(2,1)S(1)} collective-permute-done((bf16[384,768]{1,0:T(8,128)(2,1)S(1)}, bf16[384,768]{1,0:T(8,128)(2,1)S(1)}, u32[]{:S(2)}, u32[]{:S(2)}) %collective-permute-start.6) | collective-permute-done | bytes 589856 | tf_op jit(solution)/shard_map/ppermute | solution.py:21
  63.4 0.1 shard_map.75.refs_0_
  63.5 8.8 %collective-permute-done.7.refs_1_ = bf16[384,768]{1,0:T(8,128)(2,1)S(1)} collective-permute-done((bf16[384,768]{1,0:T(8,128)(2,1)S(1)}, bf16[384,768]{1,0:T(8,128)(2,1)S(1)}, u32[]{:S(2)}, u32[]{:S(2)}) %collective-permute-start.7) | collective-permute-done | bytes 589856 | tf_op jit(solution)/shard_map/ppermute | solution.py:21
  72.3 0.1 shard_map.76.refs_2_
  72.4 1.6 %shard_map.77 = (f32[384,768]{1,0:T(8,128)}, f32[384,768]{1,0:T(8,128)}, f32[384]{0:T(512)}) custom-call(f32[384,896]{1,0:T(8,128)S(1)} %get-tuple-element.21.refs_0_, f32[384,896]{1,0:T(8,128)S(1)} %collective-permute-done.4.refs_1_, f32[384,768]{1,0:T(8,128)S(1)} %shard_map.76.refs_2_), custom_call_target="tpu_custom_call" | custom-call | bytes 6292992 | tf_op jit(solution)/shard_map/pallas_call | solution.py:54
  (11 shorter events, 0.0 us)
Async XLA Ops:
  0.6 6.6 %copy-start = (bf16[384,768]{1,0:T(8,128)(2,1)S(1)}, bf16[384,768]{1,0:T(8,128)(2,1)}, u32[]{:S(2)}) copy-start(bf16[384,768]{1,0:T(8,128)(2,1)} %refs_0_.3) | copy-start | bytes 1769476
  0.6 1.1 %copy-start.2 = (bf16[384,768]{1,0:T(8,128)(2,1)S(1)}, bf16[384,768]{1,0:T(8,128)(2,1)}, u32[]{:S(2)}) copy-start(bf16[384,768]{1,0:T(8,128)(2,1)} %refs_0_.2) | copy-start | bytes 1769476
  1.8 0.7 copy-start.3
  2.4 4.8 %copy-start.1 = (bf16[384,768]{1,0:T(8,128)(2,1)S(1)}, bf16[384,768]{1,0:T(8,128)(2,1)}, u32[]{:S(2)}) copy-start(bf16[384,768]{1,0:T(8,128)(2,1)} %refs_1_.3) | copy-start | bytes 1769476
  2.5 23.8 %collective-permute-start = (bf16[2320,128]{1,0:T(8,128)(2,1)S(1)}, bf16[2320,128]{1,0:T(8,128)(2,1)S(1)}, u32[]{:S(2)}, u32[]{:S(2)}) collective-permute-start(bf16[2320,128]{1,0:T(8,128)(2,1)S(1)} %shard_map.67.refs_3_.refs_1_), channel_id=1, source_target_pairs={{0,511},{1,2},{2,1},{3,4},{4,3},{5,6},{6,5},{7,8},{8,7},{9,10},{10... | collective-permute-start | bytes 1781768 | tf_op jit(solution)/shard_map/ppermute | solution.py:21
  7.5 31.5 %collective-permute-start.2 = (bf16[4624,128]{1,0:T(8,128)(2,1)S(1)}, bf16[4624,128]{1,0:T(8,128)(2,1)S(1)}, u32[]{:S(2)}, u32[]{:S(2)}) collective-permute-start(bf16[4624,128]{1,0:T(8,128)(2,1)S(1)} %shard_map.68.refs_0_), channel_id=1, source_target_pairs={{0,1},{1,0},{2,3},{3,2},{4,5},{5,4},{6,7},{7,6},{8,9},{9,8},{10,11... | collective-permute-start | bytes 3551240 | tf_op jit(solution)/shard_map/ppermute | solution.py:21
  21.8 22.2 %collective-permute-start.3 = (bf16[2320,128]{1,0:T(8,128)(2,1)S(1)}, bf16[2320,128]{1,0:T(8,128)(2,1)S(1)}, u32[]{:S(2)}, u32[]{:S(2)}) collective-permute-start(bf16[2320,128]{1,0:T(8,128)(2,1)S(1)} %shard_map.67.refs_3_.refs_1_), channel_id=1, source_target_pairs={{0,2},{1,511},{2,4},{3,1},{4,6},{5,3},{6,8},{7,5},{8,10},{9,7},{10... | collective-permute-start | bytes 1781768 | tf_op jit(solution)/shard_map/ppermute | solution.py:21
  26.3 24.7 %collective-permute-start.1 = (bf16[2320,128]{1,0:T(8,128)(2,1)S(1)}, bf16[2320,128]{1,0:T(8,128)(2,1)S(1)}, u32[]{:S(2)}, u32[]{:S(2)}) collective-permute-start(bf16[2320,128]{1,0:T(8,128)(2,1)S(1)} %collective-permute-done.refs_1_.refs_2_), channel_id=1, source_target_pairs={{0,2},{1,511},{2,4},{3,1},{4,6},{5,3},{6,8},{7,5},{8,10},{9,7},{10... | collective-permute-start | bytes 1781768 | tf_op jit(solution)/shard_map/ppermute | solution.py:21
  42.0 15.2 %collective-permute-start.5 = (bf16[384,768]{1,0:T(8,128)(2,1)S(1)}, bf16[384,768]{1,0:T(8,128)(2,1)S(1)}, u32[]{:S(2)}, u32[]{:S(2)}) collective-permute-start(bf16[384,768]{1,0:T(8,128)(2,1)S(1)} %get-tuple-element.24), channel_id=1, source_target_pairs={{0,511},{1,2},{2,1},{3,4},{4,3},{5,6},{6,5},{7,8},{8,7},{9,10},{10... | collective-permute-start | bytes 1769480 | tf_op jit(solution)/shard_map/ppermute | solution.py:21
  46.6 16.7 %collective-permute-start.6 = (bf16[384,768]{1,0:T(8,128)(2,1)S(1)}, bf16[384,768]{1,0:T(8,128)(2,1)S(1)}, u32[]{:S(2)}, u32[]{:S(2)}) collective-permute-start(bf16[384,768]{1,0:T(8,128)(2,1)S(1)} %get-tuple-element.25), channel_id=1, source_target_pairs={{0,510},{1,3},{2,0},{3,5},{4,2},{5,7},{6,4},{7,9},{8,6},{9,11},{10... | collective-permute-start | bytes 1769480 | tf_op jit(solution)/shard_map/ppermute | solution.py:21
  48.6 23.8 %collective-permute-start.4 = (f32[384,896]{1,0:T(8,128)S(1)}, f32[384,896]{1,0:T(8,128)S(1)}, u32[]{:S(2)}, u32[]{:S(2)}) collective-permute-start(f32[384,896]{1,0:T(8,128)S(1)} %get-tuple-element.22), channel_id=1, source_target_pairs={{0,1},{1,0},{2,3},{3,2},{4,5},{5,4},{6,7},{7,6},{8,9},{9,8},{10,11... | collective-permute-start | bytes 4128776 | tf_op jit(solution)/shard_map/ppermute | solution.py:21
  52.6 19.7 %collective-permute-start.7 = (bf16[384,768]{1,0:T(8,128)(2,1)S(1)}, bf16[384,768]{1,0:T(8,128)(2,1)S(1)}, u32[]{:S(2)}, u32[]{:S(2)}) collective-permute-start(bf16[384,768]{1,0:T(8,128)(2,1)S(1)} %get-tuple-element.26), channel_id=1, source_target_pairs={{0,509},{1,4},{2,511},{3,6},{4,1},{5,8},{6,3},{7,10},{8,5},{9,12},... | collective-permute-start | bytes 1769480 | tf_op jit(solution)/shard_map/ppermute | solution.py:21

commit v9 on v7

--- a/solution.py
+++ b/solution.py
@@ -102,22 +102,19 @@
     return jnp.concatenate(tiles, axis=1)
 
 
-def write_ids(species_ref, ids_ref):
-    ids_ref[...] = digits(species_ref[...])
-
-
-def pack_text(text_ref, ids_ref, out_ref):
+def pack_text(text_ref, species_ref, out_ref):
     put(out_ref, 0, text_ref[...])
-    out_ref[out_ref.shape[0] - EXTRA :, :] = ids_ref[...]
-
-
-def pack_images(student_ref, teacher_ref, ids_ref, out_ref, teacher_out):
+    out_ref[out_ref.shape[0] - EXTRA :, :] = digits(species_ref[...])
+
+
+def pack_images(student_ref, teacher_ref, species_ref, out_ref, teacher_out):
     rows, width = student_ref.shape
+    ids = digits(species_ref[...])
     put(out_ref, 0, student_ref[...])
     put(out_ref, rows * width // LANES, teacher_ref[...])
-    out_ref[out_ref.shape[0] - EXTRA :, :] = ids_ref[...]
+    out_ref[out_ref.shape[0] - EXTRA :, :] = ids
     put(teacher_out, 0, teacher_ref[...])
-    teacher_out[teacher_out.shape[0] - EXTRA :, :] = ids_ref[...]
+    teacher_out[teacher_out.shape[0] - EXTRA :, :] = ids
 
 
 def pair(student, teacher, ids, text, text_ids):
@@ -177,7 +174,8 @@
     return text_term(slope, jnp.concatenate([student for student, _, _ in images], axis=0))
 
 
-def own_first(own_ref, text_ref, sums_ref, term_ref):
+def own_first(own_ref, text_ref, sums_ref, term_ref, text_out):
+    text_out[...] = text_ref[...]
     rows, width = term_ref.shape
     images = both_images(own_ref, rows)
     sums_ref[:, :width], sums_ref[:, width:], term_ref[...] = block(images, unpacked(text_ref, rows))
@@ -190,14 +188,11 @@
     term_ref[...] = term_in[...] + term
 
 
-def both_second(
-    own_ref, other_ref, text_ref, ids_ref, own_in, other_in, own_out, other_out, term_ref
-):
+def both(own_ref, other_ref, text_ref, own_in, other_in, own_out, other_out, term_ref):
     rows = term_ref.shape[0]
     images = [both_images(ref, rows) for ref in (own_ref, other_ref)]
     sums_in, sums_out = (own_in, other_in), (own_out, other_out)
-    texts = (text_ref[...], ids_of(ids_ref, rows))
-    term = two_blocks(images, texts, sums_in, sums_out)
+    term = two_blocks(images, unpacked(text_ref, rows), sums_in, sums_out)
     term_ref[...] = term.astype(term_ref.dtype)
 
 
@@ -257,28 +252,31 @@
     sent = spec(rows, width, BF16)
     packed = spec(rows * width // LANES + EXTRA, LANES, BF16)
     ahead_student = back(student_image_vectors)
-    second = onward(text_emb)
-    (ids,) = call(write_ids, [spec(EXTRA, LANES, BF16)], 0, species)
-    second_ids = onward(ids)
-    (text,) = call(pack_text, [packed], 0, text_emb, ids)
-    near = across(text)
+    (text,) = call(pack_text, [packed], 0, text_emb, species)
+    second = onward(text)
     images, teacher = call(
         pack_images,
         [spec(2 * rows * width // LANES + EXTRA, LANES, BF16), packed],
         0,
         student_image_vectors,
         teacher_emb,
-        ids,
+        species,
         after=(text,),
     )
     other = within(images)
     ahead_teacher = back(teacher)
-    own_sum, own_term = call(
-        own_first, [sums, term], 64 * dot, images, text, after=(ahead_student,)
-    )
+    own_sum, own_term, text_again = call(
+        own_first,
+        [sums, term, packed],
+        64 * dot,
+        images,
+        text,
+        after=(ahead_student,),
+    )
+    near = across(text_again)
     other_sum, own_term = call(other_first, [sums, term], 16 * dot, other, text, own_term)
     own_sum, other_sum, second_term = call(
-        both_second, [sums, sums, sent], 16 * dot, images, other, second, second_ids, own_sum, other_sum
+        both, [sums, sums, sent], 16 * dot, images, other, second, own_sum, other_sum
     )
     second_back = back(second_term)
     ahead_sum, far_term = call(

time: 72.1 us -> 74.2 us (1.029)
  starting transfers between devices: 39.5 us -> 46.3 us
  waiting for transfers between devices: 17.2 us -> 12.4 us
    ppermute x10 -> x9, starting transfers between devices: 39.5 us -> 46.3 us  [moved(): lax.ppermute(value, 'dp', [(i, (i + (odd if i % 2 else even)) % length) f...]
    ppermute x10 -> x9, waiting for transfers between devices: 17.2 us -> 12.4 us  [moved(): lax.ppermute(value, 'dp', [(i, (i + (odd if i % 2 else even)) % length) f...]
    pallas_call x12 -> x11, Pallas kernels: 12.4 us -> 12.5 us  [call(): pl.pallas_call(ordered, out_shape=out_shape, in_specs=[pl.BlockSpec(memor...]
  transfers between devices with their start and end apart: 10 -> 9, of which waited for: 3 -> 3; matrix products, arithmetic and copies ran while one was open for 0% -> 0% of each run, Pallas kernels for 15% -> 15%
where the time goes in v9:
time: 74.2 us; the launch traced here: 73.8 us
  starting transfers between devices  46.3 us (62%)
  Pallas kernels  12.5 us (17%)
  waiting for transfers between devices  12.4 us (17%)
  local copies, waits for them, and re-layouts  1.75 us (2%)
  between operations  0.82 us (1%)
    ppermute x9, starting transfers between devices, moved(): lax.ppermute(value, 'dp', [(i, (i + (odd if i % 2 else even)) % length) f...  46.3 us
    pallas_call x11, Pallas kernels, call(): pl.pallas_call(ordered, out_shape=out_shape, in_specs=[pl.BlockSpec(memor...  12.5 us
    ppermute x9, waiting for transfers between devices, moved(): lax.ppermute(value, 'dp', [(i, (i + (odd if i % 2 else even)) % length) f...  12.4 us
    unnamed x8, local copies, waits for them, and re-layouts  1.75 us
  transfers between devices with their start and end apart: 9, of which 3 were waited for; matrix products, arithmetic and copies ran while one was open for 0% of the time, Pallas kernels for 15%

profile of v9, /device:TPU:1, one launch (start us, length us, event | category | flops | bytes accessed | tf_op | source)
XLA Modules:
  0.0 73.8 jit_solution(15418415233625697439)
XLA Ops:
  0.6 4.0 %collective-permute-start.1 = (bf16[384,768]{1,0:T(8,128)(2,1)}, bf16[384,768]{1,0:T(8,128)(2,1)S(1)}, u32[]{:S(2)}, u32[]{:S(2)}) collective-permute-start(bf16[384,768]{1,0:T(8,128)(2,1)} %refs_0_.3), channel_id=1, source_target_pairs={{0,510},{1,3},{2,0},{3,5},{4,2},{5,7},{6,4},{7,9},{8,6},{9,11},{10... | collective-permute-start | bytes 1769480 | tf_op jit(solution)/shard_map/ppermute | solution.py:21
  4.7 1.1 %copy-done = bf16[384,768]{1,0:T(8,128)(2,1)S(1)} copy-done((bf16[384,768]{1,0:T(8,128)(2,1)S(1)}, bf16[384,768]{1,0:T(8,128)(2,1)}, u32[]{:S(2)}) %copy-start) | copy-done | bytes 589848
  5.7 0.7 copy-done.3
  6.5 14.6 %collective-permute-start.3 = (bf16[2320,128]{1,0:T(8,128)(2,1)S(1)}, bf16[2320,128]{1,0:T(8,128)(2,1)S(1)}, u32[]{:S(2)}, u32[]{:S(2)}) collective-permute-start(bf16[2320,128]{1,0:T(8,128)(2,1)S(1)} %shard_map.67.refs_3_.refs_1_), channel_id=1, source_target_pairs={{0,2},{1,511},{2,4},{3,1},{4,6},{5,3},{6,8},{7,5},{8,10},{9,7},{10... | collective-permute-start | bytes 1781768 | tf_op jit(solution)/shard_map/ppermute | solution.py:21
  21.2 0.2 shard_map.68
  21.4 2.9 %collective-permute-start = (bf16[4624,128]{1,0:T(8,128)(2,1)S(1)}, bf16[4624,128]{1,0:T(8,128)(2,1)S(1)}, u32[]{:S(2)}, u32[]{:S(2)}) collective-permute-start(bf16[4624,128]{1,0:T(8,128)(2,1)S(1)} %get-tuple-element.20.refs_0_), channel_id=1, source_target_pairs={{0,1},{1,0},{2,3},{3,2},{4,5},{5,4},{6,7},{7,6},{8,9},{9,8},{10,11... | collective-permute-start | bytes 3551240 | tf_op jit(solution)/shard_map/ppermute | solution.py:21
  24.3 1.9 %collective-permute-start.4 = (bf16[2320,128]{1,0:T(8,128)(2,1)S(1)}, bf16[2320,128]{1,0:T(8,128)(2,1)S(1)}, u32[]{:S(2)}, u32[]{:S(2)}) collective-permute-start(bf16[2320,128]{1,0:T(8,128)(2,1)S(1)} %get-tuple-element.27), channel_id=1, source_target_pairs={{0,510},{1,3},{2,0},{3,5},{4,2},{5,7},{6,4},{7,9},{8,6},{9,11},{10... | collective-permute-start | bytes 1781768 | tf_op jit(solution)/shard_map/ppermute | solution.py:21
  26.2 1.6 %shard_map.69 = (f32[384,896]{1,0:T(8,128)S(1)}, f32[384,768]{1,0:T(8,128)S(1)}, bf16[2320,128]{1,0:T(8,128)(2,1)S(1)}) custom-call(bf16[4624,128]{1,0:T(8,128)(2,1)S(1)} %get-tuple-element.20.refs_0_, bf16[2320,128]{1,0:T(8,128)(2,1)S(1)} %shard_map.67.refs_3_.refs_1_, bf16[384,768]{1,0:T(8,128)(2,1)S(1)} %collective-permute-done.1.refs_2_.refs_0_), custom_call_target="tpu_custom_call" | custom-call | flops 14495514624 | bytes 4927488 | tf_op jit(solution)/shard_map/pallas_call | solution.py:50
  27.8 3.5 %collective-permute-start.2 = (bf16[2320,128]{1,0:T(8,128)(2,1)S(1)}, bf16[2320,128]{1,0:T(8,128)(2,1)S(1)}, u32[]{:S(2)}, u32[]{:S(2)}) collective-permute-start(bf16[2320,128]{1,0:T(8,128)(2,1)S(1)} %get-tuple-element.21), channel_id=1, source_target_pairs={{0,511},{1,2},{2,1},{3,4},{4,3},{5,6},{6,5},{7,8},{8,7},{9,10},{10... | collective-permute-start | bytes 1781768 | tf_op jit(solution)/shard_map/ppermute | solution.py:21
  31.4 1.6 %shard_map.70 = (f32[384,896]{1,0:T(8,128)S(1)}, f32[384,768]{1,0:T(8,128)S(1)}) custom-call(bf16[4624,128]{1,0:T(8,128)(2,1)S(1)} %collective-permute-done.refs_0_.refs_1_, bf16[2320,128]{1,0:T(8,128)(2,1)S(1)} %shard_map.67.refs_3_.refs_1_, f32[384,768]{1,0:T(8,128)S(1)} %get-tuple-element.23.refs_2_), custom_call_target="tpu_custom_call" | custom-call | flops 3623878656 | bytes 5513216 | tf_op jit(solution)/shard_map/pallas_call | solution.py:50
  33.0 2.7 %shard_map.71 = (f32[384,896]{1,0:T(8,128)S(1)}, f32[384,896]{1,0:T(8,128)S(1)}, bf16[384,768]{1,0:T(8,128)(2,1)S(1)}) custom-call(bf16[4624,128]{1,0:T(8,128)(2,1)S(1)} %get-tuple-element.20.refs_0_, bf16[4624,128]{1,0:T(8,128)(2,1)S(1)} %collective-permute-done.refs_0_.refs_1_, bf16[2320,128]{1,0:T(8,128)(2,1)S(1)} %collective-permute-done.3.refs_2_, ...), custom_call_target="tpu_custom_call" | custom-call | flops 3623878656 | bytes 9056256 | tf_op jit(solution)/shard_map/pallas_call | solution.py:50
  35.7 1.9 %collective-permute-start.6 = (bf16[384,768]{1,0:T(8,128)(2,1)S(1)}, bf16[384,768]{1,0:T(8,128)(2,1)S(1)}, u32[]{:S(2)}, u32[]{:S(2)}) collective-permute-start(bf16[384,768]{1,0:T(8,128)(2,1)S(1)} %get-tuple-element.28.refs_3_), channel_id=1, source_target_pairs={{0,510},{1,3},{2,0},{3,5},{4,2},{5,7},{6,4},{7,9},{8,6},{9,11},{10... | collective-permute-start | bytes 1769480 | tf_op jit(solution)/shard_map/ppermute | solution.py:21
  37.6 5.5 %collective-permute-done.4.refs_1_ = bf16[2320,128]{1,0:T(8,128)(2,1)S(1)} collective-permute-done((bf16[2320,128]{1,0:T(8,128)(2,1)S(1)}, bf16[2320,128]{1,0:T(8,128)(2,1)S(1)}, u32[]{:S(2)}, u32[]{:S(2)}) %collective-permute-start.4) | collective-permute-done | bytes 593952 | tf_op jit(solution)/shard_map/ppermute | solution.py:21
  43.1 1.6 %shard_map.72 = (bf16[2320,128]{1,0:T(8,128)(2,1)S(1)}, f32[384,768]{1,0:T(8,128)S(1)}) custom-call(bf16[384,768]{1,0:T(8,128)(2,1)S(1)} %collective-permute-done.1.refs_2_.refs_0_, bf16[2320,128]{1,0:T(8,128)(2,1)S(1)} %collective-permute-done.4.refs_1_, bf16[2320,128]{1,0:T(8,128)(2,1)S(1)} %collective-permute-done.2.refs_2_, ...), custom_call_target="tpu_custom_call" | custom-call | flops 905969664 | bytes 3551232 | tf_op jit(solution)/shard_map/pallas_call | solution.py:50
  44.7 13.2 %collective-permute-start.5 = (bf16[2320,128]{1,0:T(8,128)(2,1)S(1)}, bf16[2320,128]{1,0:T(8,128)(2,1)S(1)}, u32[]{:S(2)}, u32[]{:S(2)}) collective-permute-start(bf16[2320,128]{1,0:T(8,128)(2,1)S(1)} %get-tuple-element.31), channel_id=1, source_target_pairs={{0,2},{1,511},{2,4},{3,1},{4,6},{5,3},{6,8},{7,5},{8,10},{9,7},{10... | collective-permute-start | bytes 1781768 | tf_op jit(solution)/shard_map/ppermute | solution.py:21
  57.9 2.7 %shard_map.73 = (f32[384,896]{1,0:T(8,128)S(1)}, f32[384,896]{1,0:T(8,128)S(1)}, bf16[384,768]{1,0:T(8,128)(2,1)S(1)}) custom-call(bf16[4624,128]{1,0:T(8,128)(2,1)S(1)} %get-tuple-element.20.refs_0_, bf16[4624,128]{1,0:T(8,128)(2,1)S(1)} %collective-permute-done.refs_0_.refs_1_, bf16[2320,128]{1,0:T(8,128)(2,1)S(1)} %collective-permute-done.2.refs_2_, ...), custom_call_target="tpu_custom_call" | custom-call | bytes 10235904 | tf_op jit(solution)/shard_map/pallas_call | solution.py:50
  60.5 1.9 %collective-permute-start.7 = (bf16[384,768]{1,0:T(8,128)(2,1)S(1)}, bf16[384,768]{1,0:T(8,128)(2,1)S(1)}, u32[]{:S(2)}, u32[]{:S(2)}) collective-permute-start(bf16[384,768]{1,0:T(8,128)(2,1)S(1)} %get-tuple-element.35), channel_id=1, source_target_pairs={{0,511},{1,2},{2,1},{3,4},{4,3},{5,6},{6,5},{7,8},{8,7},{9,10},{10... | collective-permute-start | bytes 1769480 | tf_op jit(solution)/shard_map/ppermute | solution.py:21
  62.5 2.3 %collective-permute-start.8 = (f32[384,896]{1,0:T(8,128)S(1)}, f32[384,896]{1,0:T(8,128)S(1)}, u32[]{:S(2)}, u32[]{:S(2)}) collective-permute-start(f32[384,896]{1,0:T(8,128)S(1)} %get-tuple-element.36), channel_id=1, source_target_pairs={{0,1},{1,0},{2,3},{3,2},{4,5},{5,4},{6,7},{7,6},{8,9},{9,8},{10,11... | collective-permute-start | bytes 4128776 | tf_op jit(solution)/shard_map/ppermute | solution.py:21
  64.8 0.1 shard_map.74.refs_2_.refs_0_
  64.9 0.9 %collective-permute-done.5.refs_1_ = bf16[2320,128]{1,0:T(8,128)(2,1)S(1)} collective-permute-done((bf16[2320,128]{1,0:T(8,128)(2,1)S(1)}, bf16[2320,128]{1,0:T(8,128)(2,1)S(1)}, u32[]{:S(2)}, u32[]{:S(2)}) %collective-permute-start.5) | collective-permute-done | bytes 593952 | tf_op jit(solution)/shard_map/ppermute | solution.py:21
  65.8 0.2 shard_map.75
  66.0 6.0 %collective-permute-done.7.refs_1_ = bf16[384,768]{1,0:T(8,128)(2,1)S(1)} collective-permute-done((bf16[384,768]{1,0:T(8,128)(2,1)S(1)}, bf16[384,768]{1,0:T(8,128)(2,1)S(1)}, u32[]{:S(2)}, u32[]{:S(2)}) %collective-permute-start.7) | collective-permute-done | bytes 589856 | tf_op jit(solution)/shard_map/ppermute | solution.py:21
  72.0 0.1 shard_map.76.refs_2_
  72.2 1.6 %shard_map.77 = (f32[384,768]{1,0:T(8,128)}, f32[384,768]{1,0:T(8,128)}, f32[384]{0:T(512)}) custom-call(f32[384,768]{1,0:T(8,128)S(1)} %get-tuple-element.33.refs_2_.refs_0_, f32[1,384]{1,0:T(1,128)S(1)} %get-tuple-element.34.refs_1_, f32[384,768]{1,0:T(8,128)S(1)} %shard_map.76.refs_2_, f32[384,896]{1,0:T(8,128)S(1)} %collective-permute-done.8.refs_3_), custom_call_target="tpu_custom_call" | custom-call | bytes 6097920 | tf_op jit(solution)/shard_map/pallas_call | solution.py:50
  (13 shorter events, 0.1 us)
Async XLA Ops:
  0.6 25.6 %collective-permute-start.1 = (bf16[384,768]{1,0:T(8,128)(2,1)}, bf16[384,768]{1,0:T(8,128)(2,1)S(1)}, u32[]{:S(2)}, u32[]{:S(2)}) collective-permute-start(bf16[384,768]{1,0:T(8,128)(2,1)} %refs_0_.3), channel_id=1, source_target_pairs={{0,510},{1,3},{2,0},{3,5},{4,2},{5,7},{6,4},{7,9},{8,6},{9,11},{10... | collective-permute-start | bytes 1769480 | tf_op jit(solution)/shard_map/ppermute | solution.py:21
  4.7 1.1 %copy-start = (bf16[384,768]{1,0:T(8,128)(2,1)S(1)}, bf16[384,768]{1,0:T(8,128)(2,1)}, u32[]{:S(2)}) copy-start(bf16[384,768]{1,0:T(8,128)(2,1)} %refs_0_.2) | copy-start | bytes 1769476
  5.7 0.7 copy-start.3
  6.4 14.7 %copy-start.1 = (bf16[384,768]{1,0:T(8,128)(2,1)S(1)}, bf16[384,768]{1,0:T(8,128)(2,1)}, u32[]{:S(2)}) copy-start(bf16[384,768]{1,0:T(8,128)(2,1)} %refs_1_.3) | copy-start | bytes 1769476
  6.4 14.7 %copy-start.2 = (bf16[384,768]{1,0:T(8,128)(2,1)S(1)}, bf16[384,768]{1,0:T(8,128)(2,1)}, u32[]{:S(2)}) copy-start(bf16[384,768]{1,0:T(8,128)(2,1)} %refs_0_.3) | copy-start | bytes 1769476
  6.5 26.4 %collective-permute-start.3 = (bf16[2320,128]{1,0:T(8,128)(2,1)S(1)}, bf16[2320,128]{1,0:T(8,128)(2,1)S(1)}, u32[]{:S(2)}, u32[]{:S(2)}) collective-permute-start(bf16[2320,128]{1,0:T(8,128)(2,1)S(1)} %shard_map.67.refs_3_.refs_1_), channel_id=1, source_target_pairs={{0,2},{1,511},{2,4},{3,1},{4,6},{5,3},{6,8},{7,5},{8,10},{9,7},{10... | collective-permute-start | bytes 1781768 | tf_op jit(solution)/shard_map/ppermute | solution.py:21
  21.4 10.0 %collective-permute-start = (bf16[4624,128]{1,0:T(8,128)(2,1)S(1)}, bf16[4624,128]{1,0:T(8,128)(2,1)S(1)}, u32[]{:S(2)}, u32[]{:S(2)}) collective-permute-start(bf16[4624,128]{1,0:T(8,128)(2,1)S(1)} %get-tuple-element.20.refs_0_), channel_id=1, source_target_pairs={{0,1},{1,0},{2,3},{3,2},{4,5},{5,4},{6,7},{7,6},{8,9},{9,8},{10,11... | collective-permute-start | bytes 3551240 | tf_op jit(solution)/shard_map/ppermute | solution.py:21
  24.3 18.8 %collective-permute-start.4 = (bf16[2320,128]{1,0:T(8,128)(2,1)S(1)}, bf16[2320,128]{1,0:T(8,128)(2,1)S(1)}, u32[]{:S(2)}, u32[]{:S(2)}) collective-permute-start(bf16[2320,128]{1,0:T(8,128)(2,1)S(1)} %get-tuple-element.27), channel_id=1, source_target_pairs={{0,510},{1,3},{2,0},{3,5},{4,2},{5,7},{6,4},{7,9},{8,6},{9,11},{10... | collective-permute-start | bytes 1781768 | tf_op jit(solution)/shard_map/ppermute | solution.py:21
  27.8 15.3 %collective-permute-start.2 = (bf16[2320,128]{1,0:T(8,128)(2,1)S(1)}, bf16[2320,128]{1,0:T(8,128)(2,1)S(1)}, u32[]{:S(2)}, u32[]{:S(2)}) collective-permute-start(bf16[2320,128]{1,0:T(8,128)(2,1)S(1)} %get-tuple-element.21), channel_id=1, source_target_pairs={{0,511},{1,2},{2,1},{3,4},{4,3},{5,6},{6,5},{7,8},{8,7},{9,10},{10... | collective-permute-start | bytes 1781768 | tf_op jit(solution)/shard_map/ppermute | solution.py:21
  35.7 29.1 %collective-permute-start.6 = (bf16[384,768]{1,0:T(8,128)(2,1)S(1)}, bf16[384,768]{1,0:T(8,128)(2,1)S(1)}, u32[]{:S(2)}, u32[]{:S(2)}) collective-permute-start(bf16[384,768]{1,0:T(8,128)(2,1)S(1)} %get-tuple-element.28.refs_3_), channel_id=1, source_target_pairs={{0,510},{1,3},{2,0},{3,5},{4,2},{5,7},{6,4},{7,9},{8,6},{9,11},{10... | collective-permute-start | bytes 1769480 | tf_op jit(solution)/shard_map/ppermute | solution.py:21
  44.7 21.1 %collective-permute-start.5 = (bf16[2320,128]{1,0:T(8,128)(2,1)S(1)}, bf16[2320,128]{1,0:T(8,128)(2,1)S(1)}, u32[]{:S(2)}, u32[]{:S(2)}) collective-permute-start(bf16[2320,128]{1,0:T(8,128)(2,1)S(1)} %get-tuple-element.31), channel_id=1, source_target_pairs={{0,2},{1,511},{2,4},{3,1},{4,6},{5,3},{6,8},{7,5},{8,10},{9,7},{10... | collective-permute-start | bytes 1781768 | tf_op jit(solution)/shard_map/ppermute | solution.py:21
  60.5 11.5 %collective-permute-start.7 = (bf16[384,768]{1,0:T(8,128)(2,1)S(1)}, bf16[384,768]{1,0:T(8,128)(2,1)S(1)}, u32[]{:S(2)}, u32[]{:S(2)}) collective-permute-start(bf16[384,768]{1,0:T(8,128)(2,1)S(1)} %get-tuple-element.35), channel_id=1, source_target_pairs={{0,511},{1,2},{2,1},{3,4},{4,3},{5,6},{6,5},{7,8},{8,7},{9,10},{10... | collective-permute-start | bytes 1769480 | tf_op jit(solution)/shard_map/ppermute | solution.py:21
  62.5 9.7 %collective-permute-start.8 = (f32[384,896]{1,0:T(8,128)S(1)}, f32[384,896]{1,0:T(8,128)S(1)}, u32[]{:S(2)}, u32[]{:S(2)}) collective-permute-start(f32[384,896]{1,0:T(8,128)S(1)} %get-tuple-element.36), channel_id=1, source_target_pairs={{0,1},{1,0},{2,3},{3,2},{4,5},{5,4},{6,7},{7,6},{8,9},{9,8},{10,11... | collective-permute-start | bytes 4128776 | tf_op jit(solution)/shard_map/ppermute | solution.py:21

commit v10 on v9

--- a/solution.py
+++ b/solution.py
@@ -107,7 +107,8 @@
     out_ref[out_ref.shape[0] - EXTRA :, :] = digits(species_ref[...])
 
 
-def pack_images(student_ref, teacher_ref, species_ref, out_ref, teacher_out):
+def pack_images(student_ref, teacher_ref, species_ref, text_ref, out_ref, teacher_out, text_out):
+    text_out[...] = text_ref[...]
     rows, width = student_ref.shape
     ids = digits(species_ref[...])
     put(out_ref, 0, student_ref[...])
@@ -174,8 +175,7 @@
     return text_term(slope, jnp.concatenate([student for student, _, _ in images], axis=0))
 
 
-def own_first(own_ref, text_ref, sums_ref, term_ref, text_out):
-    text_out[...] = text_ref[...]
+def own_first(own_ref, text_ref, sums_ref, term_ref):
     rows, width = term_ref.shape
     images = both_images(own_ref, rows)
     sums_ref[:, :width], sums_ref[:, width:], term_ref[...] = block(images, unpacked(text_ref, rows))
@@ -254,26 +254,21 @@
     ahead_student = back(student_image_vectors)
     (text,) = call(pack_text, [packed], 0, text_emb, species)
     second = onward(text)
-    images, teacher = call(
+    images, teacher, text_again = call(
         pack_images,
-        [spec(2 * rows * width // LANES + EXTRA, LANES, BF16), packed],
+        [spec(2 * rows * width // LANES + EXTRA, LANES, BF16), packed, packed],
         0,
         student_image_vectors,
         teacher_emb,
         species,
-        after=(text,),
-    )
+        text,
+    )
+    near = across(text_again)
     other = within(images)
     ahead_teacher = back(teacher)
-    own_sum, own_term, text_again = call(
-        own_first,
-        [sums, term, packed],
-        64 * dot,
-        images,
-        text,
-        after=(ahead_student,),
-    )
-    near = across(text_again)
+    own_sum, own_term = call(
+        own_first, [sums, term], 64 * dot, images, text, after=(ahead_student,)
+    )
     other_sum, own_term = call(other_first, [sums, term], 16 * dot, other, text, own_term)
     own_sum, other_sum, second_term = call(
         both, [sums, sums, sent], 16 * dot, images, other, second, own_sum, other_sum

time: 74.2 us -> 70.4 us (0.949)
  starting transfers between devices: 46.3 us -> 33 us
  waiting for transfers between devices: 12.4 us -> 22 us
    ppermute x9, starting transfers between devices: 46.3 us -> 33 us  [moved(): lax.ppermute(value, 'dp', [(i, (i + (odd if i % 2 else even)) % length) f...]
    ppermute x9, waiting for transfers between devices: 12.4 us -> 22 us  [moved(): lax.ppermute(value, 'dp', [(i, (i + (odd if i % 2 else even)) % length) f...]
  transfers between devices with their start and end apart: 9 -> 9, of which waited for: 3 -> 4; matrix products, arithmetic and copies ran while one was open for 0% -> 0% of each run, Pallas kernels for 15% -> 16%
where the time goes in v10:
time: 70.4 us; the launch traced here: 70 us
  starting transfers between devices  33 us (47%)
  waiting for transfers between devices  22 us (31%)
  Pallas kernels  12.4 us (18%)
  local copies, waits for them, and re-layouts  1.75 us (2%)
  between operations  0.82 us (1%)
    ppermute x9, starting transfers between devices, moved(): lax.ppermute(value, 'dp', [(i, (i + (odd if i % 2 else even)) % length) f...  33 us
    ppermute x9, waiting for transfers between devices, moved(): lax.ppermute(value, 'dp', [(i, (i + (odd if i % 2 else even)) % length) f...  22 us
    pallas_call x11, Pallas kernels, call(): pl.pallas_call(ordered, out_shape=out_shape, in_specs=[pl.BlockSpec(memor...  12.4 us
    unnamed x8, local copies, waits for them, and re-layouts  1.75 us
  transfers between devices with their start and end apart: 9, of which 4 were waited for; matrix products, arithmetic and copies ran while one was open for 0% of the time, Pallas kernels for 16%

profile of v10, /device:TPU:1, one launch (start us, length us, event | category | flops | bytes accessed | tf_op | source)
XLA Modules:
  0.0 70.0 jit_solution(12201043584414013756)
XLA Ops:
  0.6 4.0 %collective-permute-start.3 = (bf16[384,768]{1,0:T(8,128)(2,1)}, bf16[384,768]{1,0:T(8,128)(2,1)S(1)}, u32[]{:S(2)}, u32[]{:S(2)}) collective-permute-start(bf16[384,768]{1,0:T(8,128)(2,1)} %refs_0_.3), channel_id=1, source_target_pairs={{0,510},{1,3},{2,0},{3,5},{4,2},{5,7},{6,4},{7,9},{8,6},{9,11},{10... | collective-permute-start | bytes 1769480 | tf_op jit(solution)/shard_map/ppermute | solution.py:21
  4.7 1.1 %copy-done = bf16[384,768]{1,0:T(8,128)(2,1)S(1)} copy-done((bf16[384,768]{1,0:T(8,128)(2,1)S(1)}, bf16[384,768]{1,0:T(8,128)(2,1)}, u32[]{:S(2)}) %copy-start) | copy-done | bytes 589848
  5.7 0.7 copy-done.3
  6.5 14.6 %collective-permute-start.2 = (bf16[2320,128]{1,0:T(8,128)(2,1)S(1)}, bf16[2320,128]{1,0:T(8,128)(2,1)S(1)}, u32[]{:S(2)}, u32[]{:S(2)}) collective-permute-start(bf16[2320,128]{1,0:T(8,128)(2,1)S(1)} %shard_map.67.refs_3_.refs_1_), channel_id=1, source_target_pairs={{0,2},{1,511},{2,4},{3,1},{4,6},{5,3},{6,8},{7,5},{8,10},{9,7},{10... | collective-permute-start | bytes 1781768 | tf_op jit(solution)/shard_map/ppermute | solution.py:21
  21.2 0.3 shard_map.68
  21.4 2.9 %collective-permute-start = (bf16[4624,128]{1,0:T(8,128)(2,1)S(1)}, bf16[4624,128]{1,0:T(8,128)(2,1)S(1)}, u32[]{:S(2)}, u32[]{:S(2)}) collective-permute-start(bf16[4624,128]{1,0:T(8,128)(2,1)S(1)} %get-tuple-element.20.refs_0_), channel_id=1, source_target_pairs={{0,1},{1,0},{2,3},{3,2},{4,5},{5,4},{6,7},{7,6},{8,9},{9,8},{10,11... | collective-permute-start | bytes 3551240 | tf_op jit(solution)/shard_map/ppermute | solution.py:21
  24.3 1.9 %collective-permute-start.1 = (bf16[2320,128]{1,0:T(8,128)(2,1)S(1)}, bf16[2320,128]{1,0:T(8,128)(2,1)S(1)}, u32[]{:S(2)}, u32[]{:S(2)}) collective-permute-start(bf16[2320,128]{1,0:T(8,128)(2,1)S(1)} %get-tuple-element.21), channel_id=1, source_target_pairs={{0,511},{1,2},{2,1},{3,4},{4,3},{5,6},{6,5},{7,8},{8,7},{9,10},{10... | collective-permute-start | bytes 1781768 | tf_op jit(solution)/shard_map/ppermute | solution.py:21
  26.2 1.9 %collective-permute-start.4 = (bf16[2320,128]{1,0:T(8,128)(2,1)S(1)}, bf16[2320,128]{1,0:T(8,128)(2,1)S(1)}, u32[]{:S(2)}, u32[]{:S(2)}) collective-permute-start(bf16[2320,128]{1,0:T(8,128)(2,1)S(1)} %get-tuple-element.27), channel_id=1, source_target_pairs={{0,510},{1,3},{2,0},{3,5},{4,2},{5,7},{6,4},{7,9},{8,6},{9,11},{10... | collective-permute-start | bytes 1781768 | tf_op jit(solution)/shard_map/ppermute | solution.py:21
  28.2 1.6 %shard_map.69 = (f32[384,896]{1,0:T(8,128)S(1)}, f32[384,768]{1,0:T(8,128)S(1)}) custom-call(bf16[4624,128]{1,0:T(8,128)(2,1)S(1)} %get-tuple-element.20.refs_0_, bf16[2320,128]{1,0:T(8,128)(2,1)S(1)} %shard_map.67.refs_3_.refs_1_, bf16[384,768]{1,0:T(8,128)(2,1)S(1)} %collective-permute-done.3.refs_2_.refs_0_), custom_call_target="tpu_custom_call" | custom-call | flops 14495514624 | bytes 4333568 | tf_op jit(solution)/shard_map/pallas_call | solution.py:50
  29.8 1.6 %shard_map.70 = (f32[384,896]{1,0:T(8,128)S(1)}, f32[384,768]{1,0:T(8,128)S(1)}) custom-call(bf16[4624,128]{1,0:T(8,128)(2,1)S(1)} %collective-permute-done.refs_0_.refs_1_, bf16[2320,128]{1,0:T(8,128)(2,1)S(1)} %shard_map.67.refs_3_.refs_1_, f32[384,768]{1,0:T(8,128)S(1)} %get-tuple-element.23.refs_2_), custom_call_target="tpu_custom_call" | custom-call | flops 3623878656 | bytes 5513216 | tf_op jit(solution)/shard_map/pallas_call | solution.py:50
  31.3 0.4 collective-permute-done.2.refs_2_
  31.8 2.7 %shard_map.71 = (f32[384,896]{1,0:T(8,128)S(1)}, f32[384,896]{1,0:T(8,128)S(1)}, bf16[384,768]{1,0:T(8,128)(2,1)S(1)}) custom-call(bf16[4624,128]{1,0:T(8,128)(2,1)S(1)} %get-tuple-element.20.refs_0_, bf16[4624,128]{1,0:T(8,128)(2,1)S(1)} %collective-permute-done.refs_0_.refs_1_, bf16[2320,128]{1,0:T(8,128)(2,1)S(1)} %collective-permute-done.2.refs_2_, ...), custom_call_target="tpu_custom_call" | custom-call | flops 3623878656 | bytes 9056256 | tf_op jit(solution)/shard_map/pallas_call | solution.py:50
  34.5 1.9 %collective-permute-start.6 = (bf16[384,768]{1,0:T(8,128)(2,1)S(1)}, bf16[384,768]{1,0:T(8,128)(2,1)S(1)}, u32[]{:S(2)}, u32[]{:S(2)}) collective-permute-start(bf16[384,768]{1,0:T(8,128)(2,1)S(1)} %get-tuple-element.28.refs_3_), channel_id=1, source_target_pairs={{0,510},{1,3},{2,0},{3,5},{4,2},{5,7},{6,4},{7,9},{8,6},{9,11},{10... | collective-permute-start | bytes 1769480 | tf_op jit(solution)/shard_map/ppermute | solution.py:21
  36.4 13.1 %collective-permute-done.4.refs_1_ = bf16[2320,128]{1,0:T(8,128)(2,1)S(1)} collective-permute-done((bf16[2320,128]{1,0:T(8,128)(2,1)S(1)}, bf16[2320,128]{1,0:T(8,128)(2,1)S(1)}, u32[]{:S(2)}, u32[]{:S(2)}) %collective-permute-start.4) | collective-permute-done | bytes 593952 | tf_op jit(solution)/shard_map/ppermute | solution.py:21
  49.4 1.6 %shard_map.72 = (bf16[2320,128]{1,0:T(8,128)(2,1)S(1)}, f32[384,768]{1,0:T(8,128)S(1)}) custom-call(bf16[384,768]{1,0:T(8,128)(2,1)S(1)} %collective-permute-done.3.refs_2_.refs_0_, bf16[2320,128]{1,0:T(8,128)(2,1)S(1)} %collective-permute-done.4.refs_1_, bf16[2320,128]{1,0:T(8,128)(2,1)S(1)} %collective-permute-done.1.refs_2_, ...), custom_call_target="tpu_custom_call" | custom-call | flops 905969664 | bytes 3551232 | tf_op jit(solution)/shard_map/pallas_call | solution.py:50
  51.0 1.9 %collective-permute-start.5 = (bf16[2320,128]{1,0:T(8,128)(2,1)S(1)}, bf16[2320,128]{1,0:T(8,128)(2,1)S(1)}, u32[]{:S(2)}, u32[]{:S(2)}) collective-permute-start(bf16[2320,128]{1,0:T(8,128)(2,1)S(1)} %get-tuple-element.31), channel_id=1, source_target_pairs={{0,2},{1,511},{2,4},{3,1},{4,6},{5,3},{6,8},{7,5},{8,10},{9,7},{10... | collective-permute-start | bytes 1781768 | tf_op jit(solution)/shard_map/ppermute | solution.py:21
  52.9 2.7 %shard_map.73 = (f32[384,896]{1,0:T(8,128)S(1)}, f32[384,896]{1,0:T(8,128)S(1)}, bf16[384,768]{1,0:T(8,128)(2,1)S(1)}) custom-call(bf16[4624,128]{1,0:T(8,128)(2,1)S(1)} %get-tuple-element.20.refs_0_, bf16[4624,128]{1,0:T(8,128)(2,1)S(1)} %collective-permute-done.refs_0_.refs_1_, bf16[2320,128]{1,0:T(8,128)(2,1)S(1)} %collective-permute-done.1.refs_2_, ...), custom_call_target="tpu_custom_call" | custom-call | bytes 10235904 | tf_op jit(solution)/shard_map/pallas_call | solution.py:50
  55.6 1.9 %collective-permute-start.7 = (bf16[384,768]{1,0:T(8,128)(2,1)S(1)}, bf16[384,768]{1,0:T(8,128)(2,1)S(1)}, u32[]{:S(2)}, u32[]{:S(2)}) collective-permute-start(bf16[384,768]{1,0:T(8,128)(2,1)S(1)} %get-tuple-element.35), channel_id=1, source_target_pairs={{0,511},{1,2},{2,1},{3,4},{4,3},{5,6},{6,5},{7,8},{8,7},{9,10},{10... | collective-permute-start | bytes 1769480 | tf_op jit(solution)/shard_map/ppermute | solution.py:21
  57.6 1.9 %collective-permute-start.8 = (f32[384,896]{1,0:T(8,128)S(1)}, f32[384,896]{1,0:T(8,128)S(1)}, u32[]{:S(2)}, u32[]{:S(2)}) collective-permute-start(f32[384,896]{1,0:T(8,128)S(1)} %get-tuple-element.36), channel_id=1, source_target_pairs={{0,1},{1,0},{2,3},{3,2},{4,5},{5,4},{6,7},{7,6},{8,9},{9,8},{10,11... | collective-permute-start | bytes 4128776 | tf_op jit(solution)/shard_map/ppermute | solution.py:21
  59.6 3.5 %collective-permute-done.5.refs_1_ = bf16[2320,128]{1,0:T(8,128)(2,1)S(1)} collective-permute-done((bf16[2320,128]{1,0:T(8,128)(2,1)S(1)}, bf16[2320,128]{1,0:T(8,128)(2,1)S(1)}, u32[]{:S(2)}, u32[]{:S(2)}) %collective-permute-start.5) | collective-permute-done | bytes 593952 | tf_op jit(solution)/shard_map/ppermute | solution.py:21
  63.1 0.2 shard_map.75
  63.3 5.0 %collective-permute-done.7.refs_1_ = bf16[384,768]{1,0:T(8,128)(2,1)S(1)} collective-permute-done((bf16[384,768]{1,0:T(8,128)(2,1)S(1)}, bf16[384,768]{1,0:T(8,128)(2,1)S(1)}, u32[]{:S(2)}, u32[]{:S(2)}) %collective-permute-start.7) | collective-permute-done | bytes 589856 | tf_op jit(solution)/shard_map/ppermute | solution.py:21
  68.3 0.1 shard_map.76.refs_2_
  68.4 1.6 %shard_map.77 = (f32[384,768]{1,0:T(8,128)}, f32[384,768]{1,0:T(8,128)}, f32[384]{0:T(512)}) custom-call(f32[384,768]{1,0:T(8,128)S(1)} %get-tuple-element.33.refs_2_.refs_0_, f32[1,384]{1,0:T(1,128)S(1)} %get-tuple-element.34.refs_1_, f32[384,768]{1,0:T(8,128)S(1)} %shard_map.76.refs_2_, f32[384,896]{1,0:T(8,128)S(1)} %collective-permute-done.8.refs_3_), custom_call_target="tpu_custom_call" | custom-call | bytes 6097920 | tf_op jit(solution)/shard_map/pallas_call | solution.py:50
  (13 shorter events, 0.2 us)
Async XLA Ops:
  0.6 27.5 %collective-permute-start.3 = (bf16[384,768]{1,0:T(8,128)(2,1)}, bf16[384,768]{1,0:T(8,128)(2,1)S(1)}, u32[]{:S(2)}, u32[]{:S(2)}) collective-permute-start(bf16[384,768]{1,0:T(8,128)(2,1)} %refs_0_.3), channel_id=1, source_target_pairs={{0,510},{1,3},{2,0},{3,5},{4,2},{5,7},{6,4},{7,9},{8,6},{9,11},{10... | collective-permute-start | bytes 1769480 | tf_op jit(solution)/shard_map/ppermute | solution.py:21
  4.7 1.1 %copy-start = (bf16[384,768]{1,0:T(8,128)(2,1)S(1)}, bf16[384,768]{1,0:T(8,128)(2,1)}, u32[]{:S(2)}) copy-start(bf16[384,768]{1,0:T(8,128)(2,1)} %refs_0_.2) | copy-start | bytes 1769476
  5.7 0.7 copy-start.3
  6.4 14.7 %copy-start.1 = (bf16[384,768]{1,0:T(8,128)(2,1)S(1)}, bf16[384,768]{1,0:T(8,128)(2,1)}, u32[]{:S(2)}) copy-start(bf16[384,768]{1,0:T(8,128)(2,1)} %refs_1_.3) | copy-start | bytes 1769476
  6.4 14.7 %copy-start.2 = (bf16[384,768]{1,0:T(8,128)(2,1)S(1)}, bf16[384,768]{1,0:T(8,128)(2,1)}, u32[]{:S(2)}) copy-start(bf16[384,768]{1,0:T(8,128)(2,1)} %refs_0_.3) | copy-start | bytes 1769476
  6.5 25.2 %collective-permute-start.2 = (bf16[2320,128]{1,0:T(8,128)(2,1)S(1)}, bf16[2320,128]{1,0:T(8,128)(2,1)S(1)}, u32[]{:S(2)}, u32[]{:S(2)}) collective-permute-start(bf16[2320,128]{1,0:T(8,128)(2,1)S(1)} %shard_map.67.refs_3_.refs_1_), channel_id=1, source_target_pairs={{0,2},{1,511},{2,4},{3,1},{4,6},{5,3},{6,8},{7,5},{8,10},{9,7},{10... | collective-permute-start | bytes 1781768 | tf_op jit(solution)/shard_map/ppermute | solution.py:21
  21.4 8.3 %collective-permute-start = (bf16[4624,128]{1,0:T(8,128)(2,1)S(1)}, bf16[4624,128]{1,0:T(8,128)(2,1)S(1)}, u32[]{:S(2)}, u32[]{:S(2)}) collective-permute-start(bf16[4624,128]{1,0:T(8,128)(2,1)S(1)} %get-tuple-element.20.refs_0_), channel_id=1, source_target_pairs={{0,1},{1,0},{2,3},{3,2},{4,5},{5,4},{6,7},{7,6},{8,9},{9,8},{10,11... | collective-permute-start | bytes 3551240 | tf_op jit(solution)/shard_map/ppermute | solution.py:21
  24.3 12.1 %collective-permute-start.1 = (bf16[2320,128]{1,0:T(8,128)(2,1)S(1)}, bf16[2320,128]{1,0:T(8,128)(2,1)S(1)}, u32[]{:S(2)}, u32[]{:S(2)}) collective-permute-start(bf16[2320,128]{1,0:T(8,128)(2,1)S(1)} %get-tuple-element.21), channel_id=1, source_target_pairs={{0,511},{1,2},{2,1},{3,4},{4,3},{5,6},{6,5},{7,8},{8,7},{9,10},{10... | collective-permute-start | bytes 1781768 | tf_op jit(solution)/shard_map/ppermute | solution.py:21
  26.2 23.2 %collective-permute-start.4 = (bf16[2320,128]{1,0:T(8,128)(2,1)S(1)}, bf16[2320,128]{1,0:T(8,128)(2,1)S(1)}, u32[]{:S(2)}, u32[]{:S(2)}) collective-permute-start(bf16[2320,128]{1,0:T(8,128)(2,1)S(1)} %get-tuple-element.27), channel_id=1, source_target_pairs={{0,510},{1,3},{2,0},{3,5},{4,2},{5,7},{6,4},{7,9},{8,6},{9,11},{10... | collective-permute-start | bytes 1781768 | tf_op jit(solution)/shard_map/ppermute | solution.py:21
  34.5 25.0 %collective-permute-start.6 = (bf16[384,768]{1,0:T(8,128)(2,1)S(1)}, bf16[384,768]{1,0:T(8,128)(2,1)S(1)}, u32[]{:S(2)}, u32[]{:S(2)}) collective-permute-start(bf16[384,768]{1,0:T(8,128)(2,1)S(1)} %get-tuple-element.28.refs_3_), channel_id=1, source_target_pairs={{0,510},{1,3},{2,0},{3,5},{4,2},{5,7},{6,4},{7,9},{8,6},{9,11},{10... | collective-permute-start | bytes 1769480 | tf_op jit(solution)/shard_map/ppermute | solution.py:21
  51.0 12.1 %collective-permute-start.5 = (bf16[2320,128]{1,0:T(8,128)(2,1)S(1)}, bf16[2320,128]{1,0:T(8,128)(2,1)S(1)}, u32[]{:S(2)}, u32[]{:S(2)}) collective-permute-start(bf16[2320,128]{1,0:T(8,128)(2,1)S(1)} %get-tuple-element.31), channel_id=1, source_target_pairs={{0,2},{1,511},{2,4},{3,1},{4,6},{5,3},{6,8},{7,5},{8,10},{9,7},{10... | collective-permute-start | bytes 1781768 | tf_op jit(solution)/shard_map/ppermute | solution.py:21
  55.6 12.7 %collective-permute-start.7 = (bf16[384,768]{1,0:T(8,128)(2,1)S(1)}, bf16[384,768]{1,0:T(8,128)(2,1)S(1)}, u32[]{:S(2)}, u32[]{:S(2)}) collective-permute-start(bf16[384,768]{1,0:T(8,128)(2,1)S(1)} %get-tuple-element.35), channel_id=1, source_target_pairs={{0,511},{1,2},{2,1},{3,4},{4,3},{5,6},{6,5},{7,8},{8,7},{9,10},{10... | collective-permute-start | bytes 1769480 | tf_op jit(solution)/shard_map/ppermute | solution.py:21
  57.6 10.9 %collective-permute-start.8 = (f32[384,896]{1,0:T(8,128)S(1)}, f32[384,896]{1,0:T(8,128)S(1)}, u32[]{:S(2)}, u32[]{:S(2)}) collective-permute-start(f32[384,896]{1,0:T(8,128)S(1)} %get-tuple-element.36), channel_id=1, source_target_pairs={{0,1},{1,0},{2,3},{3,2},{4,5},{5,4},{6,7},{7,6},{8,9},{9,8},{10,11... | collective-permute-start | bytes 4128776 | tf_op jit(solution)/shard_map/ppermute | solution.py:21

commit v11 on v10

--- a/solution.py
+++ b/solution.py
@@ -196,24 +196,15 @@
     term_ref[...] = term.astype(term_ref.dtype)
 
 
-def both_near(
-    own_ref, other_ref, text_ref, own_in, other_in, term_in, own_out, other_out, term_ref
-):
-    rows = term_ref.shape[0]
-    images = [both_images(ref, rows) for ref in (own_ref, other_ref)]
-    sums_in, sums_out = (own_in, other_in), (own_out, other_out)
-    term = two_blocks(images, unpacked(text_ref, rows), sums_in, sums_out)
-    term_ref[...] = (term_in[...] + term).astype(term_ref.dtype)
-
-
 def loss_row(folded):
     return jnp.sum(jnp.transpose(folded), axis=0, keepdims=True)
 
 
-def ahead_near(student_ref, teacher_ref, near_ref, ahead_out, term_ref):
+def ahead_near(student_ref, teacher_ref, near_ref, term_in, ahead_out, term_ref):
     rows = term_ref.shape[0]
     images = (student_ref[...], *unpacked(teacher_ref, rows))
-    grad, folded, term_ref[...] = block(images, unpacked(near_ref, rows))
+    grad, folded, term = block(images, unpacked(near_ref, rows))
+    term_ref[...] = (term_in[...] + term).astype(term_ref.dtype)
     put(ahead_out, 0, grad.astype(BF16))
     loss = loss_row(folded)
     high = loss.astype(BF16).astype(F32)
@@ -274,27 +265,13 @@
         both, [sums, sums, sent], 16 * dot, images, other, second, own_sum, other_sum
     )
     second_back = back(second_term)
-    ahead_sum, far_term = call(
-        ahead_near,
-        [packed, term],
-        4 * dot,
-        ahead_student,
-        ahead_teacher,
-        near,
-        after=(second_term,),
+    own_sum, other_sum, near_term = call(
+        both, [sums, sums, term], 0 * dot, images, other, near, own_sum, other_sum
+    )
+    ahead_sum, near_term = call(
+        ahead_near, [packed, sent], 0 * dot, ahead_student, ahead_teacher, near, near_term
     )
     ahead_back = onward(ahead_sum)
-    own_sum, other_sum, near_term = call(
-        both_near,
-        [sums, sums, sent],
-        0 * dot,
-        images,
-        other,
-        near,
-        own_sum,
-        other_sum,
-        far_term,
-    )
     near_back = across(near_term)
     other_back = within(other_sum)
     (own_term,) = call(gather_text, [term], 128 * dot, own_term, second_back)

time: 70.4 us -> 70.4 us (level)
  waiting for transfers between devices: 22 us -> 20.2 us
  starting transfers between devices: 33 us -> 34.8 us
    ppermute x9, starting transfers between devices: 33 us -> 34.8 us  [moved(): lax.ppermute(value, 'dp', [(i, (i + (odd if i % 2 else even)) % length) f...]
    ppermute x9, waiting for transfers between devices: 22 us -> 20.2 us  [moved(): lax.ppermute(value, 'dp', [(i, (i + (odd if i % 2 else even)) % length) f...]
  transfers between devices with their start and end apart: 9 -> 9, of which waited for: 4 -> 4; matrix products, arithmetic and copies ran while one was open for 0% -> 0% of each run, Pallas kernels for 16% -> 15%
where the time goes in v11:
time: 70.4 us; the launch traced here: 70 us
  starting transfers between devices  34.8 us (49%)
  waiting for transfers between devices  20.2 us (29%)
  Pallas kernels  12.4 us (18%)
  local copies, waits for them, and re-layouts  1.75 us (2%)
  between operations  0.82 us (1%)
    ppermute x9, starting transfers between devices, moved(): lax.ppermute(value, 'dp', [(i, (i + (odd if i % 2 else even)) % length) f...  34.8 us
    ppermute x9, waiting for transfers between devices, moved(): lax.ppermute(value, 'dp', [(i, (i + (odd if i % 2 else even)) % length) f...  20.2 us
    pallas_call x11, Pallas kernels, call(): pl.pallas_call(ordered, out_shape=out_shape, in_specs=[pl.BlockSpec(memor...  12.4 us
    unnamed x8, local copies, waits for them, and re-layouts  1.75 us
  transfers between devices with their start and end apart: 9, of which 4 were waited for; matrix products, arithmetic and copies ran while one was open for 0% of the time, Pallas kernels for 15%

profile of v11, /device:TPU:1, one launch (start us, length us, event | category | flops | bytes accessed | tf_op | source)
XLA Modules:
  0.0 70.0 jit_solution(11504872567141634668)
XLA Ops:
  0.6 4.0 %collective-permute-start.3 = (bf16[384,768]{1,0:T(8,128)(2,1)}, bf16[384,768]{1,0:T(8,128)(2,1)S(1)}, u32[]{:S(2)}, u32[]{:S(2)}) collective-permute-start(bf16[384,768]{1,0:T(8,128)(2,1)} %refs_0_.3), channel_id=1, source_target_pairs={{0,510},{1,3},{2,0},{3,5},{4,2},{5,7},{6,4},{7,9},{8,6},{9,11},{10... | collective-permute-start | bytes 1769480 | tf_op jit(solution)/shard_map/ppermute | solution.py:21
  4.7 1.1 %copy-done = bf16[384,768]{1,0:T(8,128)(2,1)S(1)} copy-done((bf16[384,768]{1,0:T(8,128)(2,1)S(1)}, bf16[384,768]{1,0:T(8,128)(2,1)}, u32[]{:S(2)}) %copy-start) | copy-done | bytes 589848
  5.7 0.7 copy-done.3
  6.5 14.6 %collective-permute-start.2 = (bf16[2320,128]{1,0:T(8,128)(2,1)S(1)}, bf16[2320,128]{1,0:T(8,128)(2,1)S(1)}, u32[]{:S(2)}, u32[]{:S(2)}) collective-permute-start(bf16[2320,128]{1,0:T(8,128)(2,1)S(1)} %shard_map.67.refs_3_.refs_1_), channel_id=1, source_target_pairs={{0,2},{1,511},{2,4},{3,1},{4,6},{5,3},{6,8},{7,5},{8,10},{9,7},{10... | collective-permute-start | bytes 1781768 | tf_op jit(solution)/shard_map/ppermute | solution.py:21
  21.2 0.3 shard_map.68
  21.4 2.9 %collective-permute-start = (bf16[4624,128]{1,0:T(8,128)(2,1)S(1)}, bf16[4624,128]{1,0:T(8,128)(2,1)S(1)}, u32[]{:S(2)}, u32[]{:S(2)}) collective-permute-start(bf16[4624,128]{1,0:T(8,128)(2,1)S(1)} %get-tuple-element.20.refs_0_), channel_id=1, source_target_pairs={{0,1},{1,0},{2,3},{3,2},{4,5},{5,4},{6,7},{7,6},{8,9},{9,8},{10,11... | collective-permute-start | bytes 3551240 | tf_op jit(solution)/shard_map/ppermute | solution.py:21
  24.3 1.9 %collective-permute-start.1 = (bf16[2320,128]{1,0:T(8,128)(2,1)S(1)}, bf16[2320,128]{1,0:T(8,128)(2,1)S(1)}, u32[]{:S(2)}, u32[]{:S(2)}) collective-permute-start(bf16[2320,128]{1,0:T(8,128)(2,1)S(1)} %get-tuple-element.21), channel_id=1, source_target_pairs={{0,511},{1,2},{2,1},{3,4},{4,3},{5,6},{6,5},{7,8},{8,7},{9,10},{10... | collective-permute-start | bytes 1781768 | tf_op jit(solution)/shard_map/ppermute | solution.py:21
  26.2 1.9 %collective-permute-start.4 = (bf16[2320,128]{1,0:T(8,128)(2,1)S(1)}, bf16[2320,128]{1,0:T(8,128)(2,1)S(1)}, u32[]{:S(2)}, u32[]{:S(2)}) collective-permute-start(bf16[2320,128]{1,0:T(8,128)(2,1)S(1)} %get-tuple-element.28), channel_id=1, source_target_pairs={{0,510},{1,3},{2,0},{3,5},{4,2},{5,7},{6,4},{7,9},{8,6},{9,11},{10... | collective-permute-start | bytes 1781768 | tf_op jit(solution)/shard_map/ppermute | solution.py:21
  28.2 1.6 %shard_map.69 = (f32[384,896]{1,0:T(8,128)S(1)}, f32[384,768]{1,0:T(8,128)S(1)}) custom-call(bf16[4624,128]{1,0:T(8,128)(2,1)S(1)} %get-tuple-element.20.refs_0_, bf16[2320,128]{1,0:T(8,128)(2,1)S(1)} %shard_map.67.refs_3_.refs_1_, bf16[384,768]{1,0:T(8,128)(2,1)S(1)} %collective-permute-done.3.refs_2_.refs_0_), custom_call_target="tpu_custom_call" | custom-call | flops 14495514624 | bytes 4333568 | tf_op jit(solution)/shard_map/pallas_call | solution.py:50
  29.8 1.6 %shard_map.70 = (f32[384,896]{1,0:T(8,128)S(1)}, f32[384,768]{1,0:T(8,128)S(1)}) custom-call(bf16[4624,128]{1,0:T(8,128)(2,1)S(1)} %collective-permute-done.refs_0_.refs_1_, bf16[2320,128]{1,0:T(8,128)(2,1)S(1)} %shard_map.67.refs_3_.refs_1_, f32[384,768]{1,0:T(8,128)S(1)} %get-tuple-element.23.refs_2_), custom_call_target="tpu_custom_call" | custom-call | flops 3623878656 | bytes 5513216 | tf_op jit(solution)/shard_map/pallas_call | solution.py:50
  31.3 0.4 collective-permute-done.2.refs_2_
  31.8 2.7 %shard_map.71 = (f32[384,896]{1,0:T(8,128)S(1)}, f32[384,896]{1,0:T(8,128)S(1)}, bf16[384,768]{1,0:T(8,128)(2,1)S(1)}) custom-call(bf16[4624,128]{1,0:T(8,128)(2,1)S(1)} %get-tuple-element.20.refs_0_, bf16[4624,128]{1,0:T(8,128)(2,1)S(1)} %collective-permute-done.refs_0_.refs_1_, bf16[2320,128]{1,0:T(8,128)(2,1)S(1)} %collective-permute-done.2.refs_2_, ...), custom_call_target="tpu_custom_call" | custom-call | flops 3623878656 | bytes 9056256 | tf_op jit(solution)/shard_map/pallas_call | solution.py:50
  34.4 1.9 %collective-permute-start.6 = (bf16[384,768]{1,0:T(8,128)(2,1)S(1)}, bf16[384,768]{1,0:T(8,128)(2,1)S(1)}, u32[]{:S(2)}, u32[]{:S(2)}) collective-permute-start(bf16[384,768]{1,0:T(8,128)(2,1)S(1)} %get-tuple-element.32), channel_id=1, source_target_pairs={{0,510},{1,3},{2,0},{3,5},{4,2},{5,7},{6,4},{7,9},{8,6},{9,11},{10... | collective-permute-start | bytes 1769480 | tf_op jit(solution)/shard_map/ppermute | solution.py:21
  36.4 2.7 %shard_map.72 = (f32[384,896]{1,0:T(8,128)S(1)}, f32[384,896]{1,0:T(8,128)S(1)}, f32[384,768]{1,0:T(8,128)S(1)}) custom-call(bf16[4624,128]{1,0:T(8,128)(2,1)S(1)} %get-tuple-element.20.refs_0_, bf16[4624,128]{1,0:T(8,128)(2,1)S(1)} %collective-permute-done.refs_0_.refs_1_, bf16[2320,128]{1,0:T(8,128)(2,1)S(1)} %collective-permute-done.1.refs_2_, ...), custom_call_target="tpu_custom_call" | custom-call | bytes 9646080 | tf_op jit(solution)/shard_map/pallas_call | solution.py:50
  39.1 10.4 %collective-permute-done.4.refs_1_ = bf16[2320,128]{1,0:T(8,128)(2,1)S(1)} collective-permute-done((bf16[2320,128]{1,0:T(8,128)(2,1)S(1)}, bf16[2320,128]{1,0:T(8,128)(2,1)S(1)}, u32[]{:S(2)}, u32[]{:S(2)}) %collective-permute-start.4) | collective-permute-done | bytes 593952 | tf_op jit(solution)/shard_map/ppermute | solution.py:21
  49.4 1.6 %shard_map.73 = (bf16[2320,128]{1,0:T(8,128)(2,1)S(1)}, bf16[384,768]{1,0:T(8,128)(2,1)S(1)}) custom-call(bf16[384,768]{1,0:T(8,128)(2,1)S(1)} %collective-permute-done.3.refs_2_.refs_0_, bf16[2320,128]{1,0:T(8,128)(2,1)S(1)} %collective-permute-done.4.refs_1_, bf16[2320,128]{1,0:T(8,128)(2,1)S(1)} %collective-permute-done.1.refs_2_, ...), custom_call_target="tpu_custom_call" | custom-call | bytes 4141056 | tf_op jit(solution)/shard_map/pallas_call | solution.py:50
  51.0 3.3 %collective-permute-start.5 = (bf16[2320,128]{1,0:T(8,128)(2,1)S(1)}, bf16[2320,128]{1,0:T(8,128)(2,1)S(1)}, u32[]{:S(2)}, u32[]{:S(2)}) collective-permute-start(bf16[2320,128]{1,0:T(8,128)(2,1)S(1)} %get-tuple-element.30), channel_id=1, source_target_pairs={{0,2},{1,511},{2,4},{3,1},{4,6},{5,3},{6,8},{7,5},{8,10},{9,7},{10... | collective-permute-start | bytes 1781768 | tf_op jit(solution)/shard_map/ppermute | solution.py:21
  54.3 1.9 %collective-permute-start.7 = (bf16[384,768]{1,0:T(8,128)(2,1)S(1)}, bf16[384,768]{1,0:T(8,128)(2,1)S(1)}, u32[]{:S(2)}, u32[]{:S(2)}) collective-permute-start(bf16[384,768]{1,0:T(8,128)(2,1)S(1)} %get-tuple-element.35), channel_id=1, source_target_pairs={{0,511},{1,2},{2,1},{3,4},{4,3},{5,6},{6,5},{7,8},{8,7},{9,10},{10... | collective-permute-start | bytes 1769480 | tf_op jit(solution)/shard_map/ppermute | solution.py:21
  56.3 2.3 %collective-permute-start.8 = (f32[384,896]{1,0:T(8,128)S(1)}, f32[384,896]{1,0:T(8,128)S(1)}, u32[]{:S(2)}, u32[]{:S(2)}) collective-permute-start(f32[384,896]{1,0:T(8,128)S(1)} %get-tuple-element.36), channel_id=1, source_target_pairs={{0,1},{1,0},{2,3},{3,2},{4,5},{5,4},{6,7},{7,6},{8,9},{9,8},{10,11... | collective-permute-start | bytes 4128776 | tf_op jit(solution)/shard_map/ppermute | solution.py:21
  58.6 0.1 shard_map.74.refs_2_.refs_0_
  58.7 6.3 %collective-permute-done.5.refs_1_ = bf16[2320,128]{1,0:T(8,128)(2,1)S(1)} collective-permute-done((bf16[2320,128]{1,0:T(8,128)(2,1)S(1)}, bf16[2320,128]{1,0:T(8,128)(2,1)S(1)}, u32[]{:S(2)}, u32[]{:S(2)}) %collective-permute-start.5) | collective-permute-done | bytes 593952 | tf_op jit(solution)/shard_map/ppermute | solution.py:21
  65.0 0.2 shard_map.75
  65.2 3.1 %collective-permute-done.7.refs_1_ = bf16[384,768]{1,0:T(8,128)(2,1)S(1)} collective-permute-done((bf16[384,768]{1,0:T(8,128)(2,1)S(1)}, bf16[384,768]{1,0:T(8,128)(2,1)S(1)}, u32[]{:S(2)}, u32[]{:S(2)}) %collective-permute-start.7) | collective-permute-done | bytes 589856 | tf_op jit(solution)/shard_map/ppermute | solution.py:21
  68.4 1.6 %shard_map.77 = (f32[384,768]{1,0:T(8,128)}, f32[384,768]{1,0:T(8,128)}, f32[384]{0:T(512)}) custom-call(f32[384,768]{1,0:T(8,128)S(1)} %get-tuple-element.33.refs_2_.refs_0_, f32[1,384]{1,0:T(1,128)S(1)} %get-tuple-element.34.refs_1_, f32[384,768]{1,0:T(8,128)S(1)} %shard_map.76.refs_2_, f32[384,896]{1,0:T(8,128)S(1)} %collective-permute-done.8.refs_3_), custom_call_target="tpu_custom_call" | custom-call | bytes 6097920 | tf_op jit(solution)/shard_map/pallas_call | solution.py:50
  (13 shorter events, 0.2 us)
Async XLA Ops:
  0.6 27.5 %collective-permute-start.3 = (bf16[384,768]{1,0:T(8,128)(2,1)}, bf16[384,768]{1,0:T(8,128)(2,1)S(1)}, u32[]{:S(2)}, u32[]{:S(2)}) collective-permute-start(bf16[384,768]{1,0:T(8,128)(2,1)} %refs_0_.3), channel_id=1, source_target_pairs={{0,510},{1,3},{2,0},{3,5},{4,2},{5,7},{6,4},{7,9},{8,6},{9,11},{10... | collective-permute-start | bytes 1769480 | tf_op jit(solution)/shard_map/ppermute | solution.py:21
  4.7 1.1 %copy-start = (bf16[384,768]{1,0:T(8,128)(2,1)S(1)}, bf16[384,768]{1,0:T(8,128)(2,1)}, u32[]{:S(2)}) copy-start(bf16[384,768]{1,0:T(8,128)(2,1)} %refs_0_.2) | copy-start | bytes 1769476
  5.7 0.7 copy-start.3
  6.4 14.7 %copy-start.1 = (bf16[384,768]{1,0:T(8,128)(2,1)S(1)}, bf16[384,768]{1,0:T(8,128)(2,1)}, u32[]{:S(2)}) copy-start(bf16[384,768]{1,0:T(8,128)(2,1)} %refs_1_.3) | copy-start | bytes 1769476
  6.4 14.7 %copy-start.2 = (bf16[384,768]{1,0:T(8,128)(2,1)S(1)}, bf16[384,768]{1,0:T(8,128)(2,1)}, u32[]{:S(2)}) copy-start(bf16[384,768]{1,0:T(8,128)(2,1)} %refs_0_.3) | copy-start | bytes 1769476
  6.5 25.2 %collective-permute-start.2 = (bf16[2320,128]{1,0:T(8,128)(2,1)S(1)}, bf16[2320,128]{1,0:T(8,128)(2,1)S(1)}, u32[]{:S(2)}, u32[]{:S(2)}) collective-permute-start(bf16[2320,128]{1,0:T(8,128)(2,1)S(1)} %shard_map.67.refs_3_.refs_1_), channel_id=1, source_target_pairs={{0,2},{1,511},{2,4},{3,1},{4,6},{5,3},{6,8},{7,5},{8,10},{9,7},{10... | collective-permute-start | bytes 1781768 | tf_op jit(solution)/shard_map/ppermute | solution.py:21
  21.4 8.3 %collective-permute-start = (bf16[4624,128]{1,0:T(8,128)(2,1)S(1)}, bf16[4624,128]{1,0:T(8,128)(2,1)S(1)}, u32[]{:S(2)}, u32[]{:S(2)}) collective-permute-start(bf16[4624,128]{1,0:T(8,128)(2,1)S(1)} %get-tuple-element.20.refs_0_), channel_id=1, source_target_pairs={{0,1},{1,0},{2,3},{3,2},{4,5},{5,4},{6,7},{7,6},{8,9},{9,8},{10,11... | collective-permute-start | bytes 3551240 | tf_op jit(solution)/shard_map/ppermute | solution.py:21
  24.3 12.0 %collective-permute-start.1 = (bf16[2320,128]{1,0:T(8,128)(2,1)S(1)}, bf16[2320,128]{1,0:T(8,128)(2,1)S(1)}, u32[]{:S(2)}, u32[]{:S(2)}) collective-permute-start(bf16[2320,128]{1,0:T(8,128)(2,1)S(1)} %get-tuple-element.21), channel_id=1, source_target_pairs={{0,511},{1,2},{2,1},{3,4},{4,3},{5,6},{6,5},{7,8},{8,7},{9,10},{10... | collective-permute-start | bytes 1781768 | tf_op jit(solution)/shard_map/ppermute | solution.py:21
  26.2 23.2 %collective-permute-start.4 = (bf16[2320,128]{1,0:T(8,128)(2,1)S(1)}, bf16[2320,128]{1,0:T(8,128)(2,1)S(1)}, u32[]{:S(2)}, u32[]{:S(2)}) collective-permute-start(bf16[2320,128]{1,0:T(8,128)(2,1)S(1)} %get-tuple-element.28), channel_id=1, source_target_pairs={{0,510},{1,3},{2,0},{3,5},{4,2},{5,7},{6,4},{7,9},{8,6},{9,11},{10... | collective-permute-start | bytes 1781768 | tf_op jit(solution)/shard_map/ppermute | solution.py:21
  34.4 24.2 %collective-permute-start.6 = (bf16[384,768]{1,0:T(8,128)(2,1)S(1)}, bf16[384,768]{1,0:T(8,128)(2,1)S(1)}, u32[]{:S(2)}, u32[]{:S(2)}) collective-permute-start(bf16[384,768]{1,0:T(8,128)(2,1)S(1)} %get-tuple-element.32), channel_id=1, source_target_pairs={{0,510},{1,3},{2,0},{3,5},{4,2},{5,7},{6,4},{7,9},{8,6},{9,11},{10... | collective-permute-start | bytes 1769480 | tf_op jit(solution)/shard_map/ppermute | solution.py:21
  51.0 14.0 %collective-permute-start.5 = (bf16[2320,128]{1,0:T(8,128)(2,1)S(1)}, bf16[2320,128]{1,0:T(8,128)(2,1)S(1)}, u32[]{:S(2)}, u32[]{:S(2)}) collective-permute-start(bf16[2320,128]{1,0:T(8,128)(2,1)S(1)} %get-tuple-element.30), channel_id=1, source_target_pairs={{0,2},{1,511},{2,4},{3,1},{4,6},{5,3},{6,8},{7,5},{8,10},{9,7},{10... | collective-permute-start | bytes 1781768 | tf_op jit(solution)/shard_map/ppermute | solution.py:21
  54.3 14.0 %collective-permute-start.7 = (bf16[384,768]{1,0:T(8,128)(2,1)S(1)}, bf16[384,768]{1,0:T(8,128)(2,1)S(1)}, u32[]{:S(2)}, u32[]{:S(2)}) collective-permute-start(bf16[384,768]{1,0:T(8,128)(2,1)S(1)} %get-tuple-element.35), channel_id=1, source_target_pairs={{0,511},{1,2},{2,1},{3,4},{4,3},{5,6},{6,5},{7,8},{8,7},{9,10},{10... | collective-permute-start | bytes 1769480 | tf_op jit(solution)/shard_map/ppermute | solution.py:21
  56.3 12.1 %collective-permute-start.8 = (f32[384,896]{1,0:T(8,128)S(1)}, f32[384,896]{1,0:T(8,128)S(1)}, u32[]{:S(2)}, u32[]{:S(2)}) collective-permute-start(f32[384,896]{1,0:T(8,128)S(1)} %get-tuple-element.36), channel_id=1, source_target_pairs={{0,1},{1,0},{2,3},{3,2},{4,5},{5,4},{6,7},{7,6},{8,9},{9,8},{10,11... | collective-permute-start | bytes 4128776 | tf_op jit(solution)/shard_map/ppermute | solution.py:21

commit v12 on v11

--- a/solution.py
+++ b/solution.py
@@ -222,13 +222,18 @@
     loss_ref[...] = loss_row(own_ref[:, width:]) + high + low
 
 
-def finish(sums_in, loss_in, term_in, other_ref, grad_ref, text_ref, loss_ref):
+def finish_images(sums_in, loss_in, other_ref, grad_ref, loss_ref, done_ref):
     rows, width = grad_ref.shape
     scale = SOFTMAX_TEMP_VALUE / float(width) ** 0.5
-    text_ref[...] = term_in[...] * scale
     grad_ref[...] = (sums_in[...] + other_ref[:, :width]) * scale
     loss = loss_in[...] + loss_row(other_ref[:, width:])
     loss_ref[...] = (loss / float(WINDOW * rows)).reshape(rows)
+    done_ref[...] = jnp.zeros_like(done_ref)
+
+
+def finish_text(own_ref, near_ref, out_ref):
+    scale = SOFTMAX_TEMP_VALUE / float(out_ref.shape[1]) ** 0.5
+    out_ref[...] = (own_ref[...] + near_ref[...].astype(F32)) * scale
 
 
 def shards(student_image_vectors, teacher_emb, text_emb, species):
@@ -278,18 +283,15 @@
     own_sum, loss = call(
         gather_images, [term, spec(1, rows, F32)], 64 * dot, own_sum, ahead_back, after=(own_term,)
     )
-    (own_term,) = call(
-        gather_text, [term], 32 * dot, own_term, near_back, after=(own_sum,)
-    )
-    grad_student, grad_text, loss = call(
-        finish,
-        [term, term, jax.ShapeDtypeStruct((rows,), F32)],
+    grad_student, loss, done = call(
+        finish_images,
+        [term, jax.ShapeDtypeStruct((rows,), F32), spec(8, LANES, F32)],
         0,
         own_sum,
         loss,
-        own_term,
         other_back,
     )
+    (grad_text,) = call(finish_text, [term], 0, own_term, near_back, after=(done,))
     return grad_student, grad_text, loss
 
 

time: 70.4 us -> 69.9 us (level)
  waiting for transfers between devices: 20.2 us -> 18.7 us
  Pallas kernels: 12.4 us -> 13.3 us
    ppermute x9, waiting for transfers between devices: 20.2 us -> 18.7 us  [moved(): lax.ppermute(value, 'dp', [(i, (i + (odd if i % 2 else even)) % length) f...]
    pallas_call x11, Pallas kernels: 12.4 us -> 13.3 us  [call(): pl.pallas_call(ordered, out_shape=out_shape, in_specs=[pl.BlockSpec(memor...]
  transfers between devices with their start and end apart: 9 -> 9, of which waited for: 4 -> 4; matrix products, arithmetic and copies ran while one was open for 0% -> 0% of each run, Pallas kernels for 15% -> 18%
where the time goes in v12:
time: 69.9 us; the launch traced here: 69.4 us
  starting transfers between devices  34.9 us (50%)
  waiting for transfers between devices  18.7 us (27%)
  Pallas kernels  13.3 us (19%)
  local copies, waits for them, and re-layouts  1.75 us (3%)
  between operations  0.81 us (1%)
    ppermute x9, starting transfers between devices, moved(): lax.ppermute(value, 'dp', [(i, (i + (odd if i % 2 else even)) % length) f...  34.9 us
    ppermute x9, waiting for transfers between devices, moved(): lax.ppermute(value, 'dp', [(i, (i + (odd if i % 2 else even)) % length) f...  18.7 us
    pallas_call x11, Pallas kernels, call(): pl.pallas_call(ordered, out_shape=out_shape, in_specs=[pl.BlockSpec(memor...  13.3 us
    unnamed x8, local copies, waits for them, and re-layouts  1.75 us
  transfers between devices with their start and end apart: 9, of which 4 were waited for; matrix products, arithmetic and copies ran while one was open for 0% of the time, Pallas kernels for 18%

profile of v12, /device:TPU:1, one launch (start us, length us, event | category | flops | bytes accessed | tf_op | source)
XLA Modules:
  0.0 69.4 jit_solution(6100485735486022023)
XLA Ops:
  0.6 4.0 %collective-permute-start.3 = (bf16[384,768]{1,0:T(8,128)(2,1)}, bf16[384,768]{1,0:T(8,128)(2,1)S(1)}, u32[]{:S(2)}, u32[]{:S(2)}) collective-permute-start(bf16[384,768]{1,0:T(8,128)(2,1)} %refs_0_.3), channel_id=1, source_target_pairs={{0,510},{1,3},{2,0},{3,5},{4,2},{5,7},{6,4},{7,9},{8,6},{9,11},{10... | collective-permute-start | bytes 1769480 | tf_op jit(solution)/shard_map/ppermute | solution.py:21
  4.7 1.1 %copy-done = bf16[384,768]{1,0:T(8,128)(2,1)S(1)} copy-done((bf16[384,768]{1,0:T(8,128)(2,1)S(1)}, bf16[384,768]{1,0:T(8,128)(2,1)}, u32[]{:S(2)}) %copy-start) | copy-done | bytes 589848
  5.7 0.7 copy-done.3
  6.5 14.6 %collective-permute-start.2 = (bf16[2320,128]{1,0:T(8,128)(2,1)S(1)}, bf16[2320,128]{1,0:T(8,128)(2,1)S(1)}, u32[]{:S(2)}, u32[]{:S(2)}) collective-permute-start(bf16[2320,128]{1,0:T(8,128)(2,1)S(1)} %shard_map.67.refs_3_.refs_1_), channel_id=1, source_target_pairs={{0,2},{1,511},{2,4},{3,1},{4,6},{5,3},{6,8},{7,5},{8,10},{9,7},{10... | collective-permute-start | bytes 1781768 | tf_op jit(solution)/shard_map/ppermute | solution.py:21
  21.2 0.3 shard_map.68
  21.4 2.9 %collective-permute-start = (bf16[4624,128]{1,0:T(8,128)(2,1)S(1)}, bf16[4624,128]{1,0:T(8,128)(2,1)S(1)}, u32[]{:S(2)}, u32[]{:S(2)}) collective-permute-start(bf16[4624,128]{1,0:T(8,128)(2,1)S(1)} %get-tuple-element.23.refs_0_), channel_id=1, source_target_pairs={{0,1},{1,0},{2,3},{3,2},{4,5},{5,4},{6,7},{7,6},{8,9},{9,8},{10,11... | collective-permute-start | bytes 3551240 | tf_op jit(solution)/shard_map/ppermute | solution.py:21
  24.3 1.9 %collective-permute-start.1 = (bf16[2320,128]{1,0:T(8,128)(2,1)S(1)}, bf16[2320,128]{1,0:T(8,128)(2,1)S(1)}, u32[]{:S(2)}, u32[]{:S(2)}) collective-permute-start(bf16[2320,128]{1,0:T(8,128)(2,1)S(1)} %get-tuple-element.24), channel_id=1, source_target_pairs={{0,511},{1,2},{2,1},{3,4},{4,3},{5,6},{6,5},{7,8},{8,7},{9,10},{10... | collective-permute-start | bytes 1781768 | tf_op jit(solution)/shard_map/ppermute | solution.py:21
  26.2 1.9 %collective-permute-start.4 = (bf16[2320,128]{1,0:T(8,128)(2,1)S(1)}, bf16[2320,128]{1,0:T(8,128)(2,1)S(1)}, u32[]{:S(2)}, u32[]{:S(2)}) collective-permute-start(bf16[2320,128]{1,0:T(8,128)(2,1)S(1)} %get-tuple-element.31), channel_id=1, source_target_pairs={{0,510},{1,3},{2,0},{3,5},{4,2},{5,7},{6,4},{7,9},{8,6},{9,11},{10... | collective-permute-start | bytes 1781768 | tf_op jit(solution)/shard_map/ppermute | solution.py:21
  28.2 1.6 %shard_map.69 = (f32[384,896]{1,0:T(8,128)S(1)}, f32[384,768]{1,0:T(8,128)S(1)}) custom-call(bf16[4624,128]{1,0:T(8,128)(2,1)S(1)} %get-tuple-element.23.refs_0_, bf16[2320,128]{1,0:T(8,128)(2,1)S(1)} %shard_map.67.refs_3_.refs_1_, bf16[384,768]{1,0:T(8,128)(2,1)S(1)} %collective-permute-done.3.refs_2_.refs_0_), custom_call_target="tpu_custom_call" | custom-call | flops 14495514624 | bytes 4333568 | tf_op jit(solution)/shard_map/pallas_call | solution.py:50
  29.8 1.6 %shard_map.70 = (f32[384,896]{1,0:T(8,128)S(1)}, f32[384,768]{1,0:T(8,128)S(1)}) custom-call(bf16[4624,128]{1,0:T(8,128)(2,1)S(1)} %collective-permute-done.refs_0_.refs_1_, bf16[2320,128]{1,0:T(8,128)(2,1)S(1)} %shard_map.67.refs_3_.refs_1_, f32[384,768]{1,0:T(8,128)S(1)} %get-tuple-element.26.refs_2_), custom_call_target="tpu_custom_call" | custom-call | flops 3623878656 | bytes 5513216 | tf_op jit(solution)/shard_map/pallas_call | solution.py:50
  31.3 0.4 collective-permute-done.2.refs_2_
  31.8 2.7 %shard_map.71 = (f32[384,896]{1,0:T(8,128)S(1)}, f32[384,896]{1,0:T(8,128)S(1)}, bf16[384,768]{1,0:T(8,128)(2,1)S(1)}) custom-call(bf16[4624,128]{1,0:T(8,128)(2,1)S(1)} %get-tuple-element.23.refs_0_, bf16[4624,128]{1,0:T(8,128)(2,1)S(1)} %collective-permute-done.refs_0_.refs_1_, bf16[2320,128]{1,0:T(8,128)(2,1)S(1)} %collective-permute-done.2.refs_2_, ...), custom_call_target="tpu_custom_call" | custom-call | flops 3623878656 | bytes 9056256 | tf_op jit(solution)/shard_map/pallas_call | solution.py:50
  34.4 1.9 %collective-permute-start.6 = (bf16[384,768]{1,0:T(8,128)(2,1)S(1)}, bf16[384,768]{1,0:T(8,128)(2,1)S(1)}, u32[]{:S(2)}, u32[]{:S(2)}) collective-permute-start(bf16[384,768]{1,0:T(8,128)(2,1)S(1)} %get-tuple-element.35), channel_id=1, source_target_pairs={{0,510},{1,3},{2,0},{3,5},{4,2},{5,7},{6,4},{7,9},{8,6},{9,11},{10... | collective-permute-start | bytes 1769480 | tf_op jit(solution)/shard_map/ppermute | solution.py:21
  36.4 2.7 %shard_map.72 = (f32[384,896]{1,0:T(8,128)S(1)}, f32[384,896]{1,0:T(8,128)S(1)}, f32[384,768]{1,0:T(8,128)S(1)}) custom-call(bf16[4624,128]{1,0:T(8,128)(2,1)S(1)} %get-tuple-element.23.refs_0_, bf16[4624,128]{1,0:T(8,128)(2,1)S(1)} %collective-permute-done.refs_0_.refs_1_, bf16[2320,128]{1,0:T(8,128)(2,1)S(1)} %collective-permute-done.1.refs_2_, ...), custom_call_target="tpu_custom_call" | custom-call | bytes 9646080 | tf_op jit(solution)/shard_map/pallas_call | solution.py:50
  39.1 10.4 %collective-permute-done.4.refs_1_ = bf16[2320,128]{1,0:T(8,128)(2,1)S(1)} collective-permute-done((bf16[2320,128]{1,0:T(8,128)(2,1)S(1)}, bf16[2320,128]{1,0:T(8,128)(2,1)S(1)}, u32[]{:S(2)}, u32[]{:S(2)}) %collective-permute-start.4) | collective-permute-done | bytes 593952 | tf_op jit(solution)/shard_map/ppermute | solution.py:21
  49.4 1.6 %shard_map.73 = (bf16[2320,128]{1,0:T(8,128)(2,1)S(1)}, bf16[384,768]{1,0:T(8,128)(2,1)S(1)}) custom-call(bf16[384,768]{1,0:T(8,128)(2,1)S(1)} %collective-permute-done.3.refs_2_.refs_0_, bf16[2320,128]{1,0:T(8,128)(2,1)S(1)} %collective-permute-done.4.refs_1_, bf16[2320,128]{1,0:T(8,128)(2,1)S(1)} %collective-permute-done.1.refs_2_, ...), custom_call_target="tpu_custom_call" | custom-call | bytes 4141056 | tf_op jit(solution)/shard_map/pallas_call | solution.py:50
  51.0 3.3 %collective-permute-start.5 = (bf16[2320,128]{1,0:T(8,128)(2,1)S(1)}, bf16[2320,128]{1,0:T(8,128)(2,1)S(1)}, u32[]{:S(2)}, u32[]{:S(2)}) collective-permute-start(bf16[2320,128]{1,0:T(8,128)(2,1)S(1)} %get-tuple-element.33), channel_id=1, source_target_pairs={{0,2},{1,511},{2,4},{3,1},{4,6},{5,3},{6,8},{7,5},{8,10},{9,7},{10... | collective-permute-start | bytes 1781768 | tf_op jit(solution)/shard_map/ppermute | solution.py:21
  54.3 1.9 %collective-permute-start.7 = (f32[384,896]{1,0:T(8,128)S(1)}, f32[384,896]{1,0:T(8,128)S(1)}, u32[]{:S(2)}, u32[]{:S(2)}) collective-permute-start(f32[384,896]{1,0:T(8,128)S(1)} %get-tuple-element.38), channel_id=1, source_target_pairs={{0,1},{1,0},{2,3},{3,2},{4,5},{5,4},{6,7},{7,6},{8,9},{9,8},{10,11... | collective-permute-start | bytes 4128776 | tf_op jit(solution)/shard_map/ppermute | solution.py:21
  56.3 2.4 %collective-permute-start.8 = (bf16[384,768]{1,0:T(8,128)(2,1)S(1)}, bf16[384,768]{1,0:T(8,128)(2,1)S(1)}, u32[]{:S(2)}, u32[]{:S(2)}) collective-permute-start(bf16[384,768]{1,0:T(8,128)(2,1)S(1)} %get-tuple-element.40), channel_id=1, source_target_pairs={{0,511},{1,2},{2,1},{3,4},{4,3},{5,6},{6,5},{7,8},{8,7},{9,10},{10... | collective-permute-start | bytes 1769480 | tf_op jit(solution)/shard_map/ppermute | solution.py:21
  58.8 3.7 %collective-permute-done.5.refs_1_ = bf16[2320,128]{1,0:T(8,128)(2,1)S(1)} collective-permute-done((bf16[2320,128]{1,0:T(8,128)(2,1)S(1)}, bf16[2320,128]{1,0:T(8,128)(2,1)S(1)}, u32[]{:S(2)}, u32[]{:S(2)}) %collective-permute-start.5) | collective-permute-done | bytes 593952 | tf_op jit(solution)/shard_map/ppermute | solution.py:21
  62.5 0.2 shard_map.75
  62.7 1.4 %shard_map.76 = (f32[384,768]{1,0:T(8,128)}, f32[384]{0:T(512)}, f32[8,128]{1,0:T(8,128)S(1)}) custom-call(f32[384,768]{1,0:T(8,128)S(1)} %get-tuple-element.36.refs_0_, f32[1,384]{1,0:T(1,128)S(1)} %get-tuple-element.37.refs_1_, f32[384,896]{1,0:T(8,128)S(1)} %collective-permute-done.7.refs_2_), custom_call_target="tpu_custom_call" | custom-call | bytes 3742720 | tf_op jit(solution)/shard_map/pallas_call | solution.py:50
  64.1 4.3 %collective-permute-done.8.refs_1_ = bf16[384,768]{1,0:T(8,128)(2,1)S(1)} collective-permute-done((bf16[384,768]{1,0:T(8,128)(2,1)S(1)}, bf16[384,768]{1,0:T(8,128)(2,1)S(1)}, u32[]{:S(2)}, u32[]{:S(2)}) %collective-permute-start.8) | collective-permute-done | bytes 589856 | tf_op jit(solution)/shard_map/ppermute | solution.py:21
  68.3 1.1 %shard_map.77 = f32[384,768]{1,0:T(8,128)} custom-call(f32[384,768]{1,0:T(8,128)S(1)} %shard_map.74.refs_2_.refs_0_, bf16[384,768]{1,0:T(8,128)(2,1)S(1)} %collective-permute-done.8.refs_1_, f32[8,128]{1,0:T(8,128)S(1)} %get-tuple-element.41.refs_2_), custom_call_target="tpu_custom_call" | custom-call | bytes 2949120 | tf_op jit(solution)/shard_map/pallas_call | solution.py:50
  (13 shorter events, 0.3 us)
Async XLA Ops:
  0.6 27.5 %collective-permute-start.3 = (bf16[384,768]{1,0:T(8,128)(2,1)}, bf16[384,768]{1,0:T(8,128)(2,1)S(1)}, u32[]{:S(2)}, u32[]{:S(2)}) collective-permute-start(bf16[384,768]{1,0:T(8,128)(2,1)} %refs_0_.3), channel_id=1, source_target_pairs={{0,510},{1,3},{2,0},{3,5},{4,2},{5,7},{6,4},{7,9},{8,6},{9,11},{10... | collective-permute-start | bytes 1769480 | tf_op jit(solution)/shard_map/ppermute | solution.py:21
  4.7 1.1 %copy-start = (bf16[384,768]{1,0:T(8,128)(2,1)S(1)}, bf16[384,768]{1,0:T(8,128)(2,1)}, u32[]{:S(2)}) copy-start(bf16[384,768]{1,0:T(8,128)(2,1)} %refs_0_.2) | copy-start | bytes 1769476
  5.7 0.7 copy-start.3
  6.4 14.7 %copy-start.1 = (bf16[384,768]{1,0:T(8,128)(2,1)S(1)}, bf16[384,768]{1,0:T(8,128)(2,1)}, u32[]{:S(2)}) copy-start(bf16[384,768]{1,0:T(8,128)(2,1)} %refs_1_.3) | copy-start | bytes 1769476
  6.4 14.7 %copy-start.2 = (bf16[384,768]{1,0:T(8,128)(2,1)S(1)}, bf16[384,768]{1,0:T(8,128)(2,1)}, u32[]{:S(2)}) copy-start(bf16[384,768]{1,0:T(8,128)(2,1)} %refs_0_.3) | copy-start | bytes 1769476
  6.5 25.2 %collective-permute-start.2 = (bf16[2320,128]{1,0:T(8,128)(2,1)S(1)}, bf16[2320,128]{1,0:T(8,128)(2,1)S(1)}, u32[]{:S(2)}, u32[]{:S(2)}) collective-permute-start(bf16[2320,128]{1,0:T(8,128)(2,1)S(1)} %shard_map.67.refs_3_.refs_1_), channel_id=1, source_target_pairs={{0,2},{1,511},{2,4},{3,1},{4,6},{5,3},{6,8},{7,5},{8,10},{9,7},{10... | collective-permute-start | bytes 1781768 | tf_op jit(solution)/shard_map/ppermute | solution.py:21
  21.4 8.3 %collective-permute-start = (bf16[4624,128]{1,0:T(8,128)(2,1)S(1)}, bf16[4624,128]{1,0:T(8,128)(2,1)S(1)}, u32[]{:S(2)}, u32[]{:S(2)}) collective-permute-start(bf16[4624,128]{1,0:T(8,128)(2,1)S(1)} %get-tuple-element.23.refs_0_), channel_id=1, source_target_pairs={{0,1},{1,0},{2,3},{3,2},{4,5},{5,4},{6,7},{7,6},{8,9},{9,8},{10,11... | collective-permute-start | bytes 3551240 | tf_op jit(solution)/shard_map/ppermute | solution.py:21
  24.3 12.0 %collective-permute-start.1 = (bf16[2320,128]{1,0:T(8,128)(2,1)S(1)}, bf16[2320,128]{1,0:T(8,128)(2,1)S(1)}, u32[]{:S(2)}, u32[]{:S(2)}) collective-permute-start(bf16[2320,128]{1,0:T(8,128)(2,1)S(1)} %get-tuple-element.24), channel_id=1, source_target_pairs={{0,511},{1,2},{2,1},{3,4},{4,3},{5,6},{6,5},{7,8},{8,7},{9,10},{10... | collective-permute-start | bytes 1781768 | tf_op jit(solution)/shard_map/ppermute | solution.py:21
  26.2 23.2 %collective-permute-start.4 = (bf16[2320,128]{1,0:T(8,128)(2,1)S(1)}, bf16[2320,128]{1,0:T(8,128)(2,1)S(1)}, u32[]{:S(2)}, u32[]{:S(2)}) collective-permute-start(bf16[2320,128]{1,0:T(8,128)(2,1)S(1)} %get-tuple-element.31), channel_id=1, source_target_pairs={{0,510},{1,3},{2,0},{3,5},{4,2},{5,7},{6,4},{7,9},{8,6},{9,11},{10... | collective-permute-start | bytes 1781768 | tf_op jit(solution)/shard_map/ppermute | solution.py:21
  34.4 24.2 %collective-permute-start.6 = (bf16[384,768]{1,0:T(8,128)(2,1)S(1)}, bf16[384,768]{1,0:T(8,128)(2,1)S(1)}, u32[]{:S(2)}, u32[]{:S(2)}) collective-permute-start(bf16[384,768]{1,0:T(8,128)(2,1)S(1)} %get-tuple-element.35), channel_id=1, source_target_pairs={{0,510},{1,3},{2,0},{3,5},{4,2},{5,7},{6,4},{7,9},{8,6},{9,11},{10... | collective-permute-start | bytes 1769480 | tf_op jit(solution)/shard_map/ppermute | solution.py:21
  51.0 11.4 %collective-permute-start.5 = (bf16[2320,128]{1,0:T(8,128)(2,1)S(1)}, bf16[2320,128]{1,0:T(8,128)(2,1)S(1)}, u32[]{:S(2)}, u32[]{:S(2)}) collective-permute-start(bf16[2320,128]{1,0:T(8,128)(2,1)S(1)} %get-tuple-element.33), channel_id=1, source_target_pairs={{0,2},{1,511},{2,4},{3,1},{4,6},{5,3},{6,8},{7,5},{8,10},{9,7},{10... | collective-permute-start | bytes 1781768 | tf_op jit(solution)/shard_map/ppermute | solution.py:21
  54.3 8.4 %collective-permute-start.7 = (f32[384,896]{1,0:T(8,128)S(1)}, f32[384,896]{1,0:T(8,128)S(1)}, u32[]{:S(2)}, u32[]{:S(2)}) collective-permute-start(f32[384,896]{1,0:T(8,128)S(1)} %get-tuple-element.38), channel_id=1, source_target_pairs={{0,1},{1,0},{2,3},{3,2},{4,5},{5,4},{6,7},{7,6},{8,9},{9,8},{10,11... | collective-permute-start | bytes 4128776 | tf_op jit(solution)/shard_map/ppermute | solution.py:21
  56.3 12.0 %collective-permute-start.8 = (bf16[384,768]{1,0:T(8,128)(2,1)S(1)}, bf16[384,768]{1,0:T(8,128)(2,1)S(1)}, u32[]{:S(2)}, u32[]{:S(2)}) collective-permute-start(bf16[384,768]{1,0:T(8,128)(2,1)S(1)} %get-tuple-element.40), channel_id=1, source_target_pairs={{0,511},{1,2},{2,1},{3,4},{4,3},{5,6},{6,5},{7,8},{8,7},{9,10},{10... | collective-permute-start | bytes 1769480 | tf_op jit(solution)/shard_map/ppermute | solution.py:21

commit v13 on v12

--- a/solution.py
+++ b/solution.py
@@ -107,6 +107,10 @@
     out_ref[out_ref.shape[0] - EXTRA :, :] = digits(species_ref[...])
 
 
+def first_token(out_ref):
+    out_ref[...] = jnp.zeros_like(out_ref)
+
+
 def pack_images(student_ref, teacher_ref, species_ref, text_ref, out_ref, teacher_out, text_out):
     text_out[...] = text_ref[...]
     rows, width = student_ref.shape
@@ -248,7 +252,8 @@
     sent = spec(rows, width, BF16)
     packed = spec(rows * width // LANES + EXTRA, LANES, BF16)
     ahead_student = back(student_image_vectors)
-    (text,) = call(pack_text, [packed], 0, text_emb, species)
+    (token,) = call(first_token, [spec(8, LANES, F32)], 64 * dot)
+    (text,) = call(pack_text, [packed], 0, text_emb, species, after=(token,))
     second = onward(text)
     images, teacher, text_again = call(
         pack_images,

time: 69.9 us -> 70.6 us (1.010)
  the two profiles are of different devices: /device:TPU:1 before, /device:TPU:6 now
where the time goes in v13:
time: 70.6 us; the launch traced here: 70.2 us
  starting transfers between devices  46.7 us (66%)
  Pallas kernels  13.3 us (19%)
  waiting for transfers between devices  9.37 us (13%)
  between operations  0.86 us (1%)
    ppermute x9, starting transfers between devices, moved(): lax.ppermute(value, 'dp', [(i, (i + (odd if i % 2 else even)) % length) f...  46.7 us
    pallas_call x12, Pallas kernels, call(): pl.pallas_call(ordered, out_shape=out_shape, in_specs=[pl.BlockSpec(memor...  13.3 us
    ppermute x9, waiting for transfers between devices, moved(): lax.ppermute(value, 'dp', [(i, (i + (odd if i % 2 else even)) % length) f...  9.37 us
  transfers between devices with their start and end apart: 9, of which 3 were waited for; matrix products, arithmetic and copies ran while one was open for 0% of the time, Pallas kernels for 17%

profile of v13, /device:TPU:6, one launch (start us, length us, event | category | flops | bytes accessed | tf_op | source)
XLA Modules:
  0.0 70.2 jit_solution(8567016806542183522)
XLA Ops:
  0.7 14.3 %collective-permute-start.3 = (bf16[384,768]{1,0:T(8,128)(2,1)}, bf16[384,768]{1,0:T(8,128)(2,1)S(1)}, u32[]{:S(2)}, u32[]{:S(2)}) collective-permute-start(bf16[384,768]{1,0:T(8,128)(2,1)} %refs_0_.3), channel_id=1, source_target_pairs={{0,510},{1,3},{2,0},{3,5},{4,2},{5,7},{6,4},{7,9},{8,6},{9,11},{10... | collective-permute-start | bytes 1769480 | tf_op jit(solution)/shard_map/ppermute | solution.py:21
  14.9 0.0 copy-start.1
  15.0 0.1 shard_map.68.refs_3_.refs_1_
  15.1 2.1 %collective-permute-start.2 = (bf16[2320,128]{1,0:T(8,128)(2,1)S(1)}, bf16[2320,128]{1,0:T(8,128)(2,1)S(1)}, u32[]{:S(2)}, u32[]{:S(2)}) collective-permute-start(bf16[2320,128]{1,0:T(8,128)(2,1)S(1)} %shard_map.68.refs_3_.refs_1_), channel_id=1, source_target_pairs={{0,2},{1,511},{2,4},{3,1},{4,6},{5,3},{6,8},{7,5},{8,10},{9,7},{10... | collective-permute-start | bytes 1781768 | tf_op jit(solution)/shard_map/ppermute | solution.py:21
  17.1 0.3 shard_map.69
  17.4 1.9 %collective-permute-start = (bf16[4624,128]{1,0:T(8,128)(2,1)S(1)}, bf16[4624,128]{1,0:T(8,128)(2,1)S(1)}, u32[]{:S(2)}, u32[]{:S(2)}) collective-permute-start(bf16[4624,128]{1,0:T(8,128)(2,1)S(1)} %get-tuple-element.23.refs_0_), channel_id=1, source_target_pairs={{0,1},{1,0},{2,3},{3,2},{4,5},{5,4},{6,7},{7,6},{8,9},{9,8},{10,11... | collective-permute-start | bytes 3551240 | tf_op jit(solution)/shard_map/ppermute | solution.py:21
  19.3 8.2 %collective-permute-start.1 = (bf16[2320,128]{1,0:T(8,128)(2,1)S(1)}, bf16[2320,128]{1,0:T(8,128)(2,1)S(1)}, u32[]{:S(2)}, u32[]{:S(2)}) collective-permute-start(bf16[2320,128]{1,0:T(8,128)(2,1)S(1)} %get-tuple-element.24), channel_id=1, source_target_pairs={{0,511},{1,2},{2,1},{3,4},{4,3},{5,6},{6,5},{7,8},{8,7},{9,10},{10... | collective-permute-start | bytes 1781768 | tf_op jit(solution)/shard_map/ppermute | solution.py:21
  27.6 1.9 %collective-permute-start.4 = (bf16[2320,128]{1,0:T(8,128)(2,1)S(1)}, bf16[2320,128]{1,0:T(8,128)(2,1)S(1)}, u32[]{:S(2)}, u32[]{:S(2)}) collective-permute-start(bf16[2320,128]{1,0:T(8,128)(2,1)S(1)} %get-tuple-element.31), channel_id=1, source_target_pairs={{0,510},{1,3},{2,0},{3,5},{4,2},{5,7},{6,4},{7,9},{8,6},{9,11},{10... | collective-permute-start | bytes 1781768 | tf_op jit(solution)/shard_map/ppermute | solution.py:21
  29.5 1.6 %shard_map.70 = (f32[384,896]{1,0:T(8,128)S(1)}, f32[384,768]{1,0:T(8,128)S(1)}) custom-call(bf16[4624,128]{1,0:T(8,128)(2,1)S(1)} %get-tuple-element.23.refs_0_, bf16[2320,128]{1,0:T(8,128)(2,1)S(1)} %shard_map.68.refs_3_.refs_1_, bf16[384,768]{1,0:T(8,128)(2,1)S(1)} %collective-permute-done.3.refs_2_.refs_0_), custom_call_target="tpu_custom_call" | custom-call | flops 14495514624 | bytes 4333568 | tf_op jit(solution)/shard_map/pallas_call | solution.py:50
  31.1 1.6 %shard_map.71 = (f32[384,896]{1,0:T(8,128)S(1)}, f32[384,768]{1,0:T(8,128)S(1)}) custom-call(bf16[4624,128]{1,0:T(8,128)(2,1)S(1)} %collective-permute-done.refs_0_.refs_1_, bf16[2320,128]{1,0:T(8,128)(2,1)S(1)} %shard_map.68.refs_3_.refs_1_, f32[384,768]{1,0:T(8,128)S(1)} %get-tuple-element.26.refs_2_), custom_call_target="tpu_custom_call" | custom-call | flops 3623878656 | bytes 5513216 | tf_op jit(solution)/shard_map/pallas_call | solution.py:50
  32.7 0.9 %collective-permute-done.2.refs_2_ = bf16[2320,128]{1,0:T(8,128)(2,1)S(1)} collective-permute-done((bf16[2320,128]{1,0:T(8,128)(2,1)S(1)}, bf16[2320,128]{1,0:T(8,128)(2,1)S(1)}, u32[]{:S(2)}, u32[]{:S(2)}) %collective-permute-start.2) | collective-permute-done | bytes 593952 | tf_op jit(solution)/shard_map/ppermute | solution.py:21
  33.6 2.7 %shard_map.72 = (f32[384,896]{1,0:T(8,128)S(1)}, f32[384,896]{1,0:T(8,128)S(1)}, bf16[384,768]{1,0:T(8,128)(2,1)S(1)}) custom-call(bf16[4624,128]{1,0:T(8,128)(2,1)S(1)} %get-tuple-element.23.refs_0_, bf16[4624,128]{1,0:T(8,128)(2,1)S(1)} %collective-permute-done.refs_0_.refs_1_, bf16[2320,128]{1,0:T(8,128)(2,1)S(1)} %collective-permute-done.2.refs_2_, ...), custom_call_target="tpu_custom_call" | custom-call | flops 3623878656 | bytes 9056256 | tf_op jit(solution)/shard_map/pallas_call | solution.py:50
  36.2 6.2 %collective-permute-start.6 = (bf16[384,768]{1,0:T(8,128)(2,1)S(1)}, bf16[384,768]{1,0:T(8,128)(2,1)S(1)}, u32[]{:S(2)}, u32[]{:S(2)}) collective-permute-start(bf16[384,768]{1,0:T(8,128)(2,1)S(1)} %get-tuple-element.35), channel_id=1, source_target_pairs={{0,510},{1,3},{2,0},{3,5},{4,2},{5,7},{6,4},{7,9},{8,6},{9,11},{10... | collective-permute-start | bytes 1769480 | tf_op jit(solution)/shard_map/ppermute | solution.py:21
  42.5 2.7 %shard_map.73 = (f32[384,896]{1,0:T(8,128)S(1)}, f32[384,896]{1,0:T(8,128)S(1)}, f32[384,768]{1,0:T(8,128)S(1)}) custom-call(bf16[4624,128]{1,0:T(8,128)(2,1)S(1)} %get-tuple-element.23.refs_0_, bf16[4624,128]{1,0:T(8,128)(2,1)S(1)} %collective-permute-done.refs_0_.refs_1_, bf16[2320,128]{1,0:T(8,128)(2,1)S(1)} %collective-permute-done.1.refs_2_, ...), custom_call_target="tpu_custom_call" | custom-call | bytes 9646080 | tf_op jit(solution)/shard_map/pallas_call | solution.py:50
  45.2 1.6 %shard_map.74 = (bf16[2320,128]{1,0:T(8,128)(2,1)S(1)}, bf16[384,768]{1,0:T(8,128)(2,1)S(1)}) custom-call(bf16[384,768]{1,0:T(8,128)(2,1)S(1)} %collective-permute-done.3.refs_2_.refs_0_, bf16[2320,128]{1,0:T(8,128)(2,1)S(1)} %collective-permute-done.4.refs_1_, bf16[2320,128]{1,0:T(8,128)(2,1)S(1)} %collective-permute-done.1.refs_2_, ...), custom_call_target="tpu_custom_call" | custom-call | bytes 4141056 | tf_op jit(solution)/shard_map/pallas_call | solution.py:50
  46.7 1.9 %collective-permute-start.5 = (bf16[2320,128]{1,0:T(8,128)(2,1)S(1)}, bf16[2320,128]{1,0:T(8,128)(2,1)S(1)}, u32[]{:S(2)}, u32[]{:S(2)}) collective-permute-start(bf16[2320,128]{1,0:T(8,128)(2,1)S(1)} %get-tuple-element.33), channel_id=1, source_target_pairs={{0,2},{1,511},{2,4},{3,1},{4,6},{5,3},{6,8},{7,5},{8,10},{9,7},{10... | collective-permute-start | bytes 1781768 | tf_op jit(solution)/shard_map/ppermute | solution.py:21
  48.7 1.9 %collective-permute-start.7 = (f32[384,896]{1,0:T(8,128)S(1)}, f32[384,896]{1,0:T(8,128)S(1)}, u32[]{:S(2)}, u32[]{:S(2)}) collective-permute-start(f32[384,896]{1,0:T(8,128)S(1)} %get-tuple-element.38), channel_id=1, source_target_pairs={{0,1},{1,0},{2,3},{3,2},{4,5},{5,4},{6,7},{7,6},{8,9},{9,8},{10,11... | collective-permute-start | bytes 4128776 | tf_op jit(solution)/shard_map/ppermute | solution.py:21
  50.6 8.2 %collective-permute-start.8 = (bf16[384,768]{1,0:T(8,128)(2,1)S(1)}, bf16[384,768]{1,0:T(8,128)(2,1)S(1)}, u32[]{:S(2)}, u32[]{:S(2)}) collective-permute-start(bf16[384,768]{1,0:T(8,128)(2,1)S(1)} %get-tuple-element.40), channel_id=1, source_target_pairs={{0,511},{1,2},{2,1},{3,4},{4,3},{5,6},{6,5},{7,8},{8,7},{9,10},{10... | collective-permute-start | bytes 1769480 | tf_op jit(solution)/shard_map/ppermute | solution.py:21
  58.8 0.2 shard_map.75.refs_2_.refs_0_
  59.0 6.4 %collective-permute-done.5.refs_1_ = bf16[2320,128]{1,0:T(8,128)(2,1)S(1)} collective-permute-done((bf16[2320,128]{1,0:T(8,128)(2,1)S(1)}, bf16[2320,128]{1,0:T(8,128)(2,1)S(1)}, u32[]{:S(2)}, u32[]{:S(2)}) %collective-permute-start.5) | collective-permute-done | bytes 593952 | tf_op jit(solution)/shard_map/ppermute | solution.py:21
  65.4 0.2 shard_map.76
  65.6 1.4 %shard_map.77 = (f32[384,768]{1,0:T(8,128)}, f32[384]{0:T(512)}, f32[8,128]{1,0:T(8,128)S(1)}) custom-call(f32[384,768]{1,0:T(8,128)S(1)} %get-tuple-element.36.refs_0_, f32[1,384]{1,0:T(1,128)S(1)} %get-tuple-element.37.refs_1_, f32[384,896]{1,0:T(8,128)S(1)} %collective-permute-done.7.refs_2_), custom_call_target="tpu_custom_call" | custom-call | bytes 3742720 | tf_op jit(solution)/shard_map/pallas_call | solution.py:50
  67.0 2.1 %collective-permute-done.8.refs_1_ = bf16[384,768]{1,0:T(8,128)(2,1)S(1)} collective-permute-done((bf16[384,768]{1,0:T(8,128)(2,1)S(1)}, bf16[384,768]{1,0:T(8,128)(2,1)S(1)}, u32[]{:S(2)}, u32[]{:S(2)}) %collective-permute-start.8) | collective-permute-done | bytes 589856 | tf_op jit(solution)/shard_map/ppermute | solution.py:21
  69.1 1.1 %shard_map.78 = f32[384,768]{1,0:T(8,128)} custom-call(f32[384,768]{1,0:T(8,128)S(1)} %shard_map.75.refs_2_.refs_0_, bf16[384,768]{1,0:T(8,128)(2,1)S(1)} %collective-permute-done.8.refs_1_, f32[8,128]{1,0:T(8,128)S(1)} %get-tuple-element.41.refs_2_), custom_call_target="tpu_custom_call" | custom-call | bytes 2949120 | tf_op jit(solution)/shard_map/pallas_call | solution.py:50
  (14 shorter events, 0.0 us)
Async XLA Ops:
  0.6 14.3 %copy-start = (bf16[384,768]{1,0:T(8,128)(2,1)S(1)}, bf16[384,768]{1,0:T(8,128)(2,1)}, u32[]{:S(2)}) copy-start(bf16[384,768]{1,0:T(8,128)(2,1)} %refs_0_.2) | copy-start | bytes 1769476
  0.6 14.3 %copy-start.3 = (s32[384]{0:T(512)S(1)}, s32[384]{0:T(512)}, u32[]{:S(2)}) copy-start(s32[384]{0:T(512)} %refs_2_.1) | copy-start | bytes 4612
  0.7 28.9 %collective-permute-start.3 = (bf16[384,768]{1,0:T(8,128)(2,1)}, bf16[384,768]{1,0:T(8,128)(2,1)S(1)}, u32[]{:S(2)}, u32[]{:S(2)}) collective-permute-start(bf16[384,768]{1,0:T(8,128)(2,1)} %refs_0_.3), channel_id=1, source_target_pairs={{0,510},{1,3},{2,0},{3,5},{4,2},{5,7},{6,4},{7,9},{8,6},{9,11},{10... | collective-permute-start | bytes 1769480 | tf_op jit(solution)/shard_map/ppermute | solution.py:21
  14.9 2.2 %copy-start.1 = (bf16[384,768]{1,0:T(8,128)(2,1)S(1)}, bf16[384,768]{1,0:T(8,128)(2,1)}, u32[]{:S(2)}) copy-start(bf16[384,768]{1,0:T(8,128)(2,1)} %refs_1_.3) | copy-start | bytes 1769476
  15.0 2.2 %copy-start.2 = (bf16[384,768]{1,0:T(8,128)(2,1)S(1)}, bf16[384,768]{1,0:T(8,128)(2,1)}, u32[]{:S(2)}) copy-start(bf16[384,768]{1,0:T(8,128)(2,1)} %refs_0_.3) | copy-start | bytes 1769476
  15.1 18.5 %collective-permute-start.2 = (bf16[2320,128]{1,0:T(8,128)(2,1)S(1)}, bf16[2320,128]{1,0:T(8,128)(2,1)S(1)}, u32[]{:S(2)}, u32[]{:S(2)}) collective-permute-start(bf16[2320,128]{1,0:T(8,128)(2,1)S(1)} %shard_map.68.refs_3_.refs_1_), channel_id=1, source_target_pairs={{0,2},{1,511},{2,4},{3,1},{4,6},{5,3},{6,8},{7,5},{8,10},{9,7},{10... | collective-permute-start | bytes 1781768 | tf_op jit(solution)/shard_map/ppermute | solution.py:21
  17.4 13.7 %collective-permute-start = (bf16[4624,128]{1,0:T(8,128)(2,1)S(1)}, bf16[4624,128]{1,0:T(8,128)(2,1)S(1)}, u32[]{:S(2)}, u32[]{:S(2)}) collective-permute-start(bf16[4624,128]{1,0:T(8,128)(2,1)S(1)} %get-tuple-element.23.refs_0_), channel_id=1, source_target_pairs={{0,1},{1,0},{2,3},{3,2},{4,5},{5,4},{6,7},{7,6},{8,9},{9,8},{10,11... | collective-permute-start | bytes 3551240 | tf_op jit(solution)/shard_map/ppermute | solution.py:21
  19.3 23.1 %collective-permute-start.1 = (bf16[2320,128]{1,0:T(8,128)(2,1)S(1)}, bf16[2320,128]{1,0:T(8,128)(2,1)S(1)}, u32[]{:S(2)}, u32[]{:S(2)}) collective-permute-start(bf16[2320,128]{1,0:T(8,128)(2,1)S(1)} %get-tuple-element.24), channel_id=1, source_target_pairs={{0,511},{1,2},{2,1},{3,4},{4,3},{5,6},{6,5},{7,8},{8,7},{9,10},{10... | collective-permute-start | bytes 1781768 | tf_op jit(solution)/shard_map/ppermute | solution.py:21
  27.6 17.6 %collective-permute-start.4 = (bf16[2320,128]{1,0:T(8,128)(2,1)S(1)}, bf16[2320,128]{1,0:T(8,128)(2,1)S(1)}, u32[]{:S(2)}, u32[]{:S(2)}) collective-permute-start(bf16[2320,128]{1,0:T(8,128)(2,1)S(1)} %get-tuple-element.31), channel_id=1, source_target_pairs={{0,510},{1,3},{2,0},{3,5},{4,2},{5,7},{6,4},{7,9},{8,6},{9,11},{10... | collective-permute-start | bytes 1781768 | tf_op jit(solution)/shard_map/ppermute | solution.py:21
  36.2 22.6 %collective-permute-start.6 = (bf16[384,768]{1,0:T(8,128)(2,1)S(1)}, bf16[384,768]{1,0:T(8,128)(2,1)S(1)}, u32[]{:S(2)}, u32[]{:S(2)}) collective-permute-start(bf16[384,768]{1,0:T(8,128)(2,1)S(1)} %get-tuple-element.35), channel_id=1, source_target_pairs={{0,510},{1,3},{2,0},{3,5},{4,2},{5,7},{6,4},{7,9},{8,6},{9,11},{10... | collective-permute-start | bytes 1769480 | tf_op jit(solution)/shard_map/ppermute | solution.py:21
  46.7 18.7 %collective-permute-start.5 = (bf16[2320,128]{1,0:T(8,128)(2,1)S(1)}, bf16[2320,128]{1,0:T(8,128)(2,1)S(1)}, u32[]{:S(2)}, u32[]{:S(2)}) collective-permute-start(bf16[2320,128]{1,0:T(8,128)(2,1)S(1)} %get-tuple-element.33), channel_id=1, source_target_pairs={{0,2},{1,511},{2,4},{3,1},{4,6},{5,3},{6,8},{7,5},{8,10},{9,7},{10... | collective-permute-start | bytes 1781768 | tf_op jit(solution)/shard_map/ppermute | solution.py:21
  48.7 17.0 %collective-permute-start.7 = (f32[384,896]{1,0:T(8,128)S(1)}, f32[384,896]{1,0:T(8,128)S(1)}, u32[]{:S(2)}, u32[]{:S(2)}) collective-permute-start(f32[384,896]{1,0:T(8,128)S(1)} %get-tuple-element.38), channel_id=1, source_target_pairs={{0,1},{1,0},{2,3},{3,2},{4,5},{5,4},{6,7},{7,6},{8,9},{9,8},{10,11... | collective-permute-start | bytes 4128776 | tf_op jit(solution)/shard_map/ppermute | solution.py:21
  50.6 18.5 %collective-permute-start.8 = (bf16[384,768]{1,0:T(8,128)(2,1)S(1)}, bf16[384,768]{1,0:T(8,128)(2,1)S(1)}, u32[]{:S(2)}, u32[]{:S(2)}) collective-permute-start(bf16[384,768]{1,0:T(8,128)(2,1)S(1)} %get-tuple-element.40), channel_id=1, source_target_pairs={{0,511},{1,2},{2,1},{3,4},{4,3},{5,6},{6,5},{7,8},{8,7},{9,10},{10... | collective-permute-start | bytes 1769480 | tf_op jit(solution)/shard_map/ppermute | solution.py:21

commit v14 on v13

--- a/solution.py
+++ b/solution.py
@@ -267,10 +267,10 @@
     near = across(text_again)
     other = within(images)
     ahead_teacher = back(teacher)
-    own_sum, own_term = call(
-        own_first, [sums, term], 64 * dot, images, text, after=(ahead_student,)
-    )
-    other_sum, own_term = call(other_first, [sums, term], 16 * dot, other, text, own_term)
+    own_sum, own_term = call(own_first, [sums, term], 64 * dot, images, text)
+    other_sum, own_term = call(
+        other_first, [sums, term], 16 * dot, other, text, own_term, after=(ahead_student,)
+    )
     own_sum, other_sum, second_term = call(
         both, [sums, sums, sent], 16 * dot, images, other, second, own_sum, other_sum
     )

time: 70.6 us -> 69 us (0.977)
  the two profiles are of different devices: /device:TPU:6 before, /device:TPU:1 now
where the time goes in v14:
time: 69 us; the launch traced here: 67.9 us
  starting transfers between devices  35 us (51%)
  waiting for transfers between devices  18.7 us (27%)
  Pallas kernels  13.3 us (19%)
  between operations  0.85 us (1%)
    ppermute x9, starting transfers between devices, moved(): lax.ppermute(value, 'dp', [(i, (i + (odd if i % 2 else even)) % length) f...  35 us
    ppermute x9, waiting for transfers between devices, moved(): lax.ppermute(value, 'dp', [(i, (i + (odd if i % 2 else even)) % length) f...  18.7 us
    pallas_call x12, Pallas kernels, call(): pl.pallas_call(ordered, out_shape=out_shape, in_specs=[pl.BlockSpec(memor...  13.3 us
  transfers between devices with their start and end apart: 9, of which 4 were waited for; matrix products, arithmetic and copies ran while one was open for 0% of the time, Pallas kernels for 18%

profile of v14, /device:TPU:1, one launch (start us, length us, event | category | flops | bytes accessed | tf_op | source)
XLA Modules:
  0.0 67.9 jit_solution(16979850857782989521)
XLA Ops:
  0.7 4.2 %collective-permute-start.3 = (bf16[384,768]{1,0:T(8,128)(2,1)}, bf16[384,768]{1,0:T(8,128)(2,1)S(1)}, u32[]{:S(2)}, u32[]{:S(2)}) collective-permute-start(bf16[384,768]{1,0:T(8,128)(2,1)} %refs_0_.3), channel_id=1, source_target_pairs={{0,510},{1,3},{2,0},{3,5},{4,2},{5,7},{6,4},{7,9},{8,6},{9,11},{10... | collective-permute-start | bytes 1769480 | tf_op jit(solution)/shard_map/ppermute | solution.py:21
  4.9 0.1 shard_map.68.refs_3_.refs_1_
  5.0 14.6 %collective-permute-start.2 = (bf16[2320,128]{1,0:T(8,128)(2,1)S(1)}, bf16[2320,128]{1,0:T(8,128)(2,1)S(1)}, u32[]{:S(2)}, u32[]{:S(2)}) collective-permute-start(bf16[2320,128]{1,0:T(8,128)(2,1)S(1)} %shard_map.68.refs_3_.refs_1_), channel_id=1, source_target_pairs={{0,2},{1,511},{2,4},{3,1},{4,6},{5,3},{6,8},{7,5},{8,10},{9,7},{10... | collective-permute-start | bytes 1781768 | tf_op jit(solution)/shard_map/ppermute | solution.py:21
  19.6 0.3 shard_map.69
  19.9 2.9 %collective-permute-start = (bf16[4624,128]{1,0:T(8,128)(2,1)S(1)}, bf16[4624,128]{1,0:T(8,128)(2,1)S(1)}, u32[]{:S(2)}, u32[]{:S(2)}) collective-permute-start(bf16[4624,128]{1,0:T(8,128)(2,1)S(1)} %get-tuple-element.23.refs_0_), channel_id=1, source_target_pairs={{0,1},{1,0},{2,3},{3,2},{4,5},{5,4},{6,7},{7,6},{8,9},{9,8},{10,11... | collective-permute-start | bytes 3551240 | tf_op jit(solution)/shard_map/ppermute | solution.py:21
  22.8 1.9 %collective-permute-start.1 = (bf16[2320,128]{1,0:T(8,128)(2,1)S(1)}, bf16[2320,128]{1,0:T(8,128)(2,1)S(1)}, u32[]{:S(2)}, u32[]{:S(2)}) collective-permute-start(bf16[2320,128]{1,0:T(8,128)(2,1)S(1)} %get-tuple-element.24), channel_id=1, source_target_pairs={{0,511},{1,2},{2,1},{3,4},{4,3},{5,6},{6,5},{7,8},{8,7},{9,10},{10... | collective-permute-start | bytes 1781768 | tf_op jit(solution)/shard_map/ppermute | solution.py:21
  24.7 1.9 %collective-permute-start.4 = (bf16[2320,128]{1,0:T(8,128)(2,1)S(1)}, bf16[2320,128]{1,0:T(8,128)(2,1)S(1)}, u32[]{:S(2)}, u32[]{:S(2)}) collective-permute-start(bf16[2320,128]{1,0:T(8,128)(2,1)S(1)} %get-tuple-element.31), channel_id=1, source_target_pairs={{0,510},{1,3},{2,0},{3,5},{4,2},{5,7},{6,4},{7,9},{8,6},{9,11},{10... | collective-permute-start | bytes 1781768 | tf_op jit(solution)/shard_map/ppermute | solution.py:21
  26.6 1.6 %shard_map.70 = (f32[384,896]{1,0:T(8,128)S(1)}, f32[384,768]{1,0:T(8,128)S(1)}) custom-call(bf16[4624,128]{1,0:T(8,128)(2,1)S(1)} %get-tuple-element.23.refs_0_, bf16[2320,128]{1,0:T(8,128)(2,1)S(1)} %shard_map.68.refs_3_.refs_1_), custom_call_target="tpu_custom_call" | custom-call | flops 14495514624 | bytes 4333568 | tf_op jit(solution)/shard_map/pallas_call | solution.py:50
  28.2 1.6 %shard_map.71 = (f32[384,896]{1,0:T(8,128)S(1)}, f32[384,768]{1,0:T(8,128)S(1)}) custom-call(bf16[4624,128]{1,0:T(8,128)(2,1)S(1)} %collective-permute-done.refs_0_.refs_1_, bf16[2320,128]{1,0:T(8,128)(2,1)S(1)} %shard_map.68.refs_3_.refs_1_, f32[384,768]{1,0:T(8,128)S(1)} %get-tuple-element.26.refs_2_, ...), custom_call_target="tpu_custom_call" | custom-call | flops 3623878656 | bytes 5513216 | tf_op jit(solution)/shard_map/pallas_call | solution.py:50
  29.8 2.1 %collective-permute-done.2.refs_2_ = bf16[2320,128]{1,0:T(8,128)(2,1)S(1)} collective-permute-done((bf16[2320,128]{1,0:T(8,128)(2,1)S(1)}, bf16[2320,128]{1,0:T(8,128)(2,1)S(1)}, u32[]{:S(2)}, u32[]{:S(2)}) %collective-permute-start.2) | collective-permute-done | bytes 593952 | tf_op jit(solution)/shard_map/ppermute | solution.py:21
  31.9 2.7 %shard_map.72 = (f32[384,896]{1,0:T(8,128)S(1)}, f32[384,896]{1,0:T(8,128)S(1)}, bf16[384,768]{1,0:T(8,128)(2,1)S(1)}) custom-call(bf16[4624,128]{1,0:T(8,128)(2,1)S(1)} %get-tuple-element.23.refs_0_, bf16[4624,128]{1,0:T(8,128)(2,1)S(1)} %collective-permute-done.refs_0_.refs_1_, bf16[2320,128]{1,0:T(8,128)(2,1)S(1)} %collective-permute-done.2.refs_2_, ...), custom_call_target="tpu_custom_call" | custom-call | flops 3623878656 | bytes 9056256 | tf_op jit(solution)/shard_map/pallas_call | solution.py:50
  34.6 1.9 %collective-permute-start.6 = (bf16[384,768]{1,0:T(8,128)(2,1)S(1)}, bf16[384,768]{1,0:T(8,128)(2,1)S(1)}, u32[]{:S(2)}, u32[]{:S(2)}) collective-permute-start(bf16[384,768]{1,0:T(8,128)(2,1)S(1)} %get-tuple-element.35), channel_id=1, source_target_pairs={{0,510},{1,3},{2,0},{3,5},{4,2},{5,7},{6,4},{7,9},{8,6},{9,11},{10... | collective-permute-start | bytes 1769480 | tf_op jit(solution)/shard_map/ppermute | solution.py:21
  36.5 2.7 %shard_map.73 = (f32[384,896]{1,0:T(8,128)S(1)}, f32[384,896]{1,0:T(8,128)S(1)}, f32[384,768]{1,0:T(8,128)S(1)}) custom-call(bf16[4624,128]{1,0:T(8,128)(2,1)S(1)} %get-tuple-element.23.refs_0_, bf16[4624,128]{1,0:T(8,128)(2,1)S(1)} %collective-permute-done.refs_0_.refs_1_, bf16[2320,128]{1,0:T(8,128)(2,1)S(1)} %collective-permute-done.1.refs_2_, ...), custom_call_target="tpu_custom_call" | custom-call | bytes 9646080 | tf_op jit(solution)/shard_map/pallas_call | solution.py:50
  39.2 8.7 %collective-permute-done.4.refs_1_ = bf16[2320,128]{1,0:T(8,128)(2,1)S(1)} collective-permute-done((bf16[2320,128]{1,0:T(8,128)(2,1)S(1)}, bf16[2320,128]{1,0:T(8,128)(2,1)S(1)}, u32[]{:S(2)}, u32[]{:S(2)}) %collective-permute-start.4) | collective-permute-done | bytes 593952 | tf_op jit(solution)/shard_map/ppermute | solution.py:21
  47.9 1.6 %shard_map.74 = (bf16[2320,128]{1,0:T(8,128)(2,1)S(1)}, bf16[384,768]{1,0:T(8,128)(2,1)S(1)}) custom-call(bf16[384,768]{1,0:T(8,128)(2,1)S(1)} %collective-permute-done.3.refs_3_.refs_0_, bf16[2320,128]{1,0:T(8,128)(2,1)S(1)} %collective-permute-done.4.refs_1_, bf16[2320,128]{1,0:T(8,128)(2,1)S(1)} %collective-permute-done.1.refs_2_, ...), custom_call_target="tpu_custom_call" | custom-call | bytes 4141056 | tf_op jit(solution)/shard_map/pallas_call | solution.py:50
  49.5 3.3 %collective-permute-start.5 = (bf16[2320,128]{1,0:T(8,128)(2,1)S(1)}, bf16[2320,128]{1,0:T(8,128)(2,1)S(1)}, u32[]{:S(2)}, u32[]{:S(2)}) collective-permute-start(bf16[2320,128]{1,0:T(8,128)(2,1)S(1)} %get-tuple-element.33), channel_id=1, source_target_pairs={{0,2},{1,511},{2,4},{3,1},{4,6},{5,3},{6,8},{7,5},{8,10},{9,7},{10... | collective-permute-start | bytes 1781768 | tf_op jit(solution)/shard_map/ppermute | solution.py:21
  52.8 1.9 %collective-permute-start.7 = (f32[384,896]{1,0:T(8,128)S(1)}, f32[384,896]{1,0:T(8,128)S(1)}, u32[]{:S(2)}, u32[]{:S(2)}) collective-permute-start(f32[384,896]{1,0:T(8,128)S(1)} %get-tuple-element.38), channel_id=1, source_target_pairs={{0,1},{1,0},{2,3},{3,2},{4,5},{5,4},{6,7},{7,6},{8,9},{9,8},{10,11... | collective-permute-start | bytes 4128776 | tf_op jit(solution)/shard_map/ppermute | solution.py:21
  54.7 2.4 %collective-permute-start.8 = (bf16[384,768]{1,0:T(8,128)(2,1)S(1)}, bf16[384,768]{1,0:T(8,128)(2,1)S(1)}, u32[]{:S(2)}, u32[]{:S(2)}) collective-permute-start(bf16[384,768]{1,0:T(8,128)(2,1)S(1)} %get-tuple-element.40), channel_id=1, source_target_pairs={{0,511},{1,2},{2,1},{3,4},{4,3},{5,6},{6,5},{7,8},{8,7},{9,10},{10... | collective-permute-start | bytes 1769480 | tf_op jit(solution)/shard_map/ppermute | solution.py:21
  57.1 0.2 shard_map.75.refs_2_.refs_0_
  57.3 3.7 %collective-permute-done.5.refs_1_ = bf16[2320,128]{1,0:T(8,128)(2,1)S(1)} collective-permute-done((bf16[2320,128]{1,0:T(8,128)(2,1)S(1)}, bf16[2320,128]{1,0:T(8,128)(2,1)S(1)}, u32[]{:S(2)}, u32[]{:S(2)}) %collective-permute-start.5) | collective-permute-done | bytes 593952 | tf_op jit(solution)/shard_map/ppermute | solution.py:21
  60.9 0.2 shard_map.76
  61.2 1.4 %shard_map.77 = (f32[384,768]{1,0:T(8,128)}, f32[384]{0:T(512)}, f32[8,128]{1,0:T(8,128)S(1)}) custom-call(f32[384,768]{1,0:T(8,128)S(1)} %get-tuple-element.36.refs_0_, f32[1,384]{1,0:T(1,128)S(1)} %get-tuple-element.37.refs_1_, f32[384,896]{1,0:T(8,128)S(1)} %collective-permute-done.7.refs_2_), custom_call_target="tpu_custom_call" | custom-call | bytes 3742720 | tf_op jit(solution)/shard_map/pallas_call | solution.py:50
  62.5 4.3 %collective-permute-done.8.refs_1_ = bf16[384,768]{1,0:T(8,128)(2,1)S(1)} collective-permute-done((bf16[384,768]{1,0:T(8,128)(2,1)S(1)}, bf16[384,768]{1,0:T(8,128)(2,1)S(1)}, u32[]{:S(2)}, u32[]{:S(2)}) %collective-permute-start.8) | collective-permute-done | bytes 589856 | tf_op jit(solution)/shard_map/ppermute | solution.py:21
  66.8 1.1 %shard_map.78 = f32[384,768]{1,0:T(8,128)} custom-call(f32[384,768]{1,0:T(8,128)S(1)} %shard_map.75.refs_2_.refs_0_, bf16[384,768]{1,0:T(8,128)(2,1)S(1)} %collective-permute-done.8.refs_1_, f32[8,128]{1,0:T(8,128)S(1)} %get-tuple-element.41.refs_2_), custom_call_target="tpu_custom_call" | custom-call | bytes 2949120 | tf_op jit(solution)/shard_map/pallas_call | solution.py:50
  (14 shorter events, 0.0 us)
Async XLA Ops:
  0.6 4.2 %copy-start = (bf16[384,768]{1,0:T(8,128)(2,1)S(1)}, bf16[384,768]{1,0:T(8,128)(2,1)}, u32[]{:S(2)}) copy-start(bf16[384,768]{1,0:T(8,128)(2,1)} %refs_0_.2) | copy-start | bytes 1769476
  0.6 4.2 %copy-start.3 = (s32[384]{0:T(512)S(1)}, s32[384]{0:T(512)}, u32[]{:S(2)}) copy-start(s32[384]{0:T(512)} %refs_2_.1) | copy-start | bytes 4612
  0.7 27.6 %collective-permute-start.3 = (bf16[384,768]{1,0:T(8,128)(2,1)}, bf16[384,768]{1,0:T(8,128)(2,1)S(1)}, u32[]{:S(2)}, u32[]{:S(2)}) collective-permute-start(bf16[384,768]{1,0:T(8,128)(2,1)} %refs_0_.3), channel_id=1, source_target_pairs={{0,510},{1,3},{2,0},{3,5},{4,2},{5,7},{6,4},{7,9},{8,6},{9,11},{10... | collective-permute-start | bytes 1769480 | tf_op jit(solution)/shard_map/ppermute | solution.py:21
  4.9 14.7 %copy-start.1 = (bf16[384,768]{1,0:T(8,128)(2,1)S(1)}, bf16[384,768]{1,0:T(8,128)(2,1)}, u32[]{:S(2)}) copy-start(bf16[384,768]{1,0:T(8,128)(2,1)} %refs_1_.3) | copy-start | bytes 1769476
  4.9 14.7 %copy-start.2 = (bf16[384,768]{1,0:T(8,128)(2,1)S(1)}, bf16[384,768]{1,0:T(8,128)(2,1)}, u32[]{:S(2)}) copy-start(bf16[384,768]{1,0:T(8,128)(2,1)} %refs_0_.3) | copy-start | bytes 1769476
  5.0 26.9 %collective-permute-start.2 = (bf16[2320,128]{1,0:T(8,128)(2,1)S(1)}, bf16[2320,128]{1,0:T(8,128)(2,1)S(1)}, u32[]{:S(2)}, u32[]{:S(2)}) collective-permute-start(bf16[2320,128]{1,0:T(8,128)(2,1)S(1)} %shard_map.68.refs_3_.refs_1_), channel_id=1, source_target_pairs={{0,2},{1,511},{2,4},{3,1},{4,6},{5,3},{6,8},{7,5},{8,10},{9,7},{10... | collective-permute-start | bytes 1781768 | tf_op jit(solution)/shard_map/ppermute | solution.py:21
  19.9 8.3 %collective-permute-start = (bf16[4624,128]{1,0:T(8,128)(2,1)S(1)}, bf16[4624,128]{1,0:T(8,128)(2,1)S(1)}, u32[]{:S(2)}, u32[]{:S(2)}) collective-permute-start(bf16[4624,128]{1,0:T(8,128)(2,1)S(1)} %get-tuple-element.23.refs_0_), channel_id=1, source_target_pairs={{0,1},{1,0},{2,3},{3,2},{4,5},{5,4},{6,7},{7,6},{8,9},{9,8},{10,11... | collective-permute-start | bytes 3551240 | tf_op jit(solution)/shard_map/ppermute | solution.py:21
  22.8 13.7 %collective-permute-start.1 = (bf16[2320,128]{1,0:T(8,128)(2,1)S(1)}, bf16[2320,128]{1,0:T(8,128)(2,1)S(1)}, u32[]{:S(2)}, u32[]{:S(2)}) collective-permute-start(bf16[2320,128]{1,0:T(8,128)(2,1)S(1)} %get-tuple-element.24), channel_id=1, source_target_pairs={{0,511},{1,2},{2,1},{3,4},{4,3},{5,6},{6,5},{7,8},{8,7},{9,10},{10... | collective-permute-start | bytes 1781768 | tf_op jit(solution)/shard_map/ppermute | solution.py:21
  24.7 23.2 %collective-permute-start.4 = (bf16[2320,128]{1,0:T(8,128)(2,1)S(1)}, bf16[2320,128]{1,0:T(8,128)(2,1)S(1)}, u32[]{:S(2)}, u32[]{:S(2)}) collective-permute-start(bf16[2320,128]{1,0:T(8,128)(2,1)S(1)} %get-tuple-element.31), channel_id=1, source_target_pairs={{0,510},{1,3},{2,0},{3,5},{4,2},{5,7},{6,4},{7,9},{8,6},{9,11},{10... | collective-permute-start | bytes 1781768 | tf_op jit(solution)/shard_map/ppermute | solution.py:21
  34.6 22.5 %collective-permute-start.6 = (bf16[384,768]{1,0:T(8,128)(2,1)S(1)}, bf16[384,768]{1,0:T(8,128)(2,1)S(1)}, u32[]{:S(2)}, u32[]{:S(2)}) collective-permute-start(bf16[384,768]{1,0:T(8,128)(2,1)S(1)} %get-tuple-element.35), channel_id=1, source_target_pairs={{0,510},{1,3},{2,0},{3,5},{4,2},{5,7},{6,4},{7,9},{8,6},{9,11},{10... | collective-permute-start | bytes 1769480 | tf_op jit(solution)/shard_map/ppermute | solution.py:21
  49.5 11.4 %collective-permute-start.5 = (bf16[2320,128]{1,0:T(8,128)(2,1)S(1)}, bf16[2320,128]{1,0:T(8,128)(2,1)S(1)}, u32[]{:S(2)}, u32[]{:S(2)}) collective-permute-start(bf16[2320,128]{1,0:T(8,128)(2,1)S(1)} %get-tuple-element.33), channel_id=1, source_target_pairs={{0,2},{1,511},{2,4},{3,1},{4,6},{5,3},{6,8},{7,5},{8,10},{9,7},{10... | collective-permute-start | bytes 1781768 | tf_op jit(solution)/shard_map/ppermute | solution.py:21
  52.8 8.4 %collective-permute-start.7 = (f32[384,896]{1,0:T(8,128)S(1)}, f32[384,896]{1,0:T(8,128)S(1)}, u32[]{:S(2)}, u32[]{:S(2)}) collective-permute-start(f32[384,896]{1,0:T(8,128)S(1)} %get-tuple-element.38), channel_id=1, source_target_pairs={{0,1},{1,0},{2,3},{3,2},{4,5},{5,4},{6,7},{7,6},{8,9},{9,8},{10,11... | collective-permute-start | bytes 4128776 | tf_op jit(solution)/shard_map/ppermute | solution.py:21
  54.7 12.0 %collective-permute-start.8 = (bf16[384,768]{1,0:T(8,128)(2,1)S(1)}, bf16[384,768]{1,0:T(8,128)(2,1)S(1)}, u32[]{:S(2)}, u32[]{:S(2)}) collective-permute-start(bf16[384,768]{1,0:T(8,128)(2,1)S(1)} %get-tuple-element.40), channel_id=1, source_target_pairs={{0,511},{1,2},{2,1},{3,4},{4,3},{5,6},{6,5},{7,8},{8,7},{9,10},{10... | collective-permute-start | bytes 1769480 | tf_op jit(solution)/shard_map/ppermute | solution.py:21
